TPU v7x, 32 devices: a whole 2x2x4 slice. The times are simulated.
32 devices in a mesh: gx: 8 (over z, x), gy: 4 (over y, core).
Axes of the slice: x: 2, y: 2, z: 4, core: 2. Of those that a mesh axis runs over, the one named last changes fastest.
Arguments:
- velocity: float32 [3, 8, 256, 512], P(None, None, 'gx', 'gy'), may hold values from -6 to 6
- stress: float32 [6, 8, 256, 512], P(None, None, 'gx', 'gy'), may hold values from -6 to 6
- zones: int32 [8, 256, 512], P(None, 'gx', 'gy'), may hold values from 0 to 15
- zone_table: float32 [3, 16], replicated, may hold values from 0.5 to 2
- regional: float32 [8, 2, 3, 8, 1024], P('gx', None, None, None, 'gy'), may hold values from -6 to 6
- owner: int32 [4], replicated, may hold values from 0 to 7
- footprint_building: int32 [8, 4, 64], P('gx', 'gy'), may hold values from 0 to 1023
- footprint_block: int32 [8, 4, 64], P('gx', 'gy'), may hold values from 0 to 63
Outputs:
- velocity_out: float32 [3, 8, 256, 512], P(None, None, 'gx', 'gy')
- stress_out: float32 [6, 8, 256, 512], P(None, None, 'gx', 'gy')
- base_shear: float32 [2, 1024], replicated
All inputs are finite; a program needn't handle non-finite values.
Results may differ from a plain program's by a relative error of at most 0.000084.
Values sent between devices are 32-bit elements; how exact they have to be, the bound alone decides.
No kernel may reach another device: no remote copies, remote signals or barrier semaphores. Data moves between devices by JAX's collectives and lax.ppermute only.
A program may use at most 64 MiB of HBM per device.

v0:
```python
import jax
import jax.numpy as jnp
from jax import lax
from jax.sharding import PartitionSpec as P

CX = 32
CY = 128
NZ = 8
STEPS = 2
COARSE = 4
BLOCK = 8
ZONES = 16
BUILDINGS = 1024


def with_halo(value, sides, width):
    for axis, dim in sides:
        devices, length = (lax.axis_size(axis), value.shape[dim])
        up = [(i, (i + 1) % devices) for i in range(devices)]
        down = [(j, i) for i, j in up]
        last = lax.slice_in_dim(value, length - width, length, axis=dim)
        leading = lax.slice_in_dim(value, 0, width, axis=dim)
        before = lax.ppermute(last, axis, up)
        after = lax.ppermute(leading, axis, down)
        value = jnp.concatenate([before, value, after], axis=dim)
    return value


def broadcast(value, axis, source):
    kept = jnp.where(lax.axis_index(axis) == source, value, 0).astype(value.dtype)
    return lax.psum(kept, axis)


def diff_z(field):
    padded = jnp.pad(field, ((1, 1), (0, 0), (0, 0)))
    return (padded[2:] - padded[:-2]) * 0.5


def lookup(zones, column):
    total = jnp.zeros(zones.shape, jnp.float32)
    for zone in range(ZONES):
        total = total + jnp.where(zones == zone, column[zone], 0.0)
    return total


def stress_slopes(stress):
    padded = with_halo(stress, (("gx", 2), ("gy", 3)), 1)
    along_x = (padded[0:3, :, 2:, 1:-1] - padded[0:3, :, :-2, 1:-1]) * 0.5
    along_y = (padded[2:5, :, 1:-1, 2:] - padded[2:5, :, 1:-1, :-2]) * 0.5
    return (along_x, along_y)


def body(velocity, stress, zones, zone_table, regional, owner, footprint_building, footprint_block):
    lam = lookup(zones, zone_table[0])
    shear_mod = lookup(zones, zone_table[1])
    buoy = lookup(zones, zone_table[2])
    root = owner[lax.axis_index("gy")]
    columns_all = broadcast(regional[0], "gx", root)
    mine = lax.dynamic_index_in_dim(columns_all, lax.axis_index("gx"), 2, keepdims=False)
    coarse = mine.reshape(STEPS, 3, CX // COARSE, CY // COARSE)
    drm = jnp.repeat(jnp.repeat(coarse, COARSE, axis=2), COARSE, axis=3)
    for step in range(STEPS):
        along_x, along_y = stress_slopes(stress)
        force_x = along_x[0] + along_y[0] + diff_z(stress[1])
        force_y = along_x[2] + along_y[1] + diff_z(stress[4])
        force_z = along_x[1] + along_y[2] + diff_z(stress[5])
        force = jnp.stack([force_x, force_y, force_z])
        force = force.at[:, NZ - 1].add(shear_mod[NZ - 1][None] * drm[step])
        velocity = velocity + 0.2 * buoy[None] * force
        padded = with_halo(velocity, (("gx", 2), ("gy", 3)), 1)
        vel_x = (padded[:, :, 2:, 1:-1] - padded[:, :, :-2, 1:-1]) * 0.5
        vel_y = (padded[:, :, 1:-1, 2:] - padded[:, :, 1:-1, :-2]) * 0.5
        dvx_dx = vel_x[0]
        dvy_dy = vel_y[1]
        dvz_dz = diff_z(velocity[2])
        theta = dvx_dx + dvy_dy + dvz_dz
        new_xx = stress[0] + 0.2 * (lam * theta + 2.0 * shear_mod * dvx_dx)
        new_xz = stress[1] + 0.2 * shear_mod * (diff_z(velocity[0]) + vel_x[2])
        new_xy = stress[2] + 0.2 * shear_mod * (vel_y[0] + vel_x[1])
        new_yy = stress[3] + 0.2 * (lam * theta + 2.0 * shear_mod * dvy_dy)
        new_yz = stress[4] + 0.2 * shear_mod * (diff_z(velocity[1]) + vel_y[2])
        new_zz = stress[5] + 0.2 * (lam * theta + 2.0 * shear_mod * dvz_dz)
        stress = jnp.stack([new_xx, new_xz, new_xy, new_yy, new_yz, new_zz])
    plane = jnp.stack([stress[1, 1], stress[4, 1]])
    plane = plane.reshape(2, CX // BLOCK, BLOCK, CY // BLOCK, BLOCK)
    means = (jnp.sum(plane, axis=(2, 4)) * (1.0 / (BLOCK * BLOCK))).reshape(2, -1)
    block_ids = footprint_block[0, 0]
    building_ids = footprint_building[0, 0]
    block_table = (
        block_ids[:, None] == jnp.arange(means.shape[1], dtype=jnp.int32)[None, :]
    ).astype(jnp.float32)
    values = jnp.dot(means, block_table.T, precision=lax.Precision.HIGHEST)
    building_table = (
        building_ids[:, None] == jnp.arange(BUILDINGS, dtype=jnp.int32)[None, :]
    ).astype(jnp.float32)
    partial_shear = jnp.dot(values, building_table, precision=lax.Precision.HIGHEST)
    shear = lax.psum(partial_shear, ("gx", "gy"))
    return (velocity, stress, shear)


def solution(mesh):
    return jax.shard_map(
        body,
        mesh=mesh,
        in_specs=(
            P(None, None, "gx", "gy"),
            P(None, None, "gx", "gy"),
            P(None, "gx", "gy"),
            P(),
            P("gx", None, None, None, "gy"),
            P(),
            P("gx", "gy", None),
            P("gx", "gy", None),
        ),
        out_specs=(P(None, None, "gx", "gy"), P(None, None, "gx", "gy"), P()),
        check_vma=False,
    )
```

profile of v0, /device:TPU:0, one launch (start us, length us, event | category | flops | bytes accessed | tf_op | source)
XLA Modules:
  0.0 195.0 jit_solution(6467237938705955136)
XLA Ops:
  0.6 1.1 fusion.93
  1.7 3.0 %collective-permute-start.1 = (f32[6,8,1,128]{3,1,2,0:T(8,128)S(1)}, f32[6,8,1,128]{3,1,2,0:T(8,128)S(1)}, u32[]{:S(2)}, u32[]{:S(2)}) collective-permute-start(f32[6,8,1,128]{3,1,2,0:T(8,128)S(1)} %bitcast.295), channel_id=1, source_target_pairs={{0,4},{4,8},{8,12},{12,16},{16,20},{20,24},{24,28},{28,0},{1,5},{5... | collective-permute-start | bytes 73736 | tf_op jit(solution)/shard_map/ppermute | solution.py:23
  4.7 3.1 %collective-permute-start = (f32[6,8,1,128]{3,1,2,0:T(8,128)S(1)}, f32[6,8,1,128]{3,1,2,0:T(8,128)S(1)}, u32[]{:S(2)}, u32[]{:S(2)}) collective-permute-start(f32[6,8,1,128]{3,1,2,0:T(8,128)S(1)} %bitcast.294), channel_id=1, source_target_pairs={{4,0},{8,4},{12,8},{16,12},{20,16},{24,20},{28,24},{0,28},{5,1},{9... | collective-permute-start | bytes 73736 | tf_op jit(solution)/shard_map/ppermute | solution.py:24
  7.8 1.1 slice_bitcast_fusion.16
  8.9 0.7 fusion.99
  9.6 0.7 fusion.100
  10.3 0.7 fusion.98
  11.1 0.6 dynamic_slice.7
  12.3 0.6 select_bitcast_fusion
  12.9 10.6 %add_multiply_fusion.2 = (f32[8,32,128]{2,1,0:T(8,128)S(1)}, pred[8,32,128]{2,1,0:T(8,128)(4,1)S(1)}, pred[8,32,128]{2,1,0:T(8,128)(4,1)S(1)}, pred[8,32,128]{2,...) fusion(f32[]{:T(128)} %bitcast.15, f32[]{:T(128)} %bitcast.14, ...), kind=kLoop, calls=%fused_computation.189 | loop fusion | flops 1572864 | bytes 786496 | tf_op jit(solution)/shard_map/mul | solution.py:69
  23.7 0.4 copy-done.13
  24.2 10.2 %select_add_fusion.1 = f32[8,32,128]{2,1,0:T(8,128)S(1)} fusion(pred[8,32,128]{2,1,0:T(8,128)(4,1)S(1)} %get-tuple-element.78, pred[8,32,128]{2,1,0:T(8,128)(4,1)S(1)} %get-tuple-element.77, pred[8,32,128]{2,1,0:T(8,128)(4,1)S(1)} %get-tuple-element.76, pred[8,32,128]{2,1,0:T(8,128)(4,1)S(1)} %get-tuple-element.75, ...), kind=kLoop, calls=%fused_computation.185 | loop fusion | flops 1015808 | bytes 655424 | tf_op jit(solution)/shard_map/add | solution.py:42
  34.5 0.6 copy-done.49
  35.3 0.3 fusion.91
  35.6 0.4 copy.441
  36.1 0.4 copy.439
  36.5 1.8 collective-permute-start.2
  38.3 35.2 %psum.14 = f32[2,3,8,256]{3,2,1,0:T(8,128)S(1)} all-reduce(f32[2,3,8,256]{3,2,1,0:T(8,128)S(1)} %copy-done.45), channel_id=1, replica_groups=mesh['gx'=8,'gy'=4] {'gx'}, use_global_device_ids=true, to_apply=%region_0.1 | all-reduce | flops 12288 | bytes 98304 | tf_op jit(solution)/shard_map/psum | solution.py:31
  73.5 0.6 dynamic-slice_reduce_fusion
  74.4 0.7 copy.444
  75.1 0.5 copy.442
  75.6 0.5 copy.440
  76.0 0.3 copy-done.50
  76.3 0.5 fusion.15
  77.0 0.7 copy-done.47
  77.7 0.2 copy-done.11
  78.3 1.9 collective-permute-start.5
  80.1 1.7 collective-permute-done.4
  81.8 2.8 %collective-permute-done.5 = f32[3,8,1,128]{3,1,2,0:T(8,128)S(1)} collective-permute-done((f32[3,8,1,128]{3,1,2,0:T(8,128)S(1)}, f32[3,8,1,128]{3,1,2,0:T(8,128)S(1)}, u32[]{:S(2)}, u32[]{:S(2)}) %collective-permute-start.5) | collective-permute-done | bytes 12320 | tf_op jit(solution)/shard_map/ppermute | solution.py:23
  85.0 1.7 collective-permute-start.6
  86.7 9.7 %collective-permute-done.7 = f32[3,8,34,1]{3,2,1,0:T(8,128)S(1)} collective-permute-done((f32[3,8,34,1]{3,2,1,0:T(8,128)S(1)}, f32[3,8,34,1]{3,2,1,0:T(8,128)S(1)}, u32[]{:S(2)}, u32[]{:S(2)}) %collective-permute-start.7) | collective-permute-done | bytes 3296 | tf_op jit(solution)/shard_map/ppermute | solution.py:23
  96.4 1.3 collective-permute-done.6
  97.8 0.5 fusion.9
  98.7 0.5 copy-done.14
  99.2 10.7 %bitcast_dynamic-update-slice_fusion.8 = (f32[6,8,32,128]{3,2,1,0:T(8,128)S(1)}, f32[8,32,128]{2,1,0:T(8,128)S(1)}, f32[8,32,128]{2,1,0:T(8,128)}) fusion(f32[3,8,32,128]{3,2,1,0:T(8,128)S(1)} %get-tuple-element.107, f32[8,32,128]{2,1,0:T(8,128)S(1)} %select_add_fusion.1, f32[6,8,32,128]{3,2,1,0:T(8,128)S(1)} %copy-done, ...), kind=kLoop, calls=%fused_computation.178 | loop fusion | flops 1343487 | bytes 1572928
  109.9 0.7 bitcast_dynamic-update-slice_fusion.7
  110.7 0.7 bitcast_dynamic-update-slice_fusion.4
  111.4 0.7 bitcast_dynamic-update-slice_fusion.3
  112.2 4.7 %collective-permute-start.8 = (f32[6,8,1,128]{3,1,2,0:T(8,128)S(1)}, f32[6,8,1,128]{3,1,2,0:T(8,128)S(1)}, u32[]{:S(2)}, u32[]{:S(2)}) collective-permute-start(f32[6,8,1,128]{3,1,2,0:T(8,128)S(1)} %bitcast.296), channel_id=1, source_target_pairs={{4,0},{8,4},{12,8},{16,12},{20,16},{24,20},{28,24},{0,28},{5,1},{9... | collective-permute-start | bytes 73736 | tf_op jit(solution)/shard_map/ppermute | solution.py:24
  116.9 1.8 collective-permute-done.9
  118.8 0.6 copy-done.53
  119.5 0.3 fusion.90
  119.8 1.0 copy.459
  120.9 0.4 copy.457
  121.3 1.8 collective-permute-start.10
  123.3 0.7 copy.462
  124.0 0.3 collective-permute-done.11
  124.3 0.5 copy.460
  124.8 1.2 copy.458
  126.0 1.9 fusion.7
  128.2 0.8 copy-done.46
  129.1 4.8 %collective-permute-start.12 = (f32[3,8,1,128]{3,1,2,0:T(8,128)S(1)}, f32[3,8,1,128]{3,1,2,0:T(8,128)S(1)}, u32[]{:S(2)}, u32[]{:S(2)}) collective-permute-start(f32[3,8,1,128]{3,1,2,0:T(8,128)S(1)} %bitcast.301), channel_id=1, source_target_pairs={{4,0},{8,4},{12,8},{16,12},{20,16},{24,20},{28,24},{0,28},{5,1},{9... | collective-permute-start | bytes 36872 | tf_op jit(solution)/shard_map/ppermute | solution.py:24
  133.8 1.4 collective-permute-done.12
  135.2 5.0 %collective-permute-done.13 = f32[3,8,1,128]{3,1,2,0:T(8,128)S(1)} collective-permute-done((f32[3,8,1,128]{3,1,2,0:T(8,128)S(1)}, f32[3,8,1,128]{3,1,2,0:T(8,128)S(1)}, u32[]{:S(2)}, u32[]{:S(2)}) %collective-permute-start.13) | collective-permute-done | bytes 12320 | tf_op jit(solution)/shard_map/ppermute | solution.py:23
  140.5 0.6 collective-permute-start.15
  141.0 1.2 collective-permute-start.14
  142.3 9.4 %collective-permute-done.15 = f32[3,8,34,1]{3,2,1,0:T(8,128)S(1)} collective-permute-done((f32[3,8,34,1]{3,2,1,0:T(8,128)S(1)}, f32[3,8,34,1]{3,2,1,0:T(8,128)S(1)}, u32[]{:S(2)}, u32[]{:S(2)}) %collective-permute-start.15) | collective-permute-done | bytes 3296 | tf_op jit(solution)/shard_map/ppermute | solution.py:23
  151.7 1.8 collective-permute-done.14
  153.5 0.5 fusion.1
  154.2 0.9 copy-done.4
  156.0 0.7 copy-done.59
  156.8 0.7 copy-done.60
  157.5 0.3 fusion.16
  157.8 37.2 %psum.15 = f32[2,1024]{1,0:T(2,128)} all-reduce(f32[2,1024]{1,0:T(2,128)S(1)} %fusion.16), channel_id=1, replica_groups=mesh['gx'=8,'gy'=4] {'gx','gy'}, use_global_device_ids=true, to_apply=%region_2.3 | all-reduce | flops 2048 | bytes 16384 | tf_op jit(solution)/shard_map/psum | solution.py:97
  (167 shorter events, 4.1 us)
Async XLA Ops:
  1.7 32.8 %collective-permute-start.1 = (f32[6,8,1,128]{3,1,2,0:T(8,128)S(1)}, f32[6,8,1,128]{3,1,2,0:T(8,128)S(1)}, u32[]{:S(2)}, u32[]{:S(2)}) collective-permute-start(f32[6,8,1,128]{3,1,2,0:T(8,128)S(1)} %bitcast.295), channel_id=1, source_target_pairs={{0,4},{4,8},{8,12},{12,16},{16,20},{20,24},{24,28},{28,0},{1,5},{5... | collective-permute-start | bytes 73736 | tf_op jit(solution)/shard_map/ppermute | solution.py:23
  4.7 29.8 %collective-permute-start = (f32[6,8,1,128]{3,1,2,0:T(8,128)S(1)}, f32[6,8,1,128]{3,1,2,0:T(8,128)S(1)}, u32[]{:S(2)}, u32[]{:S(2)}) collective-permute-start(f32[6,8,1,128]{3,1,2,0:T(8,128)S(1)} %bitcast.294), channel_id=1, source_target_pairs={{4,0},{8,4},{12,8},{16,12},{20,16},{24,20},{28,24},{0,28},{5,1},{9... | collective-permute-start | bytes 73736 | tf_op jit(solution)/shard_map/ppermute | solution.py:24
  7.8 1.1 copy-start.12
  7.8 3.3 %copy-start.58 = (s32[4]{0:T(128)S(1)}, s32[4]{0:T(128)}, u32[]{:S(2)}) copy-start(s32[4]{0:T(128)} %param.17) | copy-start | bytes 52
  7.8 4.5 %copy-start.55 = (f32[1,2,3,8,256]{4,3,2,1,0:T(8,128)S(1)}, f32[1,2,3,8,256]{4,3,2,1,0:T(8,128)}, u32[]{:S(2)}) copy-start(f32[1,2,3,8,256]{4,3,2,1,0:T(8,128)} %param.16) | copy-start | bytes 147460
  8.9 4.0 %copy-start.48 = (s32[8,32,128]{2,1,0:T(8,128)S(1)}, s32[8,32,128]{2,1,0:T(8,128)}, u32[]{:S(2)}) copy-start(s32[8,32,128]{2,1,0:T(8,128)} %param.14) | copy-start | bytes 393220
  12.9 22.2 %copy-start = (f32[6,8,32,128]{3,2,1,0:T(8,128)S(1)}, f32[6,8,32,128]{3,2,1,0:T(8,128)}, u32[]{:S(2)}) copy-start(f32[6,8,32,128]{3,2,1,0:T(8,128)} %param.13) | copy-start | bytes 2359300
  23.6 10.8 %copy-start.17 = (pred[8,32,128]{2,1,0:T(8,128)(4,1)}, pred[8,32,128]{2,1,0:T(8,128)(4,1)S(1)}, u32[]{:S(2)}) copy-start(pred[8,32,128]{2,1,0:T(8,128)(4,1)S(1)} %get-tuple-element.65) | copy-start | bytes 98308
  23.6 10.8 %copy-start.19 = (pred[8,32,128]{2,1,0:T(8,128)(4,1)}, pred[8,32,128]{2,1,0:T(8,128)(4,1)S(1)}, u32[]{:S(2)}) copy-start(pred[8,32,128]{2,1,0:T(8,128)(4,1)S(1)} %get-tuple-element.66) | copy-start | bytes 98308
  23.6 10.8 %copy-start.21 = (pred[8,32,128]{2,1,0:T(8,128)(4,1)}, pred[8,32,128]{2,1,0:T(8,128)(4,1)S(1)}, u32[]{:S(2)}) copy-start(pred[8,32,128]{2,1,0:T(8,128)(4,1)S(1)} %get-tuple-element.67) | copy-start | bytes 98308
  23.6 10.8 %copy-start.23 = (pred[8,32,128]{2,1,0:T(8,128)(4,1)}, pred[8,32,128]{2,1,0:T(8,128)(4,1)S(1)}, u32[]{:S(2)}) copy-start(pred[8,32,128]{2,1,0:T(8,128)(4,1)S(1)} %get-tuple-element.68) | copy-start | bytes 98308
  23.6 10.8 %copy-start.25 = (pred[8,32,128]{2,1,0:T(8,128)(4,1)}, pred[8,32,128]{2,1,0:T(8,128)(4,1)S(1)}, u32[]{:S(2)}) copy-start(pred[8,32,128]{2,1,0:T(8,128)(4,1)S(1)} %get-tuple-element.69) | copy-start | bytes 98308
  23.6 10.8 %copy-start.27 = (pred[8,32,128]{2,1,0:T(8,128)(4,1)}, pred[8,32,128]{2,1,0:T(8,128)(4,1)S(1)}, u32[]{:S(2)}) copy-start(pred[8,32,128]{2,1,0:T(8,128)(4,1)S(1)} %get-tuple-element.70) | copy-start | bytes 98308
  23.6 10.8 %copy-start.29 = (pred[8,32,128]{2,1,0:T(8,128)(4,1)}, pred[8,32,128]{2,1,0:T(8,128)(4,1)S(1)}, u32[]{:S(2)}) copy-start(pred[8,32,128]{2,1,0:T(8,128)(4,1)S(1)} %get-tuple-element.71) | copy-start | bytes 98308
  23.6 10.8 %copy-start.31 = (pred[8,32,128]{2,1,0:T(8,128)(4,1)}, pred[8,32,128]{2,1,0:T(8,128)(4,1)S(1)}, u32[]{:S(2)}) copy-start(pred[8,32,128]{2,1,0:T(8,128)(4,1)S(1)} %get-tuple-element.72) | copy-start | bytes 98308
  23.7 10.8 %copy-start.33 = (pred[8,32,128]{2,1,0:T(8,128)(4,1)}, pred[8,32,128]{2,1,0:T(8,128)(4,1)S(1)}, u32[]{:S(2)}) copy-start(pred[8,32,128]{2,1,0:T(8,128)(4,1)S(1)} %get-tuple-element.73) | copy-start | bytes 98308
  23.7 10.8 %copy-start.35 = (pred[8,32,128]{2,1,0:T(8,128)(4,1)}, pred[8,32,128]{2,1,0:T(8,128)(4,1)S(1)}, u32[]{:S(2)}) copy-start(pred[8,32,128]{2,1,0:T(8,128)(4,1)S(1)} %get-tuple-element.74) | copy-start | bytes 98308
  23.7 10.8 %copy-start.37 = (pred[8,32,128]{2,1,0:T(8,128)(4,1)}, pred[8,32,128]{2,1,0:T(8,128)(4,1)S(1)}, u32[]{:S(2)}) copy-start(pred[8,32,128]{2,1,0:T(8,128)(4,1)S(1)} %get-tuple-element.75) | copy-start | bytes 98308
  23.7 10.8 %copy-start.39 = (pred[8,32,128]{2,1,0:T(8,128)(4,1)}, pred[8,32,128]{2,1,0:T(8,128)(4,1)S(1)}, u32[]{:S(2)}) copy-start(pred[8,32,128]{2,1,0:T(8,128)(4,1)S(1)} %get-tuple-element.76) | copy-start | bytes 98308
  23.7 10.8 %copy-start.41 = (pred[8,32,128]{2,1,0:T(8,128)(4,1)}, pred[8,32,128]{2,1,0:T(8,128)(4,1)S(1)}, u32[]{:S(2)}) copy-start(pred[8,32,128]{2,1,0:T(8,128)(4,1)S(1)} %get-tuple-element.77) | copy-start | bytes 98308
  23.7 10.8 %copy-start.43 = (pred[8,32,128]{2,1,0:T(8,128)(4,1)}, pred[8,32,128]{2,1,0:T(8,128)(4,1)S(1)}, u32[]{:S(2)}) copy-start(pred[8,32,128]{2,1,0:T(8,128)(4,1)S(1)} %get-tuple-element.78) | copy-start | bytes 98308
  36.0 39.1 %collective-permute-start.3 = (f32[6,8,34,1]{2,1,3,0:T(8,128)S(1)}, f32[6,8,34,1]{2,1,3,0:T(8,128)S(1)}, u32[]{:S(2)}, u32[]{:S(2)}) collective-permute-start(f32[6,8,34,1]{2,1,3,0:T(8,128)S(1)} %copy.441), channel_id=1, source_target_pairs={{0,1},{1,2},{2,3},{3,0},{4,5},{5,6},{6,7},{7,4},{8,9},{9,10},{10,1... | collective-permute-start | bytes 19592 | tf_op jit(solution)/shard_map/ppermute | solution.py:23
  36.1 2.2 %copy-start.45 = (f32[2,3,8,256]{3,2,1,0:T(8,128)S(1)}, f32[2,3,8,256]{3,2,1,0:T(8,128)}, u32[]{:S(2)}) copy-start(f32[2,3,8,256]{3,2,1,0:T(8,128)} %select_bitcast_fusion) | copy-start | bytes 147460
  36.5 39.0 %collective-permute-start.2 = (f32[6,8,34,1]{2,1,3,0:T(8,128)S(1)}, f32[6,8,34,1]{2,1,3,0:T(8,128)S(1)}, u32[]{:S(2)}, u32[]{:S(2)}) collective-permute-start(f32[6,8,34,1]{2,1,3,0:T(8,128)S(1)} %copy.439), channel_id=1, source_target_pairs={{1,0},{2,1},{3,2},{0,3},{5,4},{6,5},{7,6},{4,7},{9,8},{10,9},{11,1... | collective-permute-start | bytes 19592 | tf_op jit(solution)/shard_map/ppermute | solution.py:24
  76.9 0.8 copy-start.47
  76.9 1.0 copy-start.11
  78.1 3.7 %collective-permute-start.4 = (f32[3,8,1,128]{3,1,2,0:T(8,128)S(1)}, f32[3,8,1,128]{3,1,2,0:T(8,128)S(1)}, u32[]{:S(2)}, u32[]{:S(2)}) collective-permute-start(f32[3,8,1,128]{3,1,2,0:T(8,128)S(1)} %bitcast.300), channel_id=1, source_target_pairs={{4,0},{8,4},{12,8},{16,12},{20,16},{24,20},{28,24},{0,28},{5,1},{9... | collective-permute-start | bytes 36872 | tf_op jit(solution)/shard_map/ppermute | solution.py:24
  78.3 6.4 %collective-permute-start.5 = (f32[3,8,1,128]{3,1,2,0:T(8,128)S(1)}, f32[3,8,1,128]{3,1,2,0:T(8,128)S(1)}, u32[]{:S(2)}, u32[]{:S(2)}) collective-permute-start(f32[3,8,1,128]{3,1,2,0:T(8,128)S(1)} %bitcast.298), channel_id=1, source_target_pairs={{0,4},{4,8},{8,12},{12,16},{16,20},{20,24},{24,28},{28,0},{1,5},{5... | collective-permute-start | bytes 36872 | tf_op jit(solution)/shard_map/ppermute | solution.py:23
  84.9 11.5 %collective-permute-start.7 = (f32[3,8,34,1]{3,2,1,0:T(8,128)S(1)}, f32[3,8,34,1]{3,2,1,0:T(8,128)S(1)}, u32[]{:S(2)}, u32[]{:S(2)}) collective-permute-start(f32[3,8,34,1]{3,2,1,0:T(8,128)S(1)} %get-tuple-element.103), channel_id=1, source_target_pairs={{0,1},{1,2},{2,3},{3,0},{4,5},{5,6},{6,7},{7,4},{8,9},{9,10},{10,1... | collective-permute-start | bytes 9800 | tf_op jit(solution)/shard_map/ppermute | solution.py:23
  85.0 12.7 %collective-permute-start.6 = (f32[3,8,34,1]{3,2,1,0:T(8,128)S(1)}, f32[3,8,34,1]{3,2,1,0:T(8,128)S(1)}, u32[]{:S(2)}, u32[]{:S(2)}) collective-permute-start(f32[3,8,34,1]{3,2,1,0:T(8,128)S(1)} %get-tuple-element.102), channel_id=1, source_target_pairs={{1,0},{2,1},{3,2},{0,3},{5,4},{6,5},{7,6},{4,7},{9,8},{10,9},{11,1... | collective-permute-start | bytes 9800 | tf_op jit(solution)/shard_map/ppermute | solution.py:24
  97.7 0.8 copy-start.24
  97.7 0.8 copy-start.26
  97.7 0.8 copy-start.28
  97.7 0.8 copy-start.30
  97.7 0.8 copy-start.32
  97.8 0.9 copy-start.34
  97.8 0.9 copy-start.36
  97.8 0.9 copy-start.38
  97.8 0.9 copy-start.40
  97.8 0.9 copy-start.42
  97.8 0.9 copy-start.44
  98.3 12.3 %copy-start.5 = (f32[3,8,32,128]{3,2,1,0:T(8,128)}, f32[3,8,32,128]{3,2,1,0:T(8,128)S(1)}, u32[]{:S(2)}) copy-start(f32[3,8,32,128]{3,2,1,0:T(8,128)S(1)} %get-tuple-element.107) | copy-start | bytes 1179652
  98.3 12.4 %copy-start.3 = (f32[3,8,32,128]{3,2,1,0:T(8,128)}, f32[3,8,32,128]{3,2,1,0:T(8,128)S(1)}, u32[]{:S(2)}) copy-start(f32[3,8,32,128]{3,2,1,0:T(8,128)S(1)} %get-tuple-element.106) | copy-start | bytes 1179652
  98.3 0.9 copy-start.14
  98.3 0.9 copy-start.16
  112.1 6.6 %copy-start.2 = (f32[6,8,32,128]{3,2,1,0:T(8,128)}, f32[6,8,32,128]{3,2,1,0:T(8,128)S(1)}, u32[]{:S(2)}) copy-start(f32[6,8,32,128]{3,2,1,0:T(8,128)S(1)} %get-tuple-element.53) | copy-start | bytes 2359300
  112.2 6.6 %collective-permute-start.9 = (f32[6,8,1,128]{3,1,2,0:T(8,128)S(1)}, f32[6,8,1,128]{3,1,2,0:T(8,128)S(1)}, u32[]{:S(2)}, u32[]{:S(2)}) collective-permute-start(f32[6,8,1,128]{3,1,2,0:T(8,128)S(1)} %bitcast.297), channel_id=1, source_target_pairs={{0,4},{4,8},{8,12},{12,16},{16,20},{20,24},{24,28},{28,0},{1,5},{5... | collective-permute-start | bytes 73736 | tf_op jit(solution)/shard_map/ppermute | solution.py:23
  112.2 6.5 %collective-permute-start.8 = (f32[6,8,1,128]{3,1,2,0:T(8,128)S(1)}, f32[6,8,1,128]{3,1,2,0:T(8,128)S(1)}, u32[]{:S(2)}, u32[]{:S(2)}) collective-permute-start(f32[6,8,1,128]{3,1,2,0:T(8,128)S(1)} %bitcast.296), channel_id=1, source_target_pairs={{4,0},{8,4},{12,8},{16,12},{20,16},{24,20},{28,24},{0,28},{5,1},{9... | collective-permute-start | bytes 73736 | tf_op jit(solution)/shard_map/ppermute | solution.py:24
  120.9 3.5 %collective-permute-start.11 = (f32[6,8,34,1]{2,1,3,0:T(8,128)}, f32[6,8,34,1]{2,1,3,0:T(8,128)S(1)}, u32[]{:S(2)}, u32[]{:S(2)}) collective-permute-start(f32[6,8,34,1]{2,1,3,0:T(8,128)} %copy.459), channel_id=1, source_target_pairs={{0,1},{1,2},{2,3},{3,0},{4,5},{5,6},{6,7},{7,4},{8,9},{9,10},{10,1... | collective-permute-start | bytes 19592 | tf_op jit(solution)/shard_map/ppermute | solution.py:23
  120.9 2.2 %copy-start.57 = (f32[3,256]{1,0:T(4,128)S(1)}, f32[3,256]{1,0:T(4,128)}, u32[]{:S(2)}) copy-start(f32[3,256]{1,0:T(4,128)} %get-tuple-element.45) | copy-start | bytes 9220
  121.3 3.5 %collective-permute-start.10 = (f32[6,8,34,1]{2,1,3,0:T(8,128)S(1)}, f32[6,8,34,1]{2,1,3,0:T(8,128)}, u32[]{:S(2)}, u32[]{:S(2)}) collective-permute-start(f32[6,8,34,1]{2,1,3,0:T(8,128)S(1)} %copy.457), channel_id=1, source_target_pairs={{1,0},{2,1},{3,2},{0,3},{5,4},{6,5},{7,6},{4,7},{9,8},{10,9},{11,1... | collective-permute-start | bytes 19592 | tf_op jit(solution)/shard_map/ppermute | solution.py:24
  126.0 2.0 %copy-start.7 = (f32[8,32,128]{2,1,0:T(8,128)S(1)}, f32[8,32,128]{2,1,0:T(8,128)}, u32[]{:S(2)}) copy-start(f32[8,32,128]{2,1,0:T(8,128)} %get-tuple-element.54) | copy-start | bytes 393220
  126.0 2.0 %copy-start.8 = (f32[8,32,128]{2,1,0:T(8,128)S(1)}, f32[8,32,128]{2,1,0:T(8,128)}, u32[]{:S(2)}) copy-start(f32[8,32,128]{2,1,0:T(8,128)} %get-tuple-element.56) | copy-start | bytes 393220
  126.0 2.0 %copy-start.9 = (f32[8,32,128]{2,1,0:T(8,128)S(1)}, f32[8,32,128]{2,1,0:T(8,128)}, u32[]{:S(2)}) copy-start(f32[8,32,128]{2,1,0:T(8,128)} %get-tuple-element.58) | copy-start | bytes 393220
  128.1 0.8 copy-start.46
  129.0 24.5 %copy-start.1 = (f32[3,8,32,128]{3,2,1,0:T(8,128)}, f32[3,8,32,128]{3,2,1,0:T(8,128)S(1)}, u32[]{:S(2)}) copy-start(f32[3,8,32,128]{3,2,1,0:T(8,128)S(1)} %multiply_add_fusion) | copy-start | bytes 1179652
  129.1 6.2 %collective-permute-start.12 = (f32[3,8,1,128]{3,1,2,0:T(8,128)S(1)}, f32[3,8,1,128]{3,1,2,0:T(8,128)S(1)}, u32[]{:S(2)}, u32[]{:S(2)}) collective-permute-start(f32[3,8,1,128]{3,1,2,0:T(8,128)S(1)} %bitcast.301), channel_id=1, source_target_pairs={{4,0},{8,4},{12,8},{16,12},{20,16},{24,20},{28,24},{0,28},{5,1},{9... | collective-permute-start | bytes 36872 | tf_op jit(solution)/shard_map/ppermute | solution.py:24
  133.8 6.4 %collective-permute-start.13 = (f32[3,8,1,128]{3,1,2,0:T(8,128)S(1)}, f32[3,8,1,128]{3,1,2,0:T(8,128)S(1)}, u32[]{:S(2)}, u32[]{:S(2)}) collective-permute-start(f32[3,8,1,128]{3,1,2,0:T(8,128)S(1)} %bitcast.299), channel_id=1, source_target_pairs={{0,4},{4,8},{8,12},{12,16},{16,20},{20,24},{24,28},{28,0},{1,5},{5... | collective-permute-start | bytes 36872 | tf_op jit(solution)/shard_map/ppermute | solution.py:23
  140.5 11.3 %collective-permute-start.15 = (f32[3,8,34,1]{3,2,1,0:T(8,128)S(1)}, f32[3,8,34,1]{3,2,1,0:T(8,128)S(1)}, u32[]{:S(2)}, u32[]{:S(2)}) collective-permute-start(f32[3,8,34,1]{3,2,1,0:T(8,128)S(1)} %get-tuple-element.101), channel_id=1, source_target_pairs={{0,1},{1,2},{2,3},{3,0},{4,5},{5,6},{6,7},{7,4},{8,9},{9,10},{10,1... | collective-permute-start | bytes 9800 | tf_op jit(solution)/shard_map/ppermute | solution.py:23
  141.0 12.5 %collective-permute-start.14 = (f32[3,8,34,1]{3,2,1,0:T(8,128)S(1)}, f32[3,8,34,1]{3,2,1,0:T(8,128)S(1)}, u32[]{:S(2)}, u32[]{:S(2)}) collective-permute-start(f32[3,8,34,1]{3,2,1,0:T(8,128)S(1)} %get-tuple-element.100), channel_id=1, source_target_pairs={{1,0},{2,1},{3,2},{0,3},{5,4},{6,5},{7,6},{4,7},{9,8},{10,9},{11,1... | collective-permute-start | bytes 9800 | tf_op jit(solution)/shard_map/ppermute | solution.py:24
  142.3 11.7 %copy-start.6 = (f32[3,8,32,128]{3,2,1,0:T(8,128)S(1)}, f32[3,8,32,128]{3,2,1,0:T(8,128)}, u32[]{:S(2)}) copy-start(f32[3,8,32,128]{3,2,1,0:T(8,128)} %copy-done.5) | copy-start | bytes 1179652
  142.3 11.7 %copy-start.10 = (f32[8,32,128]{2,1,0:T(8,128)S(1)}, f32[8,32,128]{2,1,0:T(8,128)}, u32[]{:S(2)}) copy-start(f32[8,32,128]{2,1,0:T(8,128)} %get-tuple-element.61) | copy-start | bytes 393220
  154.1 1.0 copy-start.4
  155.4 39.6 %copy-start.56 = (f32[6,8,32,128]{3,2,1,0:T(8,128)}, f32[6,8,32,128]{3,2,1,0:T(8,128)S(1)}, u32[]{:S(2)}) copy-start(f32[6,8,32,128]{3,2,1,0:T(8,128)S(1)} %bitcast_dynamic-update-slice_fusion) | copy-start | bytes 2359300
  (13 other events, 8.8 us)
where the time goes:
time: 197 us; the launch traced here: 195 us
  blocking collectives  72.4 us (37%)
  other arithmetic  39 us (20%)
  waiting for transfers between devices  35.2 us (18%)
  starting transfers between devices  24.9 us (13%)
  local copies, waits for them, and re-layouts  20.9 us (11%)
  between operations  2.15 us (1%)
    psum x1, blocking collectives, body(): shear = lax.psum(partial_shear, ('gx', 'gy'))  37.2 us
    psum x1, blocking collectives, broadcast(): return lax.psum(kept, axis)  35.2 us
    ppermute x8, waiting for transfers between devices, with_halo(): before = lax.ppermute(last, axis, up)  29 us
    ppermute x8, starting transfers between devices, with_halo(): after = lax.ppermute(leading, axis, down)  19.3 us
    unnamed x10, other arithmetic  12.5 us
    mul x1, other arithmetic, body(): velocity = velocity + 0.2 * buoy[None] * force  10.6 us
    add x1, other arithmetic, lookup(): total = total + jnp.where(zones == zone, column[zone], 0.0)  10.2 us
    unnamed x122, local copies, waits for them, and re-layouts  7.02 us
  transfers between devices with their start and end apart: 16, of which 10 were waited for; matrix products, arithmetic and copies ran while one was open for 15% of the time, Pallas kernels for 0%

commit v1 on v0

v1 whole, which is shorter than its diff:
```python
import functools

import jax
import jax.numpy as jnp
from jax import lax
from jax.experimental import pallas as pl
from jax.experimental.pallas import tpu as pltpu
from jax.sharding import PartitionSpec as P

CX = 32
CY = 128
NZ = 8
STEPS = 2
COARSE = 4
BLOCK = 8
ZONES = 16
BUILDINGS = 1024
FP_DEV = 64
HALO = 4
RING = CX + 2 * HALO
FIELDS = 10
PACKS = 3
CHUNK = 16
CXC = CX // COARSE
CYC = CY // COARSE
F32 = jnp.float32
VMEM_LIMIT = 32 * 1024 * 1024


def iota(shape, dim):
    return lax.broadcasted_iota(jnp.int32, shape, dim)


def take(x, idx):
    idx = jnp.broadcast_to(idx, x.shape)
    return jnp.take_along_axis(x, idx, axis=1, mode="promise_in_bounds")


def roll(x, shift, axis):
    size = x.shape[axis]
    shift = shift % size
    return x if shift == 0 else pltpu.roll(x, shift, axis)


def pack_kernel(n_gx, n_gy, vel, stress, zones, regional, gxa, gxb, gya, gyb, mesh_out):
    gx = lax.axis_index("gx")
    gy = lax.axis_index("gy")
    even_x = (gx & 1) == 0
    even_y = (gy & 1) == 0
    slot = iota((CX, CY), 1) // HALO
    low = iota((8, CY), 0) < 4
    lane8 = iota((8, CY), 1)

    def plane(f, z, a, b):
        if f < 6:
            return stress[f, z, a:b, :]
        if f < 9:
            return vel[f - 6, z, a:b, :]
        return zones[z, a:b, :].astype(F32)

    last_cols, first_cols = [], []
    for p in range(PACKS):
        lasts = jnp.zeros((CX, CY), F32)
        firsts = jnp.zeros((CX, CY), F32)
        for s in range(4):
            f = 4 * p + s
            if f >= FIELDS:
                continue
            for z in range(NZ):
                turned = roll(plane(f, z, 0, CX), 16 * z + 4 * s + 4, 1)
                at = 4 * z + s
                lasts = jnp.where(slot == at, turned, lasts)
                firsts = jnp.where(slot == (at + 1) % 32, turned, firsts)
        last_cols.append(lasts)
        first_cols.append(firsts)
        gya[p] = jnp.where(even_y, lasts, firsts)
        gyb[p] = jnp.where(even_y, firsts, lasts)

    for f in range(FIELDS):
        for q in range(NZ // 2):
            first = jnp.where(low, plane(f, 2 * q, 0, 8), roll(plane(f, 2 * q + 1, 0, 8), 4, 0))
            last = jnp.where(low, roll(plane(f, 2 * q + 1, CX - 8, CX), 4, 0), plane(f, 2 * q, CX - 8, CX))
            gxa[f * 4 + q] = jnp.where(even_x, last, first)
            gxb[f * 4 + q] = jnp.where(even_x, first, last)

    lane_g = iota((n_gx, CY), 1)
    part = lane_g // CYC
    digit = lane_g % 10
    group = lane_g // 10
    e_last = jnp.zeros((n_gx, CY), F32)
    e_first = jnp.zeros((n_gx, CY), F32)
    for s in range(STEPS):
        halves = [[regional[0, s, c, :, t * CY:(t + 1) * CY] for t in range(2)] for c in range(3)]
        nexts = [roll(halves[c][0], n_gx - 1, 0) for c in range(3)]
        befores = [roll(halves[c][1], 1, 0) for c in range(3)]
        for r in range(CXC):
            row = jnp.zeros((n_gx, CY), F32)
            for c in range(3):
                row = jnp.where(part == c, roll(halves[c][r // 4], CYC * (c - r % 4), 1), row)
            if r < 3:
                row = jnp.where(part == 3, roll(nexts[r], 96, 1), row)
            elif r < 6:
                row = jnp.where(part == 3, befores[r - 3], row)
            mesh_out[pl.ds(gy * CHUNK + s * CXC + r, n_gx, stride=n_gy * CHUNK), :] = row
        for c in range(3):
            here = group == s * 3 + c
            for is_last in (True, False):
                col = CYC - 1 if is_last else 0
                idx_low = jnp.where(digit < 4, digit * CYC + col, 0)
                idx_high = jnp.where((digit >= 4) & (digit < 8), (digit - 4) * CYC + col, 0)
                edge = jnp.where(digit < 4, take(halves[c][0], idx_low), take(halves[c][1], idx_high))
                edge = jnp.where(digit == 8, take(nexts[c], jnp.full_like(digit, col)), edge)
                edge = jnp.where(digit == 9, take(befores[c], jnp.full_like(digit, 3 * CYC + col)), edge)
                if is_last:
                    e_last = jnp.where(here, edge, e_last)
                else:
                    e_first = jnp.where(here, edge, e_first)
    right = (gy + 1) % n_gy
    left = (gy + n_gy - 1) % n_gy
    for i in range(n_gx):
        for edges, to in ((e_last, right), (e_first, left)):
            at = pl.multiple_of((i * n_gy + to) * CHUNK + 8, 8)
            mesh_out[pl.ds(at, 8), :] = jnp.broadcast_to(edges[i:i + 1, :], (8, CY))

    for step_x, rows, natural in ((1, slice(CX - 8, CX), ~low), (n_gx - 1, slice(0, 8), low)):
        to_x = (gx + step_x) % n_gx
        for cols, to_y in ((last_cols, right), (first_cols, left)):
            at = pl.multiple_of((to_x * n_gy + to_y) * CHUNK, CHUNK)
            mesh_out[pl.ds(at, 8), :] = jnp.where(natural, cols[0][rows, :], roll(cols[1][rows, :], 4, 0))
            at = pl.multiple_of(at + 8, 8)
            mesh_out[pl.ds(at, 8), :] = jnp.where(natural, cols[2][rows, :], mesh_out[pl.ds(at, 8), :])


def step_kernel(
    n_gx, n_gy,
    vel, stress, zones, table, own_a, own_b, ra, rb, ca, cb, mesh_in, owner, building, block,
    vel_out, stress_out, shares,
    S, V, Z, LAM, MU, BUOY, BF, BM, DRM, sems, out_sems,
):
    gx = lax.axis_index("gx")
    gy = lax.axis_index("gy")
    even_x = (gx & 1) == 0
    even_y = (gy & 1) == 0
    loads = [
        pltpu.make_async_copy(stress, S.at[:, :, pl.ds(0, CX), :], sems.at[0]),
        pltpu.make_async_copy(vel, V.at[:, :, pl.ds(0, CX), :], sems.at[1]),
        pltpu.make_async_copy(zones, Z.at[:, pl.ds(0, CX), :], sems.at[2]),
    ]
    for copy in loads:
        copy.start()
    low = iota((8, CY), 0) < 4
    lane8 = iota((8, CY), 1)
    sub8 = iota((8, CY), 0)
    lane = iota((RING, CY), 1)
    quarter8 = (lane8 // 4) % 4
    quarter = (lane // 4) % 4
    tail = slice(CX, RING)

    for f in range(FIELDS):
        for q in range(NZ // 2):
            k = f * 4 + q
            after = jnp.where(even_x, ra[k], rb[k])
            before = jnp.where(even_x, rb[k], ra[k])
            one = jnp.where(low, after, before)
            two = roll(jnp.where(low, before, after), 4, 0)
            if f < 6:
                S[f, 2 * q, tail, :] = one
                S[f, 2 * q + 1, tail, :] = two
            elif f < 9:
                V[f - 6, 2 * q, tail, :] = one
                V[f - 6, 2 * q + 1, tail, :] = two
            else:
                Z[2 * q, tail, :] = one.astype(jnp.int32)
                Z[2 * q + 1, tail, :] = two.astype(jnp.int32)

    up_x = (gx + 1) % n_gx
    down_x = (gx + n_gx - 1) % n_gx
    left_y = (gy + n_gy - 1) % n_gy
    right_y = (gy + 1) % n_gy

    def tile_of(x, y, t):
        at = pl.multiple_of((x * n_gy + y) * CHUNK + 8 * t, 8)
        return mesh_in[pl.ds(at, 8), :]

    def corner_rows(y):
        a0, a1 = tile_of(up_x, y, 0), tile_of(up_x, y, 1)
        b0, b1 = tile_of(down_x, y, 0), tile_of(down_x, y, 1)
        return [
            jnp.where(low, a0, b0),
            roll(jnp.where(low, b0, a0), 4, 0),
            jnp.where(low, a1, b1),
        ]

    left_tail = corner_rows(left_y)
    right_tail = corner_rows(right_y)
    own_idx = jnp.where(quarter8 == 1, lane8 % 16 - 4, jnp.where(quarter8 == 2, lane8 % 16 - 8 + CY - 4, 0))
    for f in range(FIELDS):
        p, s = f // 4, f % 4
        own_first = jnp.where(even_y, own_b[p], own_a[p])
        own_last = jnp.where(even_y, own_a[p], own_b[p])
        from_left = jnp.where(even_y, cb[p], ca[p])
        from_right = jnp.where(even_y, ca[p], cb[p])
        part = jnp.where(
            quarter[:CX] == 0, roll(from_left, -4 * s, 1),
            jnp.where(quarter[:CX] == 1, roll(own_first, -4 * s, 1),
                      jnp.where(quarter[:CX] == 2, roll(own_last, 8 - 4 * s, 1), roll(from_right, 8 - 4 * s, 1))),
        )
        BF[f, 0:CX, :] = part
        own = jnp.zeros((8, CY), F32)
        for z in range(NZ):
            if f < 6:
                src = S[f, z, tail, :]
            elif f < 9:
                src = V[f - 6, z, tail, :]
            else:
                src = Z[z, tail, :].astype(F32)
            own = jnp.where(lane8 // 16 == z, take(src, own_idx), own)
        end = jnp.where(
            quarter8 == 0, roll(left_tail[p], -4 * s, 1),
            jnp.where(quarter8 == 3, roll(right_tail[p], 8 - 4 * s, 1), own),
        )
        BF[f, tail, :] = end

    my_owner = owner[gy]
    left_owner = owner[left_y]
    right_owner = owner[right_y]
    main_at = (my_owner * n_gy + gy) * CHUNK
    left_at = (left_owner * n_gy + left_y) * CHUNK + 8 + jnp.where(left_owner == up_x, 7, 0)
    right_at = (right_owner * n_gy + right_y) * CHUNK + 8 + jnp.where(right_owner == up_x, 7, 0)
    left_edge = jnp.broadcast_to(mesh_in[pl.ds(left_at, 1), :], (8, CY))
    right_edge = jnp.broadcast_to(mesh_in[pl.ds(right_at, 1), :], (8, CY))
    deepest = lane8 >= 16 * (NZ - 1)
    for s in range(STEPS):
        for c in range(3):
            for q in range(RING // 8):
                if q < 4:
                    row_a = mesh_in[pl.ds(main_at + s * CXC + 2 * q, 1), :]
                    row_b = mesh_in[pl.ds(main_at + s * CXC + 2 * q + 1, 1), :]
                    base = c * CYC
                else:
                    row_a = mesh_in[pl.ds(main_at + s * CXC + c, 1), :]
                    row_b = mesh_in[pl.ds(main_at + s * CXC + 3 + c, 1), :]
                    base = 3 * CYC
                rows = jnp.where(low, jnp.broadcast_to(row_a, (8, CY)), jnp.broadcast_to(row_b, (8, CY)))
                DRM[s, c, 0, 8 * q:8 * q + 8, :] = take(rows, base + lane8 // COARSE)
                inner = take(rows, base + jnp.where(quarter8 == 2, CYC - 1, 0))
                at = (s * 3 + c) * 10 + 2 * q
                edge_idx = jnp.where(low, at, at + 1)
                value = jnp.where(
                    quarter8 == 0, take(left_edge, edge_idx),
                    jnp.where(quarter8 == 3, take(right_edge, edge_idx), inner),
                )
                DRM[s, c, 1, 8 * q:8 * q + 8, :] = jnp.where(deepest, value, 0.0)

    for copy in loads:
        copy.wait()

    scaled = table[...] * 0.1
    spread = jnp.concatenate([scaled] * (CY // ZONES), axis=1)
    columns = [jnp.broadcast_to(spread[k:k + 1, :], (RING, CY)) for k in range(3)]
    for z in range(NZ):
        ids = Z[z]
        LAM[z] = take(columns[0], ids)
        MU[z] = take(columns[1], ids)
        BUOY[z] = take(columns[2], ids)
    ids = BF[9].astype(jnp.int32)
    for k in range(3):
        BM[k] = take(columns[k], ids)

    def dx(x):
        return roll(x, RING - 1, 0) - roll(x, 1, 0)

    def dy(x, band, z):
        idx = jnp.where(lane == 0, 16 * z + 3, 16 * z + 12)
        seam = take(band, idx)
        return jnp.where(lane == CY - 1, seam, roll(x, CY - 1, 1)) - jnp.where(lane == 0, seam, roll(x, 1, 1))

    def dz(ref, f, z):
        if z == 0:
            return ref[f, 1]
        if z == NZ - 1:
            return -ref[f, NZ - 2]
        return ref[f, z + 1] - ref[f, z - 1]

    def band_dy(x):
        return roll(x, CY - 1, 1) - roll(x, 1, 1)

    def band_dz(x):
        return jnp.where(lane < CY - 16, roll(x, CY - 16, 1), 0.0) - jnp.where(lane >= 16, roll(x, 16, 1), 0.0)

    XX, XZ, XY, YY, YZ, ZZ = range(6)
    saves = []
    for step in range(STEPS):
        for z in range(NZ):
            sxy, sxz, syz = S[XY, z], S[XZ, z], S[YZ, z]
            fx = dx(S[XX, z]) + dy(sxy, BF[XY], z) + dz(S, XZ, z)
            fy = dx(sxy) + dy(S[YY, z], BF[YY], z) + dz(S, YZ, z)
            fz = dx(sxz) + dy(syz, BF[YZ], z) + dz(S, ZZ, z)
            force = [fx, fy, fz]
            if z == NZ - 1:
                force = [force[c] + (20.0 * MU[z]) * DRM[step, c, 0] for c in range(3)]
            for c in range(3):
                V[c, z] = V[c, z] + BUOY[z] * force[c]
        sxy, sxz, syz = BF[XY], BF[XZ], BF[YZ]
        force = [
            dx(BF[XX]) + band_dy(sxy) + band_dz(sxz),
            dx(sxy) + band_dy(BF[YY]) + band_dz(syz),
            dx(sxz) + band_dy(syz) + band_dz(BF[ZZ]),
        ]
        for c in range(3):
            BF[6 + c] = BF[6 + c] + BM[2] * (force[c] + (20.0 * BM[1]) * DRM[step, c, 1])
        if step == STEPS - 1:
            save = pltpu.make_async_copy(V.at[:, :, pl.ds(0, CX), :], vel_out, out_sems.at[NZ])
            save.start()
            saves.append(save)
        for z in range(NZ):
            vx, vy, vz = V[0, z], V[1, z], V[2, z]
            lam, mu = LAM[z], MU[z]
            xx, yy, zz = dx(vx), dy(vy, BF[7], z), dz(V, 2, z)
            theta = lam * (xx + yy + zz)
            two = mu + mu
            S[XX, z] = S[XX, z] + (theta + two * xx)
            S[YY, z] = S[YY, z] + (theta + two * yy)
            S[ZZ, z] = S[ZZ, z] + (theta + two * zz)
            S[XZ, z] = S[XZ, z] + mu * (dz(V, 0, z) + dx(vz))
            S[XY, z] = S[XY, z] + mu * (dy(vx, BF[6], z) + dx(vy))
            S[YZ, z] = S[YZ, z] + mu * (dz(V, 1, z) + dy(vz, BF[8], z))
            if step == STEPS - 1:
                save = pltpu.make_async_copy(S.at[:, z, pl.ds(0, CX), :], stress_out.at[:, z], out_sems.at[z])
                save.start()
                saves.append(save)
        if step < STEPS - 1:
            vx, vy, vz = BF[6], BF[7], BF[8]
            lam, mu = BM[0], BM[1]
            xx, yy, zz = dx(vx), band_dy(vy), band_dz(vz)
            theta = lam * (xx + yy + zz)
            two = mu + mu
            BF[XX] = BF[XX] + (theta + two * xx)
            BF[YY] = BF[YY] + (theta + two * yy)
            BF[ZZ] = BF[ZZ] + (theta + two * zz)
            BF[XZ] = BF[XZ] + mu * (band_dz(vx) + dx(vz))
            BF[XY] = BF[XY] + mu * (band_dy(vx) + dx(vy))
            BF[YZ] = BF[YZ] + mu * (band_dz(vy) + band_dy(vz))

    total = jnp.zeros((8, CY), F32)
    for c, f in enumerate((XZ, YZ)):
        for r in range(CX // BLOCK):
            row = jnp.sum(S[f, 1, 8 * r:8 * r + 8, :], axis=0, keepdims=True)
            total = jnp.where(sub8 == 4 * c + r, jnp.broadcast_to(row, (8, CY)), total)
    for shift in (1, 2, 4):
        total = total + roll(total, CY - shift, 1)
    total = total * (1.0 / (BLOCK * BLOCK))
    ids = jnp.broadcast_to(jnp.concatenate([block[0], block[0]], axis=1), (8, CY))
    cells = CY // BLOCK
    picked = take(total, (ids % cells) * BLOCK)
    mine = (sub8 % 4 == ids // cells) & (sub8 // 4 == lane8 // FP_DEV)
    values = jnp.sum(jnp.where(mine, picked, 0.0), axis=0, keepdims=True)
    names = jnp.concatenate([building[0], building[0]], axis=1).astype(F32)
    message = jnp.concatenate([values, names], axis=0)
    shares[...] = jnp.broadcast_to(message[None], shares.shape)
    for save in saves:
        save.wait()


def sum_kernel(n, shares, out):
    half = n // 2
    low = iota((half, CY), 1) < FP_DEV
    values = shares[:, 0, :]
    names = shares[:, 1, :].astype(jnp.int32)
    entry = [
        jnp.where(low, values[:half], roll(values[half:], FP_DEV, 1)),
        jnp.where(low, roll(values[:half], FP_DEV, 1), values[half:]),
    ]
    names = jnp.where(low, names[:half], names[half:])
    high = names // CY
    names = names % CY
    n_high = BUILDINGS // CY
    rows = iota((n_high, CY), 0)
    wanted = iota((CY, CY), 0)
    acc = jnp.zeros((6 * n_high, CY), F32)
    for k in range(half):
        hot = (jnp.broadcast_to(names[k:k + 1], (CY, CY)) == wanted).astype(F32).astype(jnp.bfloat16)
        here = jnp.broadcast_to(high[k:k + 1], (n_high, CY)) == rows
        left = []
        for c in range(2):
            rest = jnp.where(here, jnp.broadcast_to(entry[c][k:k + 1], (n_high, CY)), 0.0)
            for _ in range(3):
                piece = rest.astype(jnp.bfloat16)
                rest = rest - piece.astype(F32)
                left.append(piece.astype(F32))
        left = jnp.concatenate(left, axis=0).astype(jnp.bfloat16)
        acc = acc + lax.dot_general(left, hot, (((1,), (1,)), ((), ())), preferred_element_type=F32)
    for c in range(2):
        base = 3 * c * n_high
        out[c] = acc[base:base + n_high] + acc[base + n_high:base + 2 * n_high] + acc[base + 2 * n_high:base + 3 * n_high]


def pairs_near(n):
    return [(i, i ^ 1) for i in range(n)]


def pairs_far(n):
    return [(i, (i + 1) % n if i % 2 else (i - 1) % n) for i in range(n)]


def body(n_gx, n_gy, velocity, stress, zones, zone_table, regional, owner, building, block):
    n = n_gx * n_gy
    vmem = pl.BlockSpec(memory_space=pltpu.VMEM)
    smem = pl.BlockSpec(memory_space=pltpu.SMEM)
    anywhere = pl.BlockSpec(memory_space=pl.ANY)
    params = pltpu.CompilerParams(vmem_limit_bytes=VMEM_LIMIT)
    rows = jax.ShapeDtypeStruct((FIELDS * 4, 8, CY), F32)
    cols = jax.ShapeDtypeStruct((PACKS, CX, CY), F32)
    gxa, gxb, gya, gyb, slices = pl.pallas_call(
        functools.partial(pack_kernel, n_gx, n_gy),
        out_shape=(rows, rows, cols, cols, jax.ShapeDtypeStruct((n * CHUNK, CY), F32)),
        in_specs=[vmem] * 4,
        out_specs=(vmem,) * 5,
        compiler_params=params,
        name="pack",
    )(velocity, stress, zones, regional)
    rb = lax.ppermute(gxb, "gx", pairs_far(n_gx))
    ra = lax.ppermute(gxa, "gx", pairs_near(n_gx))
    ca = lax.ppermute(gya, "gy", pairs_near(n_gy))
    cb = lax.ppermute(gyb, "gy", pairs_far(n_gy))
    got = lax.all_to_all(slices.reshape(n, CHUNK, CY), ("gx", "gy"), 0, 0).reshape(n * CHUNK, CY)
    full = (NZ, RING, CY)
    vel_out, stress_out, shares = pl.pallas_call(
        functools.partial(step_kernel, n_gx, n_gy),
        out_shape=(
            jax.ShapeDtypeStruct(velocity.shape, F32),
            jax.ShapeDtypeStruct(stress.shape, F32),
            jax.ShapeDtypeStruct((n, 2, CY), F32),
        ),
        in_specs=[anywhere] * 3 + [vmem] * 8 + [smem] + [vmem] * 2,
        out_specs=(anywhere, anywhere, vmem),
        scratch_shapes=[
            pltpu.VMEM((6,) + full, F32),
            pltpu.VMEM((3,) + full, F32),
            pltpu.VMEM(full, jnp.int32),
            pltpu.VMEM(full, F32),
            pltpu.VMEM(full, F32),
            pltpu.VMEM(full, F32),
            pltpu.VMEM((FIELDS, RING, CY), F32),
            pltpu.VMEM((3, RING, CY), F32),
            pltpu.VMEM((STEPS, 3, 2, RING, CY), F32),
            pltpu.SemaphoreType.DMA((3,)),
            pltpu.SemaphoreType.DMA((NZ + 1,)),
        ],
        compiler_params=params,
        name="steps",
    )(velocity, stress, zones, zone_table, gya, gyb, ra, rb, ca, cb, got, owner, building, block)
    every = lax.all_to_all(shares, ("gx", "gy"), 0, 0)
    shear = pl.pallas_call(
        functools.partial(sum_kernel, n),
        out_shape=jax.ShapeDtypeStruct((2, BUILDINGS // CY, CY), F32),
        in_specs=[vmem],
        out_specs=vmem,
        compiler_params=params,
        name="sum_by_building",
    )(every)
    return vel_out, stress_out, shear.reshape(2, BUILDINGS)


def solution(mesh):
    n_gx, n_gy = mesh.shape["gx"], mesh.shape["gy"]
    return jax.shard_map(
        functools.partial(body, n_gx, n_gy),
        mesh=mesh,
        in_specs=(
            P(None, None, "gx", "gy"),
            P(None, None, "gx", "gy"),
            P(None, "gx", "gy"),
            P(),
            P("gx", None, None, None, "gy"),
            P(),
            P("gx", "gy", None),
            P("gx", "gy", None),
        ),
        out_specs=(P(None, None, "gx", "gy"), P(None, None, "gx", "gy"), P()),
        check_vma=False,
    )
```

time: 197 us -> 44.3 us (0.22)
  blocking collectives: 72.4 us -> 11 us
  other arithmetic: 39 us -> 0 us
  waiting for transfers between devices: 35.2 us -> 6.57 us
  local copies, waits for them, and re-layouts: 20.9 us -> 4.46 us
  starting transfers between devices: 24.9 us -> 14.1 us
  Pallas kernels: 0 us -> 7.09 us
    psum x2 -> x0, blocking collectives: 72.4 us -> none  [the longest x1 37.2 us: body(): shear = lax.psum(partial_shear, ('gx', 'gy'))]
    ppermute x16 -> x4, waiting for transfers between devices: 35.2 us -> 6.57 us  [the longest x1 2.48 us: body(): cb = lax.ppermute(gyb, 'gy', pairs_far(n_gy))]
    ppermute x16 -> x4, starting transfers between devices: 24.9 us -> 6.76 us  [the longest x1 3.31 us: body(): rb = lax.ppermute(gxb, 'gx', pairs_far(n_gx))]
    mul x6 -> x0, other arithmetic: 14 us -> none  [the longest x1 10.6 us: body(): velocity = velocity + 0.2 * buoy[None] * force]
    unnamed x10 -> x0, other arithmetic: 12.5 us -> none
    all_to_all x0 -> x1, blocking collectives: none -> 11 us  [body(): every = lax.all_to_all(shares, ('gx', 'gy'), 0, 0)]
    add x3 -> x0, other arithmetic: 10.3 us -> none  [the longest x1 10.2 us: lookup(): total = total + jnp.where(zones == zone, column[zone], 0.0)]
    slice x20 -> x0, local copies, waits for them, and re-layouts: 7.41 us -> none  [the longest x4 2.57 us: with_halo(): last = lax.slice_in_dim(value, length - width, length, axis=dim)]
  transfers between devices with their start and end apart: 16 -> 5, of which waited for: 10 -> 3; matrix products, arithmetic and copies ran while one was open for 15% -> 0% of each run, Pallas kernels for 0% -> 0%
where the time goes in v1:
time: 44.3 us; the launch traced here: 43.9 us
  starting transfers between devices  14.1 us (32%)
  blocking collectives  11 us (25%)
  Pallas kernels  7.09 us (16%)
  waiting for transfers between devices  6.57 us (15%)
  local copies, waits for them, and re-layouts  4.46 us (10%)
  between operations  0.73 us (2%)
    all_to_all x1, blocking collectives, body(): every = lax.all_to_all(shares, ('gx', 'gy'), 0, 0)  11 us
    all_to_all x1, starting transfers between devices, body(): lax.all_to_all(slices.reshape(n, CHUNK, CY), ('gx', 'gy'), 0, 0)  7.3 us
    pallas_call x1, Pallas kernels, body(): pl.pallas_call(functools.partial(step_kernel, n_gx, n_gy), out_shape=(jax...  5.29 us
    unnamed x23, local copies, waits for them, and re-layouts  4.46 us
    ppermute x1, starting transfers between devices, body(): rb = lax.ppermute(gxb, 'gx', pairs_far(n_gx))  3.31 us
    ppermute x1, waiting for transfers between devices, body(): cb = lax.ppermute(gyb, 'gy', pairs_far(n_gy))  2.48 us
    ppermute x1, waiting for transfers between devices, body(): rb = lax.ppermute(gxb, 'gx', pairs_far(n_gx))  2.3 us
    ppermute x1, starting transfers between devices, body(): ra = lax.ppermute(gxa, 'gx', pairs_near(n_gx))  1.83 us
  transfers between devices with their start and end apart: 5, of which 3 were waited for; matrix products, arithmetic and copies ran while one was open for 0% of the time, Pallas kernels for 0%

profile of v1, /device:TPU:0, one launch (start us, length us, event | category | flops | bytes accessed | tf_op | source)
XLA Modules:
  0.0 43.9 jit_solution(6544563808511084705)
XLA Ops:
  0.6 0.0 copy-start
  0.6 1.1 %copy-done = f32[6,8,32,128]{3,2,1,0:T(8,128)S(1)} copy-done((f32[6,8,32,128]{3,2,1,0:T(8,128)S(1)}, f32[6,8,32,128]{3,2,1,0:T(8,128)}, u32[]{:S(2)}) %copy-start) | copy-done | bytes 786456
  1.8 0.0 copy-start.2
  1.8 1.0 %copy-done.2 = f32[3,8,32,128]{3,2,1,0:T(8,128)S(1)} copy-done((f32[3,8,32,128]{3,2,1,0:T(8,128)S(1)}, f32[3,8,32,128]{3,2,1,0:T(8,128)}, u32[]{:S(2)}) %copy-start.2) | copy-done | bytes 393240
  2.8 0.0 copy-start.4
  2.8 0.9 %copy-done.4 = s32[8,32,128]{2,1,0:T(8,128)S(1)} copy-done((s32[8,32,128]{2,1,0:T(8,128)S(1)}, s32[8,32,128]{2,1,0:T(8,128)}, u32[]{:S(2)}) %copy-start.4) | copy-done | bytes 131096
  3.7 0.0 copy-start.6
  3.7 0.8 %copy-done.6 = f32[1,2,3,8,256]{4,3,2,1,0:T(8,128)S(1)} copy-done((f32[1,2,3,8,256]{4,3,2,1,0:T(8,128)S(1)}, f32[1,2,3,8,256]{4,3,2,1,0:T(8,128)}, u32[]{:S(2)}) %copy-start.6) | copy-done | bytes 49176
  4.5 0.0 copy-start.1
  4.5 1.3 %pack.1 = (f32[40,8,128]{2,1,0:T(8,128)S(1)}, f32[40,8,128]{2,1,0:T(8,128)S(1)}, f32[3,32,128]{2,1,0:T(8,128)S(1)}, f32[3,32,128]{2,1,0:T(8,128)S(1)}, f32[512,128]{1,0:T(8,128)}) custom-call(f32[3,8,32,128]{3,2,1,0:T(8,128)S(1)} %copy-done.2, f32[6,8,32,128]{3,2,1,0:T(8,128)S(1)} %copy-done, s32[8,32,128]{2,1,0:T(8,128)S(1)} %copy-done.4, ...), custom_call_target="tpu_custom_call" | custom-call | tf_op jit(solution)/shard_map/pack/pallas_call | solution.py:414
  5.8 0.0 copy-start.3
  5.8 0.0 copy-start.5
  5.8 7.3 %all-to-all-start = ((f32[32,16,128]{2,1,0:T(8,128)}), f32[32,16,128]{2,1,0:T(8,128)S(1)}, u32[]{:S(2)}, u32[]{:S(2)}) async-start(f32[32,16,128]{2,1,0:T(8,128)} %bitcast), calls=%async_computation | async-start | bytes 524288 | tf_op jit(solution)/shard_map/all_to_all | solution.py:426
  13.1 1.8 %collective-permute-start = (f32[40,8,128]{2,1,0:T(8,128)S(1)}, f32[40,8,128]{2,1,0:T(8,128)S(1)}, u32[]{:S(2)}, u32[]{:S(2)}) collective-permute-start(f32[40,8,128]{2,1,0:T(8,128)S(1)} %get-tuple-element.13), channel_id=1, source_target_pairs={{0,4},{4,0},{8,12},{12,8},{16,20},{20,16},{24,28},{28,24},{1,5},{5... | collective-permute-start | bytes 491528 | tf_op jit(solution)/shard_map/ppermute | solution.py:423
  14.9 3.3 %collective-permute-start.1 = (f32[40,8,128]{2,1,0:T(8,128)S(1)}, f32[40,8,128]{2,1,0:T(8,128)S(1)}, u32[]{:S(2)}, u32[]{:S(2)}) collective-permute-start(f32[40,8,128]{2,1,0:T(8,128)S(1)} %get-tuple-element.14), channel_id=1, source_target_pairs={{0,28},{4,8},{8,4},{12,16},{16,12},{20,24},{24,20},{28,0},{1,29},{... | collective-permute-start | bytes 491528 | tf_op jit(solution)/shard_map/ppermute | solution.py:422
  18.2 0.0 copy-start.7
  18.2 0.0 collective-permute-start.2
  18.2 0.0 copy-start.8
  18.2 0.0 copy-start.9
  18.2 0.0 copy-start.10
  18.3 1.6 %collective-permute-start.3 = (f32[3,32,128]{2,1,0:T(8,128)S(1)}, f32[3,32,128]{2,1,0:T(8,128)S(1)}, u32[]{:S(2)}, u32[]{:S(2)}) collective-permute-start(f32[3,32,128]{2,1,0:T(8,128)S(1)} %get-tuple-element.12.own_b), channel_id=1, source_target_pairs={{0,3},{1,2},{2,1},{3,0},{4,7},{5,6},{6,5},{7,4},{8,11},{9,10},{10,... | collective-permute-start | bytes 147464 | tf_op jit(solution)/shard_map/ppermute | solution.py:425
  19.9 0.0 collective-permute-done.2.ca
  19.9 2.5 %collective-permute-done.3.cb = f32[3,32,128]{2,1,0:T(8,128)S(1)} collective-permute-done((f32[3,32,128]{2,1,0:T(8,128)S(1)}, f32[3,32,128]{2,1,0:T(8,128)S(1)}, u32[]{:S(2)}, u32[]{:S(2)}) %collective-permute-start.3) | collective-permute-done | bytes 49184 | tf_op jit(solution)/shard_map/ppermute | solution.py:425
  22.3 1.8 %collective-permute-done.ra = f32[40,8,128]{2,1,0:T(8,128)S(1)} collective-permute-done((f32[40,8,128]{2,1,0:T(8,128)S(1)}, f32[40,8,128]{2,1,0:T(8,128)S(1)}, u32[]{:S(2)}, u32[]{:S(2)}) %collective-permute-start) | collective-permute-done | bytes 163872 | tf_op jit(solution)/shard_map/ppermute | solution.py:423
  24.1 2.3 %collective-permute-done.1.rb = f32[40,8,128]{2,1,0:T(8,128)S(1)} collective-permute-done((f32[40,8,128]{2,1,0:T(8,128)S(1)}, f32[40,8,128]{2,1,0:T(8,128)S(1)}, u32[]{:S(2)}, u32[]{:S(2)}) %collective-permute-start.1) | collective-permute-done | bytes 163872 | tf_op jit(solution)/shard_map/ppermute | solution.py:422
  26.4 0.0 all-to-all-done
  26.4 0.0 copy-done.1
  26.4 0.0 copy-done.3
  26.4 0.0 copy-done.5
  26.5 0.0 copy-done.7
  26.5 0.0 copy-done.8
  26.5 0.0 copy-done.9
  26.5 0.0 copy-done.10
  26.5 5.3 %steps.1 = (f32[3,8,32,128]{3,2,1,0:T(8,128)}, f32[6,8,32,128]{3,2,1,0:T(8,128)}, f32[32,2,128]{2,1,0:T(2,128)S(1)}) custom-call(f32[3,8,32,128]{3,2,1,0:T(8,128)S(1)} %copy-done.3, f32[6,8,32,128]{3,2,1,0:T(8,128)S(1)} %copy-done.1, s32[8,32,128]{2,1,0:T(8,128)S(1)} %copy-done.5, f32[3,16]{1,0:T(4,128)S(1)} %copy-done.7, ...), custom_call_target="tpu_custom_call" | custom-call | tf_op jit(solution)/shard_map/steps/pallas_call | solution.py:428
  31.8 11.0 %all_to_all.10.shares = f32[32,2,128]{2,1,0:T(2,128)S(1)} all-to-all(f32[32,2,128]{2,1,0:T(2,128)S(1)} %get-tuple-element.18), channel_id=1, replica_groups=mesh['gx'=8,'gy'=4] {'gx','gy'}, dimensions={0} | all-to-all | bytes 65536 | tf_op jit(solution)/shard_map/all_to_all | solution.py:453
  42.8 0.5 %sum_by_building.1 = f32[2,8,128]{2,1,0:T(8,128)S(1)} custom-call(f32[32,2,128]{2,1,0:T(2,128)S(1)} %all_to_all.10.shares), custom_call_target="tpu_custom_call" | custom-call | tf_op jit(solution)/shard_map/sum_by_building/pallas_call | solution.py:454
  43.3 0.6 %copy.13 = f32[1,2,8,128]{3,1,2,0:T(2,128)} copy(f32[1,2,8,128]{3,2,1,0:T(8,128)S(1)} %bitcast.7) | data formatting | bytes 16384
Async XLA Ops:
  0.6 1.1 %copy-start = (f32[6,8,32,128]{3,2,1,0:T(8,128)S(1)}, f32[6,8,32,128]{3,2,1,0:T(8,128)}, u32[]{:S(2)}) copy-start(f32[6,8,32,128]{3,2,1,0:T(8,128)} %stress.3) | copy-start | bytes 2359300
  1.8 1.0 %copy-start.2 = (f32[3,8,32,128]{3,2,1,0:T(8,128)S(1)}, f32[3,8,32,128]{3,2,1,0:T(8,128)}, u32[]{:S(2)}) copy-start(f32[3,8,32,128]{3,2,1,0:T(8,128)} %vel.3) | copy-start | bytes 1179652
  2.8 0.9 %copy-start.4 = (s32[8,32,128]{2,1,0:T(8,128)S(1)}, s32[8,32,128]{2,1,0:T(8,128)}, u32[]{:S(2)}) copy-start(s32[8,32,128]{2,1,0:T(8,128)} %zones.3) | copy-start | bytes 393220
  3.7 0.8 %copy-start.6 = (f32[1,2,3,8,256]{4,3,2,1,0:T(8,128)S(1)}, f32[1,2,3,8,256]{4,3,2,1,0:T(8,128)}, u32[]{:S(2)}) copy-start(f32[1,2,3,8,256]{4,3,2,1,0:T(8,128)} %regional.1) | copy-start | bytes 147460
  4.5 22.0 %copy-start.1 = (f32[6,8,32,128]{3,2,1,0:T(8,128)S(1)}, f32[6,8,32,128]{3,2,1,0:T(8,128)}, u32[]{:S(2)}) copy-start(f32[6,8,32,128]{3,2,1,0:T(8,128)} %stress.3) | copy-start | bytes 2359300
  5.8 20.7 %copy-start.3 = (f32[3,8,32,128]{3,2,1,0:T(8,128)S(1)}, f32[3,8,32,128]{3,2,1,0:T(8,128)}, u32[]{:S(2)}) copy-start(f32[3,8,32,128]{3,2,1,0:T(8,128)} %vel.3) | copy-start | bytes 1179652
  5.8 20.7 %copy-start.5 = (s32[8,32,128]{2,1,0:T(8,128)S(1)}, s32[8,32,128]{2,1,0:T(8,128)}, u32[]{:S(2)}) copy-start(s32[8,32,128]{2,1,0:T(8,128)} %zones.3) | copy-start | bytes 393220
  5.8 20.7 %all-to-all-start = ((f32[32,16,128]{2,1,0:T(8,128)}), f32[32,16,128]{2,1,0:T(8,128)S(1)}, u32[]{:S(2)}, u32[]{:S(2)}) async-start(f32[32,16,128]{2,1,0:T(8,128)} %bitcast), calls=%async_computation | async-start | bytes 524288 | tf_op jit(solution)/shard_map/all_to_all | solution.py:426
  13.1 11.1 %collective-permute-start = (f32[40,8,128]{2,1,0:T(8,128)S(1)}, f32[40,8,128]{2,1,0:T(8,128)S(1)}, u32[]{:S(2)}, u32[]{:S(2)}) collective-permute-start(f32[40,8,128]{2,1,0:T(8,128)S(1)} %get-tuple-element.13), channel_id=1, source_target_pairs={{0,4},{4,0},{8,12},{12,8},{16,20},{20,16},{24,28},{28,24},{1,5},{5... | collective-permute-start | bytes 491528 | tf_op jit(solution)/shard_map/ppermute | solution.py:423
  14.9 11.5 %collective-permute-start.1 = (f32[40,8,128]{2,1,0:T(8,128)S(1)}, f32[40,8,128]{2,1,0:T(8,128)S(1)}, u32[]{:S(2)}, u32[]{:S(2)}) collective-permute-start(f32[40,8,128]{2,1,0:T(8,128)S(1)} %get-tuple-element.14), channel_id=1, source_target_pairs={{0,28},{4,8},{8,4},{12,16},{16,12},{20,24},{24,20},{28,0},{1,29},{... | collective-permute-start | bytes 491528 | tf_op jit(solution)/shard_map/ppermute | solution.py:422
  18.2 8.2 %copy-start.7 = (f32[3,16]{1,0:T(4,128)S(1)}, f32[3,16]{1,0:T(4,128)}, u32[]{:S(2)}) copy-start(f32[3,16]{1,0:T(4,128)} %table.1) | copy-start | bytes 580
  18.2 1.6 %collective-permute-start.2 = (f32[3,32,128]{2,1,0:T(8,128)S(1)}, f32[3,32,128]{2,1,0:T(8,128)S(1)}, u32[]{:S(2)}, u32[]{:S(2)}) collective-permute-start(f32[3,32,128]{2,1,0:T(8,128)S(1)} %get-tuple-element.11.own_a), channel_id=1, source_target_pairs={{0,1},{1,0},{2,3},{3,2},{4,5},{5,4},{6,7},{7,6},{8,9},{9,8},{10,11... | collective-permute-start | bytes 147464 | tf_op jit(solution)/shard_map/ppermute | solution.py:424
  18.2 8.2 %copy-start.8 = (s32[4]{0:T(128)S(1)}, s32[4]{0:T(128)}, u32[]{:S(2)}) copy-start(s32[4]{0:T(128)} %owner.1) | copy-start | bytes 52
  18.2 8.2 %copy-start.9 = (s32[1,1,64]{2,1,0:T(1,128)S(1)}, s32[1,1,64]{2,1,0:T(1,128)}, u32[]{:S(2)}) copy-start(s32[1,1,64]{2,1,0:T(1,128)} %building.1) | copy-start | bytes 772
  18.2 8.2 %copy-start.10 = (s32[1,1,64]{2,1,0:T(1,128)S(1)}, s32[1,1,64]{2,1,0:T(1,128)}, u32[]{:S(2)}) copy-start(s32[1,1,64]{2,1,0:T(1,128)} %block.1) | copy-start | bytes 772
  18.3 4.1 %collective-permute-start.3 = (f32[3,32,128]{2,1,0:T(8,128)S(1)}, f32[3,32,128]{2,1,0:T(8,128)S(1)}, u32[]{:S(2)}, u32[]{:S(2)}) collective-permute-start(f32[3,32,128]{2,1,0:T(8,128)S(1)} %get-tuple-element.12.own_b), channel_id=1, source_target_pairs={{0,3},{1,2},{2,1},{3,0},{4,7},{5,6},{6,5},{7,4},{8,11},{9,10},{10,... | collective-permute-start | bytes 147464 | tf_op jit(solution)/shard_map/ppermute | solution.py:425

commit v2 on v0

v2 whole, which is shorter than its diff:
```python
import functools

import jax
import jax.numpy as jnp
from jax import lax
from jax.experimental import pallas as pl
from jax.experimental.pallas import tpu as pltpu
from jax.sharding import PartitionSpec as P

CX = 32
CY = 128
NZ = 8
STEPS = 2
COARSE = 4
BLOCK = 8
ZONES = 16
BUILDINGS = 1024
FP_DEV = 64
HALO = 4
RING = CX + 2 * HALO
FIELDS = 10
PACKS = 3
CHUNK = 16
COLS = PACKS * CX
CXC = CX // COARSE
CYC = CY // COARSE
F32 = jnp.float32
VMEM_LIMIT = 32 * 1024 * 1024


def iota(shape, dim):
    return lax.broadcasted_iota(jnp.int32, shape, dim)


def take(x, idx):
    idx = jnp.broadcast_to(idx, x.shape)
    return jnp.take_along_axis(x, idx, axis=1, mode="promise_in_bounds")


def roll(x, shift, axis):
    size = x.shape[axis]
    shift = shift % size
    return x if shift == 0 else pltpu.roll(x, shift, axis)


def pack_kernel(
    n_gx, n_gy, vel, stress, zones, regional, table_in, building_in, block_in, owner,
    S, V, gxa, gxb, gya, gyb, slices, source, table, building, block, Z, R, sems,
):
    gx = lax.axis_index("gx")
    gy = lax.axis_index("gy")
    even_x = (gx & 1) == 0
    even_y = (gy & 1) == 0
    inner = pl.ds(0, CX)
    loads = [pltpu.make_async_copy(stress.at[f], S.at[f, :, inner, :], sems.at[f]) for f in range(6)]
    loads += [pltpu.make_async_copy(vel.at[f], V.at[f, :, inner, :], sems.at[6 + f]) for f in range(3)]
    loads.append(pltpu.make_async_copy(zones, Z, sems.at[9]))
    loads.append(pltpu.make_async_copy(regional, R, sems.at[10]))
    loads.append(pltpu.make_async_copy(table_in, table, sems.at[11]))
    loads.append(pltpu.make_async_copy(building_in, building, sems.at[12]))
    loads.append(pltpu.make_async_copy(block_in, block, sems.at[13]))
    for copy in loads:
        copy.start()
    row = iota((CHUNK, CY), 0)
    edge = (iota((CHUNK, CY), 1) >= 96) & ((row & 7) >= 6)
    sides = jnp.where(row < CXC, owner[(gy + n_gy - 1) % n_gy], owner[(gy + 1) % n_gy])
    source[...] = jnp.where(edge, sides, owner[gy])
    slot = iota((CX, CY), 1) // HALO
    low = iota((8, CY), 0) < 4

    def plane(f, z, a, b):
        if f < 6:
            return S[f, z, a:b, :]
        if f < 9:
            return V[f - 6, z, a:b, :]
        return Z[z, a:b, :].astype(F32)

    for p in range(PACKS):
        lasts = jnp.zeros((CX, CY), F32)
        firsts = jnp.zeros((CX, CY), F32)
        for s in range(4):
            f = 4 * p + s
            if f >= FIELDS:
                continue
            loads[f].wait()
            for z in range(NZ):
                turned = roll(plane(f, z, 0, CX), 16 * z + 4 * s + 4, 1)
                at = 4 * z + s
                lasts = jnp.where(slot == at, turned, lasts)
                firsts = jnp.where(slot == (at + 1) % 32, turned, firsts)
            for q in range(NZ // 2):
                first = jnp.where(low, plane(f, 2 * q, 0, 8), roll(plane(f, 2 * q + 1, 0, 8), 4, 0))
                last = jnp.where(low, roll(plane(f, 2 * q + 1, CX - 8, CX), 4, 0), plane(f, 2 * q, CX - 8, CX))
                gxa[f * 4 + q] = jnp.where(even_x, last, first)
                gxb[f * 4 + q] = jnp.where(even_x, first, last)
        gya[p * CX:(p + 1) * CX, :] = jnp.where(even_y, lasts, firsts)
        gyb[p * CX:(p + 1) * CX, :] = jnp.where(even_y, firsts, lasts)

    loads[10].wait()
    lane = iota((n_gx, CY), 1)
    part = lane // CYC
    digit = (lane - 96) % 10
    group = (lane - 96) // 10
    for s in range(STEPS):
        halves = [[R[0, s, c, :, t * CY:(t + 1) * CY] for t in range(2)] for c in range(3)]
        nexts = [roll(halves[c][0], n_gx - 1, 0) for c in range(3)]
        befores = [roll(halves[c][1], 1, 0) for c in range(3)]
        for r in range(CXC):
            row = jnp.zeros((n_gx, CY), F32)
            for c in range(3):
                row = jnp.where(part == c, roll(halves[c][r // 4], CYC * (c - r % 4), 1), row)
            if r < 3:
                row = jnp.where(part == 3, roll(nexts[r], 96, 1), row)
            elif r < 6:
                row = jnp.where(part == 3, befores[r - 3], row)
            slices[pl.ds(s * CXC + r, n_gx, stride=CHUNK), :] = row
        ends = []
        for col in (CYC - 1, 0):
            ends.append(jnp.zeros((n_gx, CY), F32))
            idx_low = jnp.where(digit < 4, digit * CYC + col, 0)
            idx_high = jnp.where((digit >= 4) & (digit < 8), (digit - 4) * CYC + col, 0)
            for c in range(3):
                edge = jnp.where(digit < 4, take(halves[c][0], idx_low), take(halves[c][1], idx_high))
                edge = jnp.where(digit == 8, take(nexts[c], jnp.full_like(digit, col)), edge)
                edge = jnp.where(digit == 9, take(befores[c], jnp.full_like(digit, 3 * CYC + col)), edge)
                ends[-1] = jnp.where((lane >= 96) & (group == c), edge, ends[-1])
        at = COLS + s * n_gx
        gya[at:at + n_gx, :] = jnp.where(even_y, ends[0], ends[1])
        gyb[at:at + n_gx, :] = jnp.where(even_y, ends[1], ends[0])
    for copy in loads[11:]:
        copy.wait()


def relay_kernel(n_gx, ca, cb, slices, ea, eb, sent, kept):
    gx = lax.axis_index("gx")
    even_x = (gx & 1) == 0
    even_y = (lax.axis_index("gy") & 1) == 0
    low = iota((8, CY), 0) < 4

    for p in range(PACKS):
        top, end = slice(p * CX, p * CX + 8), slice((p + 1) * CX - 8, (p + 1) * CX)
        left_top, right_top = jnp.where(even_y, cb[top], ca[top]), jnp.where(even_y, ca[top], cb[top])
        left_end, right_end = jnp.where(even_y, cb[end], ca[end]), jnp.where(even_y, ca[end], cb[end])
        first = jnp.where(low, left_top, roll(right_top, 4, 0))
        last = jnp.where(low, roll(left_end, 4, 0), right_end)
        ea[p] = jnp.where(even_x, last, first)
        eb[p] = jnp.where(even_x, first, last)

    half = n_gx // 2
    bit = (gx >= half).astype(jnp.int32)
    lane = iota((CHUNK, CY), 1)
    row = iota((CHUNK, CY), 0)
    for out, side in ((sent, 1 - bit), (kept, bit)):
        for i in range(half):
            at = side * half + i
            value = slices[pl.ds(pl.multiple_of(at * CHUNK, CHUNK), CHUNK), :]
            for s in range(STEPS):
                a, b = ca[pl.ds(COLS + s * n_gx + at, 1), :], cb[pl.ds(COLS + s * n_gx + at, 1), :]
                ends = (jnp.where(even_y, b, a), jnp.where(even_y, a, b))
                for k in range(2):
                    here = (lane >= 96) & (row == k * CXC + 6 + s)
                    value = jnp.where(here, jnp.broadcast_to(ends[k], (CHUNK, CY)), value)
            out[i] = value


def spread_table(table):
    scaled = table[...] * 0.1
    spread = jnp.concatenate([scaled] * (CY // ZONES), axis=1)
    return [spread[k:k + 1, :] for k in range(3)]


def material_kernel(zones, table, LAM, MU, BUOY):
    columns = [jnp.broadcast_to(row, (CX, CY)) for row in spread_table(table)]
    for z in range(NZ):
        ids = zones[z]
        for k, ref in enumerate((LAM, MU, BUOY)):
            ref[z, 0:CX, :] = take(columns[k], ids)


XX, XZ, XY, YY, YZ, ZZ = range(6)


def dx(x):
    return roll(x, RING - 1, 0) - roll(x, 1, 0)


def dy(x, seam, z):
    lane = iota((RING, CY), 1)
    seam = roll(seam, -(16 * z + 3), 1)
    return jnp.where(lane == CY - 1, seam, roll(x, CY - 1, 1)) - jnp.where(lane == 0, seam, roll(x, 1, 1))


def dz(ref, f, z):
    if z == 0:
        return ref[f, 1]
    if z == NZ - 1:
        return -ref[f, NZ - 2]
    return ref[f, z + 1] - ref[f, z - 1]


def band_dy(x):
    return roll(x, CY - 1, 1) - roll(x, 1, 1)


def band_dz(x):
    lane = iota((RING, CY), 1)
    return jnp.where(lane < CY - 16, roll(x, CY - 16, 1), 0.0) - jnp.where(lane >= 16, roll(x, 16, 1), 0.0)


def seams(band, fields):
    lane = iota((RING, CY), 1)
    return {f: jnp.where(lane % 16 == 2, roll(band[f], -10, 1), band[f]) for f in fields}


def velocity_planes(planes, S, V, MU, BUOY, band, drm):
    seam = seams(band, (XY, YY, YZ))
    for z in planes:
        sxy, sxz, syz = S[XY, z], S[XZ, z], S[YZ, z]
        force = [
            dx(S[XX, z]) + dy(sxy, seam[XY], z) + dz(S, XZ, z),
            dx(sxy) + dy(S[YY, z], seam[YY], z) + dz(S, YZ, z),
            dx(sxz) + dy(syz, seam[YZ], z) + dz(S, ZZ, z),
        ]
        if z == NZ - 1:
            force = [force[c] + (20.0 * MU[z]) * drm(c, 0) for c in range(3)]
        for c in range(3):
            V[c, z] = V[c, z] + BUOY[z] * force[c]


def velocity_band(band, new, BM, drm):
    sxy, sxz, syz = band[XY], band[XZ], band[YZ]
    force = [
        dx(band[XX]) + band_dy(sxy) + band_dz(sxz),
        dx(sxy) + band_dy(band[YY]) + band_dz(syz),
        dx(sxz) + band_dy(syz) + band_dz(band[ZZ]),
    ]
    for c in range(3):
        if drm is not None:
            force[c] = force[c] + (20.0 * BM[1]) * drm(c, 1)
        new[6 + c] = band[6 + c] + BM[2] * force[c]


def stress_plane(z, seam, S, V, LAM, MU, fields):
    vx, vy, vz = V[0, z], V[1, z], V[2, z]
    mu = MU[z]
    if XX in fields:
        lam = LAM[z]
        xx, yy, zz = dx(vx), dy(vy, seam[7], z), dz(V, 2, z)
        theta = lam * (xx + yy + zz)
        two = mu + mu
        S[XX, z] = S[XX, z] + (theta + two * xx)
        S[YY, z] = S[YY, z] + (theta + two * yy)
        S[ZZ, z] = S[ZZ, z] + (theta + two * zz)
    if XZ in fields:
        S[XZ, z] = S[XZ, z] + mu * (dz(V, 0, z) + dx(vz))
    if XY in fields:
        S[XY, z] = S[XY, z] + mu * (dy(vx, seam[6], z) + dx(vy))
    if YZ in fields:
        S[YZ, z] = S[YZ, z] + mu * (dz(V, 1, z) + dy(vz, seam[8], z))


def stress_band(band, new, BM):
    vx, vy, vz = new[6], new[7], new[8]
    lam, mu = BM[0], BM[1]
    xx, yy, zz = dx(vx), band_dy(vy), band_dz(vz)
    theta = lam * (xx + yy + zz)
    two = mu + mu
    new[XX] = band[XX] + (theta + two * xx)
    new[YY] = band[YY] + (theta + two * yy)
    new[ZZ] = band[ZZ] + (theta + two * zz)
    new[XZ] = band[XZ] + mu * (band_dz(vx) + dx(vz))
    new[XY] = band[XY] + mu * (band_dy(vx) + dx(vy))
    new[YZ] = band[YZ] + mu * (band_dz(vy) + band_dy(vz))


ALL = (XX, XZ, XY, YY, YZ, ZZ)


def cone_kernel(
    S_in, V_in, LAM_in, MU_in, BUOY_in, table, own_a, own_b, ra, rb, ca, cb, ea, eb, building, block,
    S, V, LAM, MU, BUOY, BF, BM, shares, BW,
):
    even_x = (lax.axis_index("gx") & 1) == 0
    even_y = (lax.axis_index("gy") & 1) == 0
    low = iota((8, CY), 0) < 4
    lane8 = iota((8, CY), 1)
    sub8 = iota((8, CY), 0)
    quarter8 = (lane8 // 4) % 4
    quarter = (iota((CX, CY), 1) // 4) % 4
    tail = slice(CX, RING)
    columns = spread_table(table)
    columns8 = [jnp.broadcast_to(row, (8, CY)) for row in columns]

    own_idx = jnp.where(quarter8 == 1, lane8 % 16 - 4, jnp.where(quarter8 == 2, lane8 % 16 - 8 + CY - 4, 0))
    own_tail = []
    for f in range(FIELDS):
        own = jnp.zeros((8, CY), F32)
        for q in range(NZ // 2):
            k = f * 4 + q
            after = jnp.where(even_x, ra[k], rb[k])
            before = jnp.where(even_x, rb[k], ra[k])
            both = (jnp.where(low, after, before), roll(jnp.where(low, before, after), 4, 0))
            for z in (2 * q, 2 * q + 1):
                rows = both[z % 2]
                own = jnp.where(lane8 // 16 == z, take(rows, own_idx), own)
                if f < 6:
                    S[f, z, tail, :] = rows
                elif f < 9:
                    V[f - 6, z, tail, :] = rows
                else:
                    ids = rows.astype(jnp.int32)
                    for column, ref in zip(columns8, (LAM, MU, BUOY)):
                        ref[z, tail, :] = take(column, ids)
        own_tail.append(own)

    for p in range(PACKS):
        at = slice(p * CX, (p + 1) * CX)
        own_first = jnp.where(even_y, own_b[at], own_a[at])
        own_last = jnp.where(even_y, own_a[at], own_b[at])
        from_left = jnp.where(even_y, cb[at], ca[at])
        from_right = jnp.where(even_y, ca[at], cb[at])
        after = jnp.where(even_x, ea[p], eb[p])
        before = jnp.where(even_x, eb[p], ea[p])
        left_tail = jnp.where(low, after, roll(before, 4, 0))
        right_tail = jnp.where(low, roll(after, 4, 0), before)
        for s in range(4):
            f = 4 * p + s
            if f >= FIELDS:
                continue
            BF[f, 0:CX, :] = jnp.where(
                quarter == 0, roll(from_left, -4 * s, 1),
                jnp.where(quarter == 1, roll(own_first, -4 * s, 1),
                          jnp.where(quarter == 2, roll(own_last, 8 - 4 * s, 1), roll(from_right, 8 - 4 * s, 1))),
            )
            BF[f, tail, :] = jnp.where(
                quarter8 == 0, roll(left_tail, -4 * s, 1),
                jnp.where(quarter8 == 3, roll(right_tail, 8 - 4 * s, 1), own_tail[f]),
            )
    ids = BF[9].astype(jnp.int32)
    for k in range(3):
        BM[k] = take(jnp.broadcast_to(columns[k], (RING, CY)), ids)

    velocity_planes(range(0, 5), S, V, MU, BUOY, BF, None)
    velocity_band(BF, BW, BM, None)
    seam = seams(BW, (6, 7, 8))
    for z in range(0, 4):
        stress_plane(z, seam, S, V, LAM, MU, ALL)
    stress_band(BF, BW, BM)
    velocity_planes(range(0, 3), S, V, MU, BUOY, BW, None)
    velocity_band(BW, BW, BM, None)
    stress_plane(1, seams(BW, (8,)), S, V, LAM, MU, (XZ, YZ))

    total = jnp.zeros((8, CY), F32)
    for c, f in enumerate((XZ, YZ)):
        for r in range(CX // BLOCK):
            row = jnp.sum(S[f, 1, 8 * r:8 * r + 8, :], axis=0, keepdims=True)
            total = jnp.where(sub8 == 4 * c + r, jnp.broadcast_to(row, (8, CY)), total)
    for shift in (1, 2, 4):
        total = total + roll(total, CY - shift, 1)
    total = total * (1.0 / (BLOCK * BLOCK))
    ids = jnp.broadcast_to(jnp.concatenate([block[0], block[0]], axis=1), (8, CY))
    cells = CY // BLOCK
    picked = take(total, (ids % cells) * BLOCK)
    mine = (sub8 % 4 == ids // cells) & (sub8 // 4 == lane8 // FP_DEV)
    values = jnp.sum(jnp.where(mine, picked, 0.0), axis=0, keepdims=True)
    names = jnp.concatenate([building[0], building[0]], axis=1).astype(F32)
    message = jnp.concatenate([values, names], axis=0)
    shares[...] = jnp.broadcast_to(message[None], shares.shape)


def rest_kernel(
    S_in, V_in, LAM, MU, BUOY, BF_in, BM, drm_in,
    S, V, BF, vel_out, stress_out, DRM, sems,
):
    low = iota((8, CY), 0) < 4
    lane8 = iota((8, CY), 1)
    quarter8 = (lane8 // 4) % 4
    deepest = lane8 >= 16 * (NZ - 1)

    def wide(row):
        return jnp.broadcast_to(drm_in[row:row + 1, :], (8, CY))

    for s in range(STEPS):
        left_edge, right_edge = wide(6 + s), wide(CXC + 6 + s)
        for c in range(3):
            for q in range(RING // 8):
                if q < 4:
                    rows = jnp.where(low, wide(s * CXC + 2 * q), wide(s * CXC + 2 * q + 1))
                    base = c * CYC
                else:
                    rows = jnp.where(low, wide(s * CXC + c), wide(s * CXC + 3 + c))
                    base = 3 * CYC
                DRM[s, c, 0, 8 * q:8 * q + 8, :] = take(rows, base + lane8 // COARSE)
                inner = take(rows, base + jnp.where(quarter8 == 2, CYC - 1, 0))
                at = 96 + c * 10 + 2 * q
                edge_idx = jnp.where(low, at, at + 1)
                value = jnp.where(
                    quarter8 == 0, take(left_edge, edge_idx),
                    jnp.where(quarter8 == 3, take(right_edge, edge_idx), inner),
                )
                DRM[s, c, 1, 8 * q:8 * q + 8, :] = jnp.where(deepest, value, 0.0)

    def drm(step):
        return lambda c, k: DRM[step, c, k]

    saves = []
    velocity_planes(range(5, NZ), S, V, MU, BUOY, BF, drm(0))
    velocity_band(BF, BF, BM, drm(0))
    seam = seams(BF, (6, 7, 8))
    for z in range(4, NZ):
        stress_plane(z, seam, S, V, LAM, MU, ALL)
    stress_band(BF, BF, BM)
    velocity_planes(range(3, NZ), S, V, MU, BUOY, BF, drm(1))
    velocity_band(BF, BF, BM, drm(1))
    inner = pl.ds(0, CX)
    saves.append(pltpu.make_async_copy(V.at[:, :, inner, :], vel_out, sems.at[NZ]))
    saves[-1].start()
    seam = seams(BF, (6, 7, 8))
    for z in range(NZ):
        stress_plane(z, seam, S, V, LAM, MU, (XX, XY) if z == 1 else ALL)
        saves.append(pltpu.make_async_copy(S.at[:, z, inner, :], stress_out.at[:, z], sems.at[z]))
        saves[-1].start()
    for save in saves:
        save.wait()


def sum_kernel(n, shares, out):
    half = n // 2
    low = iota((half, CY), 1) < FP_DEV
    values = shares[:, 0, :]
    names = shares[:, 1, :].astype(jnp.int32)
    entry = [
        jnp.where(low, values[:half], roll(values[half:], FP_DEV, 1)),
        jnp.where(low, roll(values[:half], FP_DEV, 1), values[half:]),
    ]
    names = jnp.where(low, names[:half], names[half:])
    high = names // CY
    names = names % CY
    n_high = BUILDINGS // CY
    rows = iota((n_high, CY), 0)
    wanted = iota((CY, CY), 0)
    acc = jnp.zeros((6 * n_high, CY), F32)
    for k in range(half):
        hot = (jnp.broadcast_to(names[k:k + 1], (CY, CY)) == wanted).astype(F32).astype(jnp.bfloat16)
        here = jnp.broadcast_to(high[k:k + 1], (n_high, CY)) == rows
        left = []
        for c in range(2):
            rest = jnp.where(here, jnp.broadcast_to(entry[c][k:k + 1], (n_high, CY)), 0.0)
            for _ in range(3):
                piece = rest.astype(jnp.bfloat16)
                rest = rest - piece.astype(F32)
                left.append(piece.astype(F32))
        left = jnp.concatenate(left, axis=0).astype(jnp.bfloat16)
        acc = acc + lax.dot_general(left, hot, (((1,), (1,)), ((), ())), preferred_element_type=F32)
    sums = []
    for c in range(2):
        base = 3 * c * n_high
        sums.append(acc[base:base + n_high] + acc[base + n_high:base + 2 * n_high] + acc[base + 2 * n_high:base + 3 * n_high])
    for h in range(n_high):
        out[:, h * CY:(h + 1) * CY] = jnp.concatenate([sums[0][h:h + 1], sums[1][h:h + 1]], axis=0)


def pairs_near(n):
    return [(i, i ^ 1) for i in range(n)]


def pairs_far(n):
    return [(i, (i + 1) % n if i % 2 else (i - 1) % n) for i in range(n)]


def body(n_gx, n_gy, velocity, stress, zones, zone_table, regional, owner, building, block):
    n = n_gx * n_gy
    gx = lax.axis_index("gx")
    vmem = pl.BlockSpec(memory_space=pltpu.VMEM)
    hbm = pl.BlockSpec(memory_space=pltpu.HBM)
    params = pltpu.CompilerParams(vmem_limit_bytes=VMEM_LIMIT)

    def shaped(*shape):
        return jax.ShapeDtypeStruct(shape, F32)

    def whole(shape, dtype):
        return jax.ShapeDtypeStruct(shape, dtype)

    s_ring = shaped(6, NZ, RING, CY)
    v_ring = shaped(3, NZ, RING, CY)
    m_ring = shaped(NZ, RING, CY)
    rows = shaped(FIELDS * 4, 8, CY)
    cols = shaped(COLS + STEPS * n_gx, CY)
    from_hbm = [
        pltpu.with_memory_space_constraint(x, pltpu.HBM)
        for x in (velocity, stress, zones, regional, zone_table, building, block)
    ]
    S, V, gxa, gxb, gya, gyb, slices, source, zone_table, building, block = pl.pallas_call(
        functools.partial(pack_kernel, n_gx, n_gy),
        out_shape=(
            s_ring, v_ring, rows, rows, cols, cols, shaped(n_gx * CHUNK, CY), whole((CHUNK, CY), jnp.int32),
            whole(zone_table.shape, F32), whole(building.shape, jnp.int32), whole(block.shape, jnp.int32),
        ),
        in_specs=[hbm] * 7 + [pl.BlockSpec(memory_space=pltpu.SMEM)],
        out_specs=(vmem,) * 11,
        scratch_shapes=[
            pltpu.VMEM(zones.shape, jnp.int32),
            pltpu.VMEM(regional.shape, F32),
            pltpu.SemaphoreType.DMA((14,)),
        ],
        compiler_params=params,
        name="pack",
    )(*from_hbm, owner)
    near_x, far_x = pairs_near(n_gx), pairs_far(n_gx)
    ca = lax.ppermute(gya, "gy", pairs_near(n_gy))
    cb = lax.ppermute(gyb, "gy", pairs_far(n_gy))
    rb = lax.ppermute(gxb, "gx", far_x)
    ra = lax.ppermute(gxa, "gx", near_x)
    half = n_gx // 2
    corner = shaped(PACKS, 8, CY)
    part = shaped(half, CHUNK, CY)
    msg_a, msg_b, sent, kept = pl.pallas_call(
        functools.partial(relay_kernel, n_gx),
        out_shape=(corner, corner, part, part),
        in_specs=[vmem] * 3,
        out_specs=(vmem,) * 4,
        compiler_params=params,
        name="relay",
    )(ca, cb, slices)
    eb = lax.ppermute(msg_b, "gx", far_x)
    ea = lax.ppermute(msg_a, "gx", near_x)

    def trade(sent, kept, width):
        got = lax.ppermute(sent, "gx", [(i, i ^ width) for i in range(n_gx)])
        held = jnp.where(((source ^ gx) & width) == 0, kept, got)
        if width == 1:
            return held, None
        width //= 2
        halves = held.reshape(2, width, CHUNK, CY)
        upper = (gx & width) != 0
        return jnp.where(upper, halves[0], halves[1]), jnp.where(upper, halves[1], halves[0])

    sent, kept = trade(sent, kept, half)
    LAM, MU, BUOY = pl.pallas_call(
        material_kernel,
        out_shape=(m_ring,) * 3,
        in_specs=[vmem] * 2,
        out_specs=(vmem,) * 3,
        compiler_params=params,
        name="materials",
    )(zones, zone_table)
    S, V, LAM, MU, BUOY, BF, BM, shares = pl.pallas_call(
        cone_kernel,
        out_shape=(s_ring, v_ring, m_ring, m_ring, m_ring, shaped(FIELDS, RING, CY), shaped(3, RING, CY), shaped(n, 2, CY)),
        in_specs=[vmem] * 16,
        out_specs=(vmem,) * 8,
        scratch_shapes=[pltpu.VMEM((9, RING, CY), F32)],
        input_output_aliases={k: k for k in range(5)},
        compiler_params=params,
        name="cone",
    )(S, V, LAM, MU, BUOY, zone_table, gya, gyb, ra, rb, ca, cb, ea, eb, building, block)
    sent, BM = lax.optimization_barrier((sent, BM))
    width = half // 2
    while width > 1:
        sent, kept = trade(sent, kept, width)
        width //= 2
    drm = trade(sent, kept, 1)[0].reshape(CHUNK, CY)
    every = lax.all_to_all(shares, ("gx", "gy"), 0, 0)
    _, _, _, vel_out, stress_out = pl.pallas_call(
        rest_kernel,
        out_shape=(s_ring, v_ring, shaped(FIELDS, RING, CY), shaped(*velocity.shape), shaped(*stress.shape)),
        in_specs=[vmem] * 8,
        out_specs=(vmem, vmem, vmem, hbm, hbm),
        scratch_shapes=[
            pltpu.VMEM((STEPS, 3, 2, RING, CY), F32),
            pltpu.SemaphoreType.DMA((NZ + 1,)),
        ],
        input_output_aliases={0: 0, 1: 1, 5: 2},
        compiler_params=params,
        name="rest",
    )(S, V, LAM, MU, BUOY, BF, BM, drm)
    shear = pl.pallas_call(
        functools.partial(sum_kernel, n),
        out_shape=shaped(2, BUILDINGS),
        in_specs=[vmem],
        out_specs=vmem,
        compiler_params=params,
        name="sum_by_building",
    )(every)
    return vel_out, stress_out, shear


def solution(mesh):
    n_gx, n_gy = mesh.shape["gx"], mesh.shape["gy"]
    return jax.shard_map(
        functools.partial(body, n_gx, n_gy),
        mesh=mesh,
        in_specs=(
            P(None, None, "gx", "gy"),
            P(None, None, "gx", "gy"),
            P(None, "gx", "gy"),
            P(),
            P("gx", None, None, None, "gy"),
            P(),
            P("gx", "gy", None),
            P("gx", "gy", None),
        ),
        out_specs=(P(None, None, "gx", "gy"), P(None, None, "gx", "gy"), P()),
        check_vma=False,
    )
```

time: 197 us -> 38.7 us (0.20)
  blocking collectives: 72.4 us -> 0 us
  other arithmetic: 39 us -> 0.04 us
  waiting for transfers between devices: 35.2 us -> 13.8 us
  local copies, waits for them, and re-layouts: 20.9 us -> 0.65 us
  starting transfers between devices: 24.9 us -> 13.9 us
  Pallas kernels: 0 us -> 9.37 us
    psum x2 -> x0, blocking collectives: 72.4 us -> none  [the longest x1 37.2 us: body(): shear = lax.psum(partial_shear, ('gx', 'gy'))]
    ppermute x16 -> x9, waiting for transfers between devices: 35.2 us -> 10.3 us  [the longest x3 6.67 us: trade(): got = lax.ppermute(sent, 'gx', [(i, i ^ width) for i in range(n_gx)])]
    mul x6 -> x0, other arithmetic: 14 us -> none  [the longest x1 10.6 us: body(): velocity = velocity + 0.2 * buoy[None] * force]
    ppermute x16 -> x9, starting transfers between devices: 24.9 us -> 11.3 us  [the longest x1 3.57 us: body(): rb = lax.ppermute(gxb, 'gx', far_x)]
    unnamed x10 -> x0, other arithmetic: 12.5 us -> none
    add x3 -> x0, other arithmetic: 10.3 us -> none  [the longest x1 10.2 us: lookup(): total = total + jnp.where(zones == zone, column[zone], 0.0)]
    pallas_call x0 -> x6, Pallas kernels: none -> 9.37 us  [the longest x1 2.84 us: body(): pl.pallas_call(functools.partial(pack_kernel, n_gx, n_gy), out_shape=(s_r...]
    slice x20 -> x0, local copies, waits for them, and re-layouts: 7.41 us -> none  [the longest x4 2.57 us: with_halo(): last = lax.slice_in_dim(value, length - width, length, axis=dim)]
  transfers between devices with their start and end apart: 16 -> 10, of which waited for: 10 -> 5; matrix products, arithmetic and copies ran while one was open for 15% -> 0% of each run, Pallas kernels for 0% -> 8%
where the time goes in v2:
time: 38.7 us; the launch traced here: 38.5 us
  starting transfers between devices  13.9 us (36%)
  waiting for transfers between devices  13.8 us (36%)
  Pallas kernels  9.37 us (24%)
  between operations  0.73 us (2%)
  local copies, waits for them, and re-layouts  0.65 us (2%)
    ppermute x3, waiting for transfers between devices, trade(): got = lax.ppermute(sent, 'gx', [(i, i ^ width) for i in range(n_gx)])  6.67 us
    ppermute x1, waiting for transfers between devices, body(): eb = lax.ppermute(msg_b, 'gx', far_x)  3.62 us
    ppermute x1, starting transfers between devices, body(): rb = lax.ppermute(gxb, 'gx', far_x)  3.57 us
    all_to_all x1, waiting for transfers between devices, body(): every = lax.all_to_all(shares, ('gx', 'gy'), 0, 0)  3.53 us
    pallas_call x1, Pallas kernels, body(): pl.pallas_call(functools.partial(pack_kernel, n_gx, n_gy), out_shape=(s_r...  2.84 us
    pallas_call x1, Pallas kernels, body(): pl.pallas_call(rest_kernel, out_shape=(s_ring, v_ring, shaped(FIELDS, RIN...  2.66 us
    ppermute x1, starting transfers between devices, body(): cb = lax.ppermute(gyb, 'gy', pairs_far(n_gy))  2.64 us
    all_to_all x1, starting transfers between devices, body(): every = lax.all_to_all(shares, ('gx', 'gy'), 0, 0)  2.58 us
  transfers between devices with their start and end apart: 10, of which 5 were waited for; matrix products, arithmetic and copies ran while one was open for 0% of the time, Pallas kernels for 8%

profile of v2, /device:TPU:0, one launch (start us, length us, event | category | flops | bytes accessed | tf_op | source)
XLA Modules:
  0.0 38.5 jit_solution(14600169428347420731)
XLA Ops:
  0.6 0.0 copy-start.1
  0.6 0.6 %copy-done.1 = s32[4]{0:T(128)S(1)} copy-done((s32[4]{0:T(128)S(1)}, s32[4]{0:T(128)}, u32[]{:S(2)}) %copy-start.1) | copy-done | bytes 40
  1.3 2.8 %pack.1 = (f32[6,8,40,128]{3,2,1,0:T(8,128)S(1)}, f32[3,8,40,128]{3,2,1,0:T(8,128)S(1)}, f32[40,8,128]{2,1,0:T(8,128)S(1)}, f32[40,8,128]{2,1,0:T(8,128)S(1)}, f...) custom-call(f32[3,8,32,128]{3,2,1,0:T(8,128)} %vel.1, ...), custom_call_target="tpu_custom_call" | custom-call | tf_op jit(solution)/shard_map/pack/pallas_call | solution.py:493
  4.1 0.0 copy-start
  4.1 0.5 %collective-permute-start.2 = (f32[112,128]{1,0:T(8,128)S(1)}, f32[112,128]{1,0:T(8,128)S(1)}, u32[]{:S(2)}, u32[]{:S(2)}) collective-permute-start(f32[112,128]{1,0:T(8,128)S(1)} %get-tuple-element.39.own_a), channel_id=1, source_target_pairs={{0,1},{1,0},{2,3},{3,2},{4,5},{5,4},{6,7},{7,6},{8,9},{9,8},{10,11... | collective-permute-start | bytes 172040 | tf_op jit(solution)/shard_map/ppermute | solution.py:510
  4.7 2.6 %collective-permute-start.3 = (f32[112,128]{1,0:T(8,128)S(1)}, f32[112,128]{1,0:T(8,128)S(1)}, u32[]{:S(2)}, u32[]{:S(2)}) collective-permute-start(f32[112,128]{1,0:T(8,128)S(1)} %get-tuple-element.40.own_b), channel_id=1, source_target_pairs={{0,3},{1,2},{2,1},{3,0},{4,7},{5,6},{6,5},{7,4},{8,11},{9,10},{10,... | collective-permute-start | bytes 172040 | tf_op jit(solution)/shard_map/ppermute | solution.py:511
  7.3 1.5 %collective-permute-start = (f32[40,8,128]{2,1,0:T(8,128)S(1)}, f32[40,8,128]{2,1,0:T(8,128)S(1)}, u32[]{:S(2)}, u32[]{:S(2)}) collective-permute-start(f32[40,8,128]{2,1,0:T(8,128)S(1)} %get-tuple-element.41), channel_id=1, source_target_pairs={{0,4},{4,0},{8,12},{12,8},{16,20},{20,16},{24,28},{28,24},{1,5},{5... | collective-permute-start | bytes 491528 | tf_op jit(solution)/shard_map/ppermute | solution.py:513
  8.8 3.6 %collective-permute-start.1 = (f32[40,8,128]{2,1,0:T(8,128)S(1)}, f32[40,8,128]{2,1,0:T(8,128)S(1)}, u32[]{:S(2)}, u32[]{:S(2)}) collective-permute-start(f32[40,8,128]{2,1,0:T(8,128)S(1)} %get-tuple-element.42), channel_id=1, source_target_pairs={{0,28},{4,8},{8,4},{12,16},{16,12},{20,24},{24,20},{28,0},{1,29},{... | collective-permute-start | bytes 491528 | tf_op jit(solution)/shard_map/ppermute | solution.py:512
  12.4 0.0 collective-permute-done.2.ca
  12.4 0.0 collective-permute-done.3.cb
  12.4 0.1 collective-permute-start.6
  12.5 0.0 copy-done
  12.5 0.4 %materials.1 = (f32[8,40,128]{2,1,0:T(8,128)S(1)}, f32[8,40,128]{2,1,0:T(8,128)S(1)}, f32[8,40,128]{2,1,0:T(8,128)S(1)}) custom-call(s32[8,32,128]{2,1,0:T(8,128)S(1)} %copy-done, f32[3,16]{1,0:T(4,128)S(1)} %get-tuple-element.35.table), custom_call_target="tpu_custom_call" | custom-call | tf_op jit(solution)/shard_map/materials/pallas_call | solution.py:539
  12.9 2.1 %collective-permute-start.4 = (f32[3,8,128]{2,1,0:T(8,128)S(1)}, f32[3,8,128]{2,1,0:T(8,128)S(1)}, u32[]{:S(2)}, u32[]{:S(2)}) collective-permute-start(f32[3,8,128]{2,1,0:T(8,128)S(1)} %get-tuple-element.44), channel_id=1, source_target_pairs={{0,4},{4,0},{8,12},{12,8},{16,20},{20,16},{24,28},{28,24},{1,5},{5... | collective-permute-start | bytes 36872 | tf_op jit(solution)/shard_map/ppermute | solution.py:526
  15.0 0.9 %collective-permute-start.5 = (f32[3,8,128]{2,1,0:T(8,128)S(1)}, f32[3,8,128]{2,1,0:T(8,128)S(1)}, u32[]{:S(2)}, u32[]{:S(2)}) collective-permute-start(f32[3,8,128]{2,1,0:T(8,128)S(1)} %get-tuple-element.45), channel_id=1, source_target_pairs={{0,28},{4,8},{8,4},{12,16},{16,12},{20,24},{24,20},{28,0},{1,29},{... | collective-permute-start | bytes 36872 | tf_op jit(solution)/shard_map/ppermute | solution.py:525
  15.9 1.9 %collective-permute-done.6 = f32[4,16,128]{2,1,0:T(8,128)S(1)} collective-permute-done((f32[4,16,128]{2,1,0:T(8,128)S(1)}, f32[4,16,128]{2,1,0:T(8,128)S(1)}, u32[]{:S(2)}, u32[]{:S(2)}) %collective-permute-start.6) | collective-permute-done | bytes 32800 | tf_op jit(solution)/shard_map/ppermute | solution.py:529
  17.8 0.0 collective-permute-done.4.ea
  17.8 3.6 %collective-permute-done.5.eb = f32[3,8,128]{2,1,0:T(8,128)S(1)} collective-permute-done((f32[3,8,128]{2,1,0:T(8,128)S(1)}, f32[3,8,128]{2,1,0:T(8,128)S(1)}, u32[]{:S(2)}, u32[]{:S(2)}) %collective-permute-start.5) | collective-permute-done | bytes 12320 | tf_op jit(solution)/shard_map/ppermute | solution.py:525
  21.4 0.0 collective-permute-done.ra
  21.4 0.0 collective-permute-done.1.rb
  21.4 2.4 %cone.1 = (f32[6,8,40,128]{3,2,1,0:T(8,128)S(1)}, f32[3,8,40,128]{3,2,1,0:T(8,128)S(1)}, f32[8,40,128]{2,1,0:T(8,128)S(1)}, f32[8,40,128]{2,1,0:T(8,128)S(1)}, f...) custom-call(f32[6,8,40,128]{3,2,1,0:T(8,128)S(1)} %get-tuple-element, ...), custom_call_target="tpu_custom_call", output_to_operand_aliasing={{0}: (0, {}), {1}: (1, {}), {2}: (2, {}), {3}: (3, {}), {4}... | custom-call | tf_op jit(solution)/shard_map/cone/pallas_call | solution.py:547
  23.8 0.0 collective-permute-start.7
  23.8 3.7 %collective-permute-done.7 = f32[2,16,128]{2,1,0:T(8,128)S(1)} collective-permute-done((f32[2,16,128]{2,1,0:T(8,128)S(1)}, f32[2,16,128]{2,1,0:T(8,128)S(1)}, u32[]{:S(2)}, u32[]{:S(2)}) %collective-permute-start.7) | collective-permute-done | bytes 16416 | tf_op jit(solution)/shard_map/ppermute | solution.py:529
  27.5 0.1 collective-permute-start.8
  27.6 2.6 %all-to-all-start = ((f32[32,2,128]{2,1,0:T(2,128)}), f32[32,2,128]{2,1,0:T(2,128)S(1)}, u32[]{:S(2)}, u32[]{:S(2)}) async-start(f32[32,2,128]{2,1,0:T(2,128)} %get-tuple-element.62), calls=%async_computation | async-start | bytes 65536 | tf_op jit(solution)/shard_map/all_to_all | solution.py:563
  30.2 1.0 %collective-permute-done.8 = f32[1,16,128]{2,1,0:T(8,128)S(1)} collective-permute-done((f32[1,16,128]{2,1,0:T(8,128)S(1)}, f32[1,16,128]{2,1,0:T(8,128)S(1)}, u32[]{:S(2)}, u32[]{:S(2)}) %collective-permute-start.8) | collective-permute-done | bytes 8224 | tf_op jit(solution)/shard_map/ppermute | solution.py:529
  31.2 2.7 %rest.1 = (f32[6,8,40,128]{3,2,1,0:T(8,128)S(1)}, f32[3,8,40,128]{3,2,1,0:T(8,128)S(1)}, f32[10,40,128]{2,1,0:T(8,128)S(1)}, f32[3,8,32,128]{3,2,1,0:T(8,128)}, f32[6,8,32,128]{3,2,1,0:T(8,128)}) custom-call(f32[6,8,40,128]{3,2,1,0:T(8,128)S(1)} %get-tuple-element.48.S_in, ...), custom_call_target="tpu_custom_call", output_to_operand_aliasing={{0}: (0, {}), {1}: (1, {}), {2}: (5, {})} | custom-call | tf_op jit(solution)/shard_map/rest/pallas_call | solution.py:564
  33.9 3.5 %all-to-all-done.shares = f32[32,2,128]{2,1,0:T(2,128)S(1)} async-done(((f32[32,2,128]{2,1,0:T(2,128)}), f32[32,2,128]{2,1,0:T(2,128)S(1)}, u32[]{:S(2)}, u32[]{:S(2)}) %all-to-all-start) | async-done | bytes 32800 | tf_op jit(solution)/shard_map/all_to_all | solution.py:563
  37.4 1.1 %sum_by_building.1 = f32[2,1024]{1,0:T(2,128)} custom-call(f32[32,2,128]{2,1,0:T(2,128)S(1)} %all-to-all-done.shares), custom_call_target="tpu_custom_call" | custom-call | tf_op jit(solution)/shard_map/sum_by_building/pallas_call | solution.py:577
  (7 shorter events, 0.1 us)
Async XLA Ops:
  0.6 0.7 %copy-start.1 = (s32[4]{0:T(128)S(1)}, s32[4]{0:T(128)}, u32[]{:S(2)}) copy-start(s32[4]{0:T(128)} %owner.1) | copy-start | bytes 52
  4.1 8.4 %copy-start = (s32[8,32,128]{2,1,0:T(8,128)S(1)}, s32[8,32,128]{2,1,0:T(8,128)}, u32[]{:S(2)}) copy-start(s32[8,32,128]{2,1,0:T(8,128)} %zones.3) | copy-start | bytes 393220
  4.1 8.2 %collective-permute-start.2 = (f32[112,128]{1,0:T(8,128)S(1)}, f32[112,128]{1,0:T(8,128)S(1)}, u32[]{:S(2)}, u32[]{:S(2)}) collective-permute-start(f32[112,128]{1,0:T(8,128)S(1)} %get-tuple-element.39.own_a), channel_id=1, source_target_pairs={{0,1},{1,0},{2,3},{3,2},{4,5},{5,4},{6,7},{7,6},{8,9},{9,8},{10,11... | collective-permute-start | bytes 172040 | tf_op jit(solution)/shard_map/ppermute | solution.py:510
  4.7 7.7 %collective-permute-start.3 = (f32[112,128]{1,0:T(8,128)S(1)}, f32[112,128]{1,0:T(8,128)S(1)}, u32[]{:S(2)}, u32[]{:S(2)}) collective-permute-start(f32[112,128]{1,0:T(8,128)S(1)} %get-tuple-element.40.own_b), channel_id=1, source_target_pairs={{0,3},{1,2},{2,1},{3,0},{4,7},{5,6},{6,5},{7,4},{8,11},{9,10},{10,... | collective-permute-start | bytes 172040 | tf_op jit(solution)/shard_map/ppermute | solution.py:511
  7.3 14.1 %collective-permute-start = (f32[40,8,128]{2,1,0:T(8,128)S(1)}, f32[40,8,128]{2,1,0:T(8,128)S(1)}, u32[]{:S(2)}, u32[]{:S(2)}) collective-permute-start(f32[40,8,128]{2,1,0:T(8,128)S(1)} %get-tuple-element.41), channel_id=1, source_target_pairs={{0,4},{4,0},{8,12},{12,8},{16,20},{20,16},{24,28},{28,24},{1,5},{5... | collective-permute-start | bytes 491528 | tf_op jit(solution)/shard_map/ppermute | solution.py:513
  8.8 12.6 %collective-permute-start.1 = (f32[40,8,128]{2,1,0:T(8,128)S(1)}, f32[40,8,128]{2,1,0:T(8,128)S(1)}, u32[]{:S(2)}, u32[]{:S(2)}) collective-permute-start(f32[40,8,128]{2,1,0:T(8,128)S(1)} %get-tuple-element.42), channel_id=1, source_target_pairs={{0,28},{4,8},{8,4},{12,16},{16,12},{20,24},{24,20},{28,0},{1,29},{... | collective-permute-start | bytes 491528 | tf_op jit(solution)/shard_map/ppermute | solution.py:512
  12.4 5.3 %collective-permute-start.6 = (f32[4,16,128]{2,1,0:T(8,128)S(1)}, f32[4,16,128]{2,1,0:T(8,128)S(1)}, u32[]{:S(2)}, u32[]{:S(2)}) collective-permute-start(f32[4,16,128]{2,1,0:T(8,128)S(1)} %get-tuple-element.56), channel_id=1, source_target_pairs={{0,16},{4,20},{8,24},{12,28},{16,0},{20,4},{24,8},{28,12},{1,17},{... | collective-permute-start | bytes 98312 | tf_op jit(solution)/shard_map/ppermute | solution.py:529
  12.9 4.9 %collective-permute-start.4 = (f32[3,8,128]{2,1,0:T(8,128)S(1)}, f32[3,8,128]{2,1,0:T(8,128)S(1)}, u32[]{:S(2)}, u32[]{:S(2)}) collective-permute-start(f32[3,8,128]{2,1,0:T(8,128)S(1)} %get-tuple-element.44), channel_id=1, source_target_pairs={{0,4},{4,0},{8,12},{12,8},{16,20},{20,16},{24,28},{28,24},{1,5},{5... | collective-permute-start | bytes 36872 | tf_op jit(solution)/shard_map/ppermute | solution.py:526
  15.0 6.4 %collective-permute-start.5 = (f32[3,8,128]{2,1,0:T(8,128)S(1)}, f32[3,8,128]{2,1,0:T(8,128)S(1)}, u32[]{:S(2)}, u32[]{:S(2)}) collective-permute-start(f32[3,8,128]{2,1,0:T(8,128)S(1)} %get-tuple-element.45), channel_id=1, source_target_pairs={{0,28},{4,8},{8,4},{12,16},{16,12},{20,24},{24,20},{28,0},{1,29},{... | collective-permute-start | bytes 36872 | tf_op jit(solution)/shard_map/ppermute | solution.py:525
  23.8 3.7 %collective-permute-start.7 = (f32[2,16,128]{2,1,0:T(8,128)S(1)}, f32[2,16,128]{2,1,0:T(8,128)S(1)}, u32[]{:S(2)}, u32[]{:S(2)}) collective-permute-start(f32[2,16,128]{2,1,0:T(8,128)S(1)} %slice_select_fusion), channel_id=1, source_target_pairs={{0,8},{4,12},{8,0},{12,4},{16,24},{20,28},{24,16},{28,20},{1,9},{5... | collective-permute-start | bytes 49160 | tf_op jit(solution)/shard_map/ppermute | solution.py:529
  27.5 3.7 %collective-permute-start.8 = (f32[1,16,128]{2,1,0:T(8,128)S(1)}, f32[1,16,128]{2,1,0:T(8,128)S(1)}, u32[]{:S(2)}, u32[]{:S(2)}) collective-permute-start(f32[1,16,128]{2,1,0:T(8,128)S(1)} %slice_select_fusion.1), channel_id=1, source_target_pairs={{0,4},{4,0},{8,12},{12,8},{16,20},{20,16},{24,28},{28,24},{1,5},{5... | collective-permute-start | bytes 24584 | tf_op jit(solution)/shard_map/ppermute | solution.py:529
  27.6 9.8 %all-to-all-start = ((f32[32,2,128]{2,1,0:T(2,128)}), f32[32,2,128]{2,1,0:T(2,128)S(1)}, u32[]{:S(2)}, u32[]{:S(2)}) async-start(f32[32,2,128]{2,1,0:T(2,128)} %get-tuple-element.62), calls=%async_computation | async-start | bytes 65536 | tf_op jit(solution)/shard_map/all_to_all | solution.py:563

commit v3 on v2

v3 whole, which is shorter than its diff:
```python
import functools

import jax
import jax.numpy as jnp
from jax import lax
from jax.experimental import pallas as pl
from jax.experimental.pallas import tpu as pltpu
from jax.sharding import PartitionSpec as P

CX = 32
CY = 128
NZ = 8
STEPS = 2
COARSE = 4
BLOCK = 8
ZONES = 16
BUILDINGS = 1024
FP_DEV = 64
HALO = 4
RING = CX + 2 * HALO
FIELDS = 10
PACKS = 3
CHUNK = 16
COLS = PACKS * CX
CXC = CX // COARSE
CYC = CY // COARSE
F32 = jnp.float32
VMEM_LIMIT = 32 * 1024 * 1024


def iota(shape, dim):
    return lax.broadcasted_iota(jnp.int32, shape, dim)


def take(x, idx):
    idx = jnp.broadcast_to(idx, x.shape)
    return jnp.take_along_axis(x, idx, axis=1, mode="promise_in_bounds")


def roll(x, shift, axis):
    size = x.shape[axis]
    shift = shift % size
    return x if shift == 0 else pltpu.roll(x, shift, axis)


def rows_kernel(
    vel, stress, zones, regional_in, table_in, building_in, block_in,
    gxa, gxb, regional, table, building, block, F, Z, sems,
):
    even_x = (lax.axis_index("gx") & 1) == 0
    low = iota((8, CY), 0) < 4
    loads = []
    for end, at in enumerate((0, CX - 8)):
        rows = pl.ds(at, 8)
        loads.append(pltpu.make_async_copy(stress.at[:, :, rows, :], F.at[end, pl.ds(0, 6)], sems.at[3 * end]))
        loads.append(pltpu.make_async_copy(vel.at[:, :, rows, :], F.at[end, pl.ds(6, 3)], sems.at[3 * end + 1]))
        loads.append(pltpu.make_async_copy(zones.at[:, rows, :], Z.at[end], sems.at[3 * end + 2]))
    small = ((regional_in, regional), (table_in, table), (building_in, building), (block_in, block))
    loads += [pltpu.make_async_copy(src, dst, sems.at[6 + k]) for k, (src, dst) in enumerate(small)]
    for copy in loads:
        copy.start()
    for copy in loads:
        copy.wait()

    for f in range(FIELDS):
        for q in range(NZ // 2):
            tiles = [F[end, f, z] if f < 9 else Z[end, z].astype(F32) for end in range(2) for z in (2 * q, 2 * q + 1)]
            first = jnp.where(low, tiles[0], roll(tiles[1], 4, 0))
            last = jnp.where(low, roll(tiles[3], 4, 0), tiles[2])
            gxa[f * 4 + q] = jnp.where(even_x, last, first)
            gxb[f * 4 + q] = jnp.where(even_x, first, last)


def cols_kernel(vel, stress, zones, S, V, gya, gyb, sems):
    even_y = (lax.axis_index("gy") & 1) == 0
    inner = pl.ds(0, CX)
    loads = [
        pltpu.make_async_copy(stress, S.at[:, :, inner, :], sems.at[0]),
        pltpu.make_async_copy(vel, V.at[:, :, inner, :], sems.at[1]),
    ]
    for copy in loads:
        copy.start()
    slot = iota((CX, CY), 1) // HALO

    def plane(f, z):
        if f < 6:
            return stress[f, z]
        if f < 9:
            return vel[f - 6, z]
        return zones[z].astype(F32)

    for p in range(PACKS):
        lasts = jnp.zeros((CX, CY), F32)
        firsts = jnp.zeros((CX, CY), F32)
        for s in range(4):
            f = 4 * p + s
            if f >= FIELDS:
                continue
            for z in range(NZ):
                turned = roll(plane(f, z), 16 * z + 4 * s + 4, 1)
                at = 4 * z + s
                lasts = jnp.where(slot == at, turned, lasts)
                firsts = jnp.where(slot == (at + 1) % 32, turned, firsts)
        gya[p * CX:(p + 1) * CX, :] = jnp.where(even_y, lasts, firsts)
        gyb[p * CX:(p + 1) * CX, :] = jnp.where(even_y, firsts, lasts)

    for copy in loads:
        copy.wait()


def split(count):
    return [(4 * (k // 2) + k % 2, 2) for k in range(count // 2)]


def slices_kernel(n_gx, n_gy, R, owner, source, sent, kept, slices):
    gy = lax.axis_index("gy")
    row = iota((CHUNK, CY), 0)
    edge = (iota((CHUNK, CY), 1) >= 96) & ((row & 7) >= 6)
    sides = jnp.where(row < CXC, owner[(gy + n_gy - 1) % n_gy], owner[(gy + 1) % n_gy])
    source[...] = jnp.where(edge, sides, owner[gy])
    part = iota((n_gx, CY), 1) // CYC
    for s in range(STEPS):
        halves = [[R[0, s, c, :, t * CY:(t + 1) * CY] for t in range(2)] for c in range(3)]
        for r in range(CXC):
            turned = jnp.zeros((n_gx, CY), F32)
            for c in range(3):
                turned = jnp.where(part == c, roll(halves[c][r // 4], CYC * (c - r % 4), 1), turned)
            if r < 3:
                turned = jnp.where(part == 3, roll(roll(halves[r][0], n_gx - 1, 0), 96, 1), turned)
            elif r < 6:
                turned = jnp.where(part == 3, roll(halves[r - 3][1], 1, 0), turned)
            slices[pl.ds(s * CXC + r, n_gx, stride=CHUNK), :] = turned
    bit = (lax.axis_index("gx") >> 1) & 1
    for k, (at, step) in enumerate(split(n_gx)):
        for out, side in ((sent, 1 - bit), (kept, bit)):
            out[k] = slices[pl.ds(pl.multiple_of((at + step * side) * CHUNK, CHUNK), CHUNK), :]


def trade_kernel(width, got, kept, source, sent, kept_out, held):
    gx = lax.axis_index("gx")
    mine = ((source[...] ^ gx) & width) == 0
    count = got.shape[0]
    for i in range(count):
        held[i] = jnp.where(mine, kept[i], got[i])
    bit = (gx & (2 * width)) // (2 * width)
    for k, (at, step) in enumerate(split(count)):
        sent[k] = held[at + step * (1 - bit)]
        kept_out[k] = held[at + step * bit]


def ends_kernel(width, got, kept, source, pair, ta, tb):
    even_y = (lax.axis_index("gy") & 1) == 0
    mine = ((source[...] ^ lax.axis_index("gx")) & width) == 0
    lane = iota((8, CY), 1)
    sub = iota((8, CY), 0)
    digit, group = (lane - 96) % 10, (lane - 96) // 10
    row = jnp.where(digit < 8, digit, jnp.where(digit == 8, group, 3 + group))
    here = (lane >= 96) & (group < 3) & (sub == row)
    tiles = [jnp.zeros((8, CY), F32), jnp.zeros((8, CY), F32)]
    for i in range(4):
        pair[i] = jnp.where(mine, kept[i], got[i])
        for s in range(STEPS):
            tile = pair[i, s * CXC:(s + 1) * CXC, :]
            for k, col in enumerate((CYC - 1, 0)):
                idx = jnp.where(here, jnp.where(digit < 8, group * CYC, 96) + col, 0)
                ends = jnp.sum(jnp.where(here, take(tile, idx), 0.0), axis=0, keepdims=True)
                tiles[k] = jnp.where(sub == 2 * i + s, jnp.broadcast_to(ends, (8, CY)), tiles[k])
    ta[...] = jnp.where(even_y, tiles[0], tiles[1])
    tb[...] = jnp.where(even_y, tiles[1], tiles[0])


def edges_kernel(width, quad, tca, tcb, own, sent, kept):
    even_y = (lax.axis_index("gy") & 1) == 0
    bit = (lax.axis_index("gx") & width) // width
    beside = iota((1, CY), 1) >= 96
    for k, (first, step) in enumerate(split(4)):
        for out, side in ((sent, 1 - bit), (kept, bit)):
            at = first + step * side
            out[k] = quad[at]
            for s in range(STEPS):
                a, b = tca[PACKS, pl.ds(2 * at + s, 1), :], tcb[PACKS, pl.ds(2 * at + s, 1), :]
                for j, ends in enumerate((jnp.where(even_y, b, a), jnp.where(even_y, a, b))):
                    put = j * CXC + 6 + s
                    out[k, put:put + 1, :] = jnp.where(beside, ends, out[k, put:put + 1, :])


def spread_table(table):
    scaled = table[...] * 0.1
    spread = jnp.concatenate([scaled] * (CY // ZONES), axis=1)
    return [spread[k:k + 1, :] for k in range(3)]


def material_kernel(zones, zone_tail, table, LAM, MU, BUOY):
    columns = [jnp.broadcast_to(row, (RING, CY)) for row in spread_table(table)]
    for z in range(NZ):
        ids = jnp.concatenate([zones[z], zone_tail[z].astype(jnp.int32)], axis=0)
        for k, ref in enumerate((LAM, MU, BUOY)):
            ref[z] = take(columns[k], ids)


XX, XZ, XY, YY, YZ, ZZ = range(6)


def dx(x):
    return roll(x, RING - 1, 0) - roll(x, 1, 0)


def dy(x, seam, z):
    lane = iota((RING, CY), 1)
    if seam is None:
        return jnp.where(lane == CY - 1, 0.0, roll(x, CY - 1, 1)) - jnp.where(lane == 0, 0.0, roll(x, 1, 1))
    seam = roll(seam, -(16 * z + 3), 1)
    return jnp.where(lane == CY - 1, seam, roll(x, CY - 1, 1)) - jnp.where(lane == 0, seam, roll(x, 1, 1))


def dz(ref, f, z):
    if z == 0:
        return ref[f, 1]
    if z == NZ - 1:
        return -ref[f, NZ - 2]
    return ref[f, z + 1] - ref[f, z - 1]


def band_dy(x):
    return roll(x, CY - 1, 1) - roll(x, 1, 1)


def band_dz(x):
    lane = iota((RING, CY), 1)
    return jnp.where(lane < CY - 16, roll(x, CY - 16, 1), 0.0) - jnp.where(lane >= 16, roll(x, 16, 1), 0.0)


def seams(band, fields):
    lane = iota((RING, CY), 1)
    return {f: jnp.where(lane % 16 == 2, roll(band[f], -10, 1), band[f]) for f in fields}


def velocity_planes(planes, S, V, MU, BUOY, band, drm):
    seam = {XY: None, YY: None, YZ: None} if band is None else seams(band, (XY, YY, YZ))
    for z in planes:
        sxy, sxz, syz = S[XY, z], S[XZ, z], S[YZ, z]
        force = [
            dx(S[XX, z]) + dy(sxy, seam[XY], z) + dz(S, XZ, z),
            dx(sxy) + dy(S[YY, z], seam[YY], z) + dz(S, YZ, z),
            dx(sxz) + dy(syz, seam[YZ], z) + dz(S, ZZ, z),
        ]
        if z == NZ - 1:
            force = [force[c] + (20.0 * MU[z]) * drm(c, 0) for c in range(3)]
        for c in range(3):
            V[c, z] = V[c, z] + BUOY[z] * force[c]


def velocity_seams(planes, V, BUOY, band):
    lane = iota((RING, CY), 1)
    sign = jnp.where(lane == 0, -1.0, jnp.where(lane == CY - 1, 1.0, 0.0))
    seam = seams(band, (XY, YY, YZ))
    for z in planes:
        scale = BUOY[z] * sign
        for c, f in enumerate((XY, YY, YZ)):
            V[c, z] = V[c, z] + scale * roll(seam[f], -(16 * z + 3), 1)


def velocity_band(band, new, BM, drm):
    sxy, sxz, syz = band[XY], band[XZ], band[YZ]
    force = [
        dx(band[XX]) + band_dy(sxy) + band_dz(sxz),
        dx(sxy) + band_dy(band[YY]) + band_dz(syz),
        dx(sxz) + band_dy(syz) + band_dz(band[ZZ]),
    ]
    for c in range(3):
        if drm is not None:
            force[c] = force[c] + (20.0 * BM[1]) * drm(c, 1)
        new[6 + c] = band[6 + c] + BM[2] * force[c]


def stress_plane(z, seam, S, V, LAM, MU, fields):
    vx, vy, vz = V[0, z], V[1, z], V[2, z]
    mu = MU[z]
    if XX in fields:
        lam = LAM[z]
        xx, yy, zz = dx(vx), dy(vy, seam[7], z), dz(V, 2, z)
        theta = lam * (xx + yy + zz)
        two = mu + mu
        S[XX, z] = S[XX, z] + (theta + two * xx)
        S[YY, z] = S[YY, z] + (theta + two * yy)
        S[ZZ, z] = S[ZZ, z] + (theta + two * zz)
    if XZ in fields:
        S[XZ, z] = S[XZ, z] + mu * (dz(V, 0, z) + dx(vz))
    if XY in fields:
        S[XY, z] = S[XY, z] + mu * (dy(vx, seam[6], z) + dx(vy))
    if YZ in fields:
        S[YZ, z] = S[YZ, z] + mu * (dz(V, 1, z) + dy(vz, seam[8], z))


def stress_band(band, new, BM):
    vx, vy, vz = new[6], new[7], new[8]
    lam, mu = BM[0], BM[1]
    xx, yy, zz = dx(vx), band_dy(vy), band_dz(vz)
    theta = lam * (xx + yy + zz)
    two = mu + mu
    new[XX] = band[XX] + (theta + two * xx)
    new[YY] = band[YY] + (theta + two * yy)
    new[ZZ] = band[ZZ] + (theta + two * zz)
    new[XZ] = band[XZ] + mu * (band_dz(vx) + dx(vz))
    new[XY] = band[XY] + mu * (band_dy(vx) + dx(vy))
    new[YZ] = band[YZ] + mu * (band_dz(vy) + band_dy(vz))


ALL = (XX, XZ, XY, YY, YZ, ZZ)


def unpack_kernel(
    S_in, V_in, ra, rb, ends_a, ends_b, ca, cb,
    S, V, zone_tail, ta, tb,
):
    even_x = (lax.axis_index("gx") & 1) == 0
    even_y = (lax.axis_index("gy") & 1) == 0
    low = iota((8, CY), 0) < 4
    slot = iota((8, CY), 1) // HALO
    tail = slice(CX, RING)
    for p in range(PACKS):
        lasts = jnp.zeros((8, CY), F32)
        firsts = jnp.zeros((8, CY), F32)
        for s in range(4):
            f = 4 * p + s
            if f >= FIELDS:
                continue
            for q in range(NZ // 2):
                k = f * 4 + q
                after = jnp.where(even_x, ra[k], rb[k])
                before = jnp.where(even_x, rb[k], ra[k])
                both = (jnp.where(low, after, before), roll(jnp.where(low, before, after), 4, 0))
                for z in (2 * q, 2 * q + 1):
                    rows = both[z % 2]
                    turned = roll(rows, 16 * z + 4 * s + 4, 1)
                    at = 4 * z + s
                    lasts = jnp.where(slot == at, turned, lasts)
                    firsts = jnp.where(slot == (at + 1) % 32, turned, firsts)
                    if f < 6:
                        S[f, z, tail, :] = rows
                    elif f < 9:
                        V[f - 6, z, tail, :] = rows
                    else:
                        zone_tail[z] = rows
        ta[p] = jnp.where(even_y, lasts, firsts)
        tb[p] = jnp.where(even_y, firsts, lasts)
    ta[PACKS] = ends_a[...]
    tb[PACKS] = ends_b[...]


def inner_kernel(S, V_in, MU, BUOY, own_a, own_b, ta, tb, V, own):
    even_y = (lax.axis_index("gy") & 1) == 0
    quarter = (iota((RING, CY), 1) // 4) % 4
    for p in range(PACKS):
        at = slice(p * CX, (p + 1) * CX)
        one, two = jnp.concatenate([own_a[at], ta[p]], axis=0), jnp.concatenate([own_b[at], tb[p]], axis=0)
        last, first = jnp.where(even_y, one, two), jnp.where(even_y, two, one)
        for s in range(4):
            if 4 * p + s < FIELDS:
                own[4 * p + s] = jnp.where(quarter == 1, roll(first, -4 * s, 1), roll(last, 8 - 4 * s, 1))
    velocity_planes(range(0, 5), S, V, MU, BUOY, None, None)


def cone_kernel(
    S_in, V_in, LAM, MU, BUOY, table, own, ca, cb, tca, tcb, building, block,
    S, V, BF, BM, BV, BW, shares,
):
    even_y = (lax.axis_index("gy") & 1) == 0
    lane8 = iota((8, CY), 1)
    sub8 = iota((8, CY), 0)
    quarter = (iota((RING, CY), 1) // 4) % 4
    columns = spread_table(table)

    for p in range(PACKS):
        at = slice(p * CX, (p + 1) * CX)
        one, two = jnp.concatenate([ca[at], tca[p]], axis=0), jnp.concatenate([cb[at], tcb[p]], axis=0)
        from_right, from_left = jnp.where(even_y, one, two), jnp.where(even_y, two, one)
        for s in range(4):
            f = 4 * p + s
            if f < FIELDS:
                BF[f] = jnp.where(
                    quarter == 0, roll(from_left, -4 * s, 1),
                    jnp.where(quarter == 3, roll(from_right, 8 - 4 * s, 1), own[f]),
                )
    ids = BF[9].astype(jnp.int32)
    for k in range(3):
        BM[k] = take(jnp.broadcast_to(columns[k], (RING, CY)), ids)

    velocity_seams(range(0, 5), V, BUOY, BF)
    velocity_band(BF, BW, BM, None)
    for c in range(3):
        BV[c] = BW[6 + c]
    seam = seams(BW, (6, 7, 8))
    for z in range(0, 4):
        stress_plane(z, seam, S, V, LAM, MU, ALL)
    stress_band(BF, BW, BM)
    velocity_planes(range(0, 3), S, V, MU, BUOY, BW, None)
    velocity_band(BW, BW, BM, None)
    stress_plane(1, seams(BW, (8,)), S, V, LAM, MU, (XZ, YZ))

    total = jnp.zeros((8, CY), F32)
    for c, f in enumerate((XZ, YZ)):
        for r in range(CX // BLOCK):
            row = jnp.sum(S[f, 1, 8 * r:8 * r + 8, :], axis=0, keepdims=True)
            total = jnp.where(sub8 == 4 * c + r, jnp.broadcast_to(row, (8, CY)), total)
    for shift in (1, 2, 4):
        total = total + roll(total, CY - shift, 1)
    total = total * (1.0 / (BLOCK * BLOCK))
    ids = jnp.broadcast_to(jnp.concatenate([block[0], block[0]], axis=1), (8, CY))
    cells = CY // BLOCK
    picked = take(total, (ids % cells) * BLOCK)
    mine = (sub8 % 4 == ids // cells) & (sub8 // 4 == lane8 // FP_DEV)
    values = jnp.sum(jnp.where(mine, picked, 0.0), axis=0, keepdims=True)
    names = jnp.concatenate([building[0], building[0]], axis=1).astype(F32)
    message = jnp.concatenate([values, names], axis=0)
    shares[...] = jnp.broadcast_to(message[None], shares.shape)


def upper_kernel(S_in, V_in, LAM, MU, BUOY, BF, BV, BW, S, V):
    velocity_planes(range(5, 7), S, V, MU, BUOY, BF, None)
    seam = {6 + c: value for c, value in seams(BV, range(3)).items()}
    for z in range(4, 6):
        stress_plane(z, seam, S, V, LAM, MU, ALL)
    velocity_planes(range(3, 5), S, V, MU, BUOY, BW, None)
    seam = seams(BW, (6, 7, 8))
    for z in range(0, 4):
        stress_plane(z, seam, S, V, LAM, MU, (XX, XY) if z == 1 else ALL)


def lower_kernel(
    S_in, V_in, LAM, MU, BUOY, BF_in, BM, source, got, kept,
    S, V, BF, vel_out, stress_out, DRM, drm_in, sems,
):
    saves = []

    def save(ref, out, first, count):
        at = pl.ds(first, count)
        copy = pltpu.make_async_copy(ref.at[:, at, pl.ds(0, CX), :], out.at[:, at], sems.at[len(saves)])
        copy.start()
        saves.append(copy)

    save(V, vel_out, 0, 5)
    save(S, stress_out, 0, 4)
    low = iota((8, CY), 0) < 4
    lane8 = iota((8, CY), 1)
    quarter8 = (lane8 // 4) % 4
    deepest = lane8 >= 16 * (NZ - 1)

    mine = ((source[...] ^ lax.axis_index("gx")) & 1) == 0
    drm_in[...] = jnp.where(mine, kept[0], got[0])

    def wide(row):
        return jnp.broadcast_to(drm_in[row:row + 1, :], (8, CY))

    for s in range(STEPS):
        both = jnp.where(lane8 >= 96, wide(6 + s), roll(wide(CXC + 6 + s), 32, 1))
        for c in range(3):
            for q in range(RING // 8):
                if q < 4:
                    rows = jnp.where(low, wide(s * CXC + 2 * q), wide(s * CXC + 2 * q + 1))
                    base = c * CYC
                else:
                    rows = jnp.where(low, wide(s * CXC + c), wide(s * CXC + 3 + c))
                    base = 3 * CYC
                DRM[s, c, 0, 8 * q:8 * q + 8, :] = take(rows, base + lane8 // COARSE)
                inner = take(rows, base + jnp.where(quarter8 == 2, CYC - 1, 0))
                at = c * 10 + 2 * q + jnp.where(low, 0, 1) + jnp.where(quarter8 == 0, 96, 0)
                value = jnp.where((quarter8 & 1) == (quarter8 >> 1), take(both, at), inner)
                DRM[s, c, 1, 8 * q:8 * q + 8, :] = jnp.where(deepest, value, 0.0)

    def drm(step):
        return lambda c, k: DRM[step, c, k]

    velocity_planes(range(7, NZ), S, V, MU, BUOY, BF, drm(0))
    velocity_band(BF, BF, BM, drm(0))
    seam = seams(BF, (6, 7, 8))
    for z in range(6, NZ):
        stress_plane(z, seam, S, V, LAM, MU, ALL)
    stress_band(BF, BF, BM)
    velocity_planes(range(5, NZ), S, V, MU, BUOY, BF, drm(1))
    velocity_band(BF, BF, BM, drm(1))
    save(V, vel_out, 5, NZ - 5)
    seam = seams(BF, (6, 7, 8))
    for z in range(4, NZ):
        stress_plane(z, seam, S, V, LAM, MU, ALL)
        save(S, stress_out, z, 1)
    for copy in saves:
        copy.wait()


def sum_kernel(n, shares, out):
    half = n // 2
    low = iota((half, CY), 1) < FP_DEV
    values = shares[:, 0, :]
    names = shares[:, 1, :].astype(jnp.int32)
    entry = [
        jnp.where(low, values[:half], roll(values[half:], FP_DEV, 1)),
        jnp.where(low, roll(values[:half], FP_DEV, 1), values[half:]),
    ]
    names = jnp.where(low, names[:half], names[half:])
    high = names // CY
    names = names % CY
    n_high = BUILDINGS // CY
    rows = iota((n_high, CY), 0)
    wanted = iota((CY, CY), 0)
    acc = jnp.zeros((6 * n_high, CY), F32)
    for k in range(half):
        hot = (jnp.broadcast_to(names[k:k + 1], (CY, CY)) == wanted).astype(F32).astype(jnp.bfloat16)
        here = jnp.broadcast_to(high[k:k + 1], (n_high, CY)) == rows
        left = []
        for c in range(2):
            rest = jnp.where(here, jnp.broadcast_to(entry[c][k:k + 1], (n_high, CY)), 0.0)
            for _ in range(3):
                piece = rest.astype(jnp.bfloat16)
                rest = rest - piece.astype(F32)
                left.append(piece.astype(F32))
        left = jnp.concatenate(left, axis=0).astype(jnp.bfloat16)
        acc = acc + lax.dot_general(left, hot, (((1,), (1,)), ((), ())), preferred_element_type=F32)
    sums = []
    for c in range(2):
        base = 3 * c * n_high
        sums.append(acc[base:base + n_high] + acc[base + n_high:base + 2 * n_high] + acc[base + 2 * n_high:base + 3 * n_high])
    for h in range(n_high):
        out[:, h * CY:(h + 1) * CY] = jnp.concatenate([sums[0][h:h + 1], sums[1][h:h + 1]], axis=0)


def pairs_near(n):
    return [(i, i ^ 1) for i in range(n)]


def pairs_far(n):
    return [(i, (i + 1) % n if i % 2 else (i - 1) % n) for i in range(n)]


def after(x, *done):
    return lax.optimization_barrier((x,) + done)[0]


def body(n_gx, n_gy, velocity, stress, zones, zone_table, regional, owner, building, block):
    n = n_gx * n_gy
    gx = lax.axis_index("gx")
    vmem = pl.BlockSpec(memory_space=pltpu.VMEM)
    hbm = pl.BlockSpec(memory_space=pltpu.HBM)
    anywhere = pl.BlockSpec(memory_space=pl.ANY)
    params = pltpu.CompilerParams(vmem_limit_bytes=VMEM_LIMIT)

    def shaped(*shape):
        return jax.ShapeDtypeStruct(shape, F32)

    def whole(shape, dtype):
        return jax.ShapeDtypeStruct(shape, dtype)

    s_ring = shaped(6, NZ, RING, CY)
    v_ring = shaped(3, NZ, RING, CY)
    m_ring = shaped(NZ, RING, CY)
    rows = shaped(FIELDS * 4, 8, CY)
    cols = shaped(COLS, CY)
    from_hbm = [
        pltpu.with_memory_space_constraint(x, pltpu.HBM)
        for x in (velocity, stress, zones, regional, zone_table, building, block)
    ]
    gxa, gxb, regional, zone_table, building, block = pl.pallas_call(
        rows_kernel,
        out_shape=(
            rows, rows, whole(regional.shape, F32), whole(zone_table.shape, F32),
            whole(building.shape, jnp.int32), whole(block.shape, jnp.int32),
        ),
        in_specs=[hbm] * 7,
        out_specs=(vmem,) * 6,
        scratch_shapes=[
            pltpu.VMEM((2, 9, NZ, 8, CY), F32),
            pltpu.VMEM((2, NZ, 8, CY), jnp.int32),
            pltpu.SemaphoreType.DMA((10,)),
        ],
        compiler_params=params,
        name="pack_rows",
    )(*from_hbm)
    rb = lax.ppermute(gxb, "gx", pairs_far(n_gx))
    ra = lax.ppermute(gxa, "gx", pairs_near(n_gx))
    S, V, gya, gyb = pl.pallas_call(
        cols_kernel,
        out_shape=(s_ring, v_ring, cols, cols),
        in_specs=[vmem] * 3,
        out_specs=(vmem,) * 4,
        scratch_shapes=[pltpu.SemaphoreType.DMA((2,))],
        compiler_params=params,
        name="pack_columns",
    )(velocity, stress, zones)
    cb = lax.ppermute(gyb, "gy", pairs_far(n_gy))
    ca = lax.ppermute(gya, "gy", pairs_near(n_gy))

    def across(x, width):
        return lax.ppermute(x, "gx", [(i, i ^ width) for i in range(n_gx)])

    half = shaped(n_gx // 2, CHUNK, CY)
    source, sent, kept = pl.pallas_call(
        functools.partial(slices_kernel, n_gx, n_gy),
        out_shape=(whole((CHUNK, CY), jnp.int32), half, half),
        in_specs=[vmem, pl.BlockSpec(memory_space=pltpu.SMEM)],
        out_specs=(vmem,) * 3,
        scratch_shapes=[pltpu.VMEM((n_gx * CHUNK, CY), F32)],
        compiler_params=params,
        name="slices",
    )(regional, owner)
    width = 2
    while 4 * width < n_gx:
        count = sent.shape[0]
        part = shaped(count // 2, CHUNK, CY)
        sent, kept = pl.pallas_call(
            functools.partial(trade_kernel, width),
            out_shape=(part, part),
            in_specs=[vmem] * 3,
            out_specs=(vmem,) * 2,
            scratch_shapes=[pltpu.VMEM((count, CHUNK, CY), F32)],
            compiler_params=params,
            name="trade",
        )(across(sent, width), kept, source)
        width *= 2
    tile = shaped(8, CY)
    quad, ends_a, ends_b = pl.pallas_call(
        functools.partial(ends_kernel, width),
        out_shape=(shaped(4, CHUNK, CY), tile, tile),
        in_specs=[vmem] * 3,
        out_specs=(vmem,) * 3,
        compiler_params=params,
        name="ends",
    )(across(sent, width), kept, source)
    ends = shaped(PACKS + 1, 8, CY)
    S, V, zone_tail, ta, tb = pl.pallas_call(
        unpack_kernel,
        out_shape=(s_ring, v_ring, shaped(NZ, 8, CY), ends, ends),
        in_specs=[vmem] * 6 + [anywhere] * 2,
        out_specs=(vmem,) * 5,
        input_output_aliases={0: 0, 1: 1},
        compiler_params=params,
        name="unpack",
    )(S, V, ra, rb, ends_a, ends_b, ca, cb)
    tcb = lax.ppermute(tb, "gy", pairs_far(n_gy))
    tca = lax.ppermute(ta, "gy", pairs_near(n_gy))
    LAM, MU, BUOY = pl.pallas_call(
        material_kernel,
        out_shape=(m_ring,) * 3,
        in_specs=[vmem] * 3,
        out_specs=(vmem,) * 3,
        compiler_params=params,
        name="materials",
    )(zones, zone_tail, zone_table)
    V, own = pl.pallas_call(
        inner_kernel,
        out_shape=(v_ring, shaped(FIELDS, RING, CY)),
        in_specs=[vmem] * 8,
        out_specs=(vmem,) * 2,
        input_output_aliases={1: 0},
        compiler_params=params,
        name="inner",
    )(S, V, MU, BUOY, gya, gyb, ta, tb)
    two = shaped(2, CHUNK, CY)
    width *= 2
    sent, kept = pl.pallas_call(
        functools.partial(edges_kernel, width),
        out_shape=(two, two),
        in_specs=[vmem] * 3 + [anywhere],
        out_specs=(vmem,) * 2,
        compiler_params=params,
        name="edges",
    )(quad, tca, tcb, own)
    band = shaped(3, RING, CY)
    S, V, BF, BM, BV, BW, shares = pl.pallas_call(
        cone_kernel,
        out_shape=(s_ring, v_ring, shaped(FIELDS, RING, CY), band, band, shaped(9, RING, CY), shaped(n, 2, CY)),
        in_specs=[vmem] * 13,
        out_specs=(vmem,) * 7,
        input_output_aliases={0: 0, 1: 1},
        compiler_params=params,
        name="cone",
    )(S, V, LAM, MU, BUOY, zone_table, own, ca, cb, tca, tcb, building, block)
    held = jnp.where(((source ^ gx) & width) == 0, kept, across(sent, width))
    odd = (gx & 1) != 0
    sent, kept = jnp.where(odd, held[0], held[1])[None], jnp.where(odd, held[1], held[0])[None]
    got = across(sent, 1)
    every = lax.all_to_all(shares, ("gx", "gy"), 0, 0)
    S, V = pl.pallas_call(
        upper_kernel,
        out_shape=(s_ring, v_ring),
        in_specs=[vmem] * 8,
        out_specs=(vmem,) * 2,
        input_output_aliases={0: 0, 1: 1},
        compiler_params=params,
        name="upper",
    )(S, V, LAM, MU, BUOY, BF, BV, BW)
    shear = pl.pallas_call(
        functools.partial(sum_kernel, n),
        out_shape=shaped(2, BUILDINGS),
        in_specs=[vmem],
        out_specs=vmem,
        compiler_params=params,
        name="sum_by_building",
    )(every)
    _, _, _, vel_out, stress_out = pl.pallas_call(
        lower_kernel,
        out_shape=(s_ring, v_ring, shaped(FIELDS, RING, CY), shaped(*velocity.shape), shaped(*stress.shape)),
        in_specs=[vmem] * 10,
        out_specs=(vmem, vmem, vmem, hbm, hbm),
        scratch_shapes=[
            pltpu.VMEM((STEPS, 3, 2, RING, CY), F32),
            pltpu.VMEM((CHUNK, CY), F32),
            pltpu.SemaphoreType.DMA((NZ,)),
        ],
        input_output_aliases={0: 0, 1: 1, 5: 2},
        compiler_params=params,
        name="lower",
    )(S, V, LAM, MU, BUOY, BF, BM, source, got, kept)
    return vel_out, stress_out, shear


def solution(mesh):
    n_gx, n_gy = mesh.shape["gx"], mesh.shape["gy"]
    return jax.shard_map(
        functools.partial(body, n_gx, n_gy),
        mesh=mesh,
        in_specs=(
            P(None, None, "gx", "gy"),
            P(None, None, "gx", "gy"),
            P(None, "gx", "gy"),
            P(),
            P("gx", None, None, None, "gy"),
            P(),
            P("gx", "gy", None),
            P("gx", "gy", None),
        ),
        out_specs=(P(None, None, "gx", "gy"), P(None, None, "gx", "gy"), P()),
        check_vma=False,
    )
```

time: 38.7 us -> 33.6 us (0.87)
  waiting for transfers between devices: 13.8 us -> 8.08 us
  starting transfers between devices: 13.9 us -> 14.7 us
  local copies, waits for them, and re-layouts: 0.65 us -> 0.02 us
  Pallas kernels: 9.37 us -> 9.81 us
    ppermute x7, waiting for transfers between devices: 10.3 us -> 6.75 us  [the longest x3 4.98 us: across(): return lax.ppermute(x, 'gx', [(i, i ^ width) for i in range(n_gx)])]
    all_to_all x1, waiting for transfers between devices: 3.53 us -> 1.32 us  [body(): every = lax.all_to_all(shares, ('gx', 'gy'), 0, 0)]
    ppermute x7, starting transfers between devices: 8.16 us -> 9.28 us  [the longest x1 3.57 us: body(): rb = lax.ppermute(gxb, 'gx', pairs_far(n_gx))]
    all_to_all x1, starting transfers between devices: 2.58 us -> 3.68 us  [body(): every = lax.all_to_all(shares, ('gx', 'gy'), 0, 0)]
    ppermute x1, starting transfers between devices: 2.64 us -> 1.63 us  [body(): cb = lax.ppermute(gyb, 'gy', pairs_far(n_gy))]
    unnamed x4 -> x8, local copies, waits for them, and re-layouts: 0.65 us -> 0.02 us
    ppermute x1, starting transfers between devices: 0.52 us -> 0.07 us  [body(): ca = lax.ppermute(gya, 'gy', pairs_near(n_gy))]
    pallas_call x4 -> x10, Pallas kernels: 7.88 us -> 8.25 us  [the longest x1 2.16 us: body(): pl.pallas_call(lower_kernel, out_shape=(s_ring, v_ring, shaped(FIELDS, RI...]
  transfers between devices with their start and end apart: 10 -> 10, of which waited for: 5 -> 4; matrix products, arithmetic and copies ran while one was open for 0% -> 0% of each run, Pallas kernels for 8% -> 21%
where the time goes in v3:
time: 33.6 us; the launch traced here: 33.4 us
  starting transfers between devices  14.7 us (44%)
  Pallas kernels  9.81 us (29%)
  waiting for transfers between devices  8.08 us (24%)
  between operations  0.84 us (2%)
    ppermute x3, waiting for transfers between devices, across(): return lax.ppermute(x, 'gx', [(i, i ^ width) for i in range(n_gx)])  4.98 us
    all_to_all x1, starting transfers between devices, body(): every = lax.all_to_all(shares, ('gx', 'gy'), 0, 0)  3.68 us
    ppermute x1, starting transfers between devices, body(): rb = lax.ppermute(gxb, 'gx', pairs_far(n_gx))  3.57 us
    ppermute x1, starting transfers between devices, body(): ra = lax.ppermute(gxa, 'gx', pairs_near(n_gx))  3 us
    pallas_call x1, Pallas kernels, body(): pl.pallas_call(lower_kernel, out_shape=(s_ring, v_ring, shaped(FIELDS, RI...  2.16 us
    pallas_call x1, Pallas kernels, body(): pl.pallas_call(cone_kernel, out_shape=(s_ring, v_ring, shaped(FIELDS, RIN...  2.07 us
    ppermute x3, starting transfers between devices, across(): return lax.ppermute(x, 'gx', [(i, i ^ width) for i in range(n_gx)])  1.97 us
    ppermute x1, waiting for transfers between devices, body(): tcb = lax.ppermute(tb, 'gy', pairs_far(n_gy))  1.76 us
  transfers between devices with their start and end apart: 10, of which 4 were waited for; matrix products, arithmetic and copies ran while one was open for 0% of the time, Pallas kernels for 21%

profile of v3, /device:TPU:0, one launch (start us, length us, event | category | flops | bytes accessed | tf_op | source)
XLA Modules:
  0.0 33.4 jit_solution(1438102571797786000)
XLA Ops:
  0.6 0.0 copy-start.2
  0.6 0.0 copy-start
  0.7 0.0 copy-start.1
  0.7 1.4 %pack_rows.1 = (f32[40,8,128]{2,1,0:T(8,128)S(1)}, f32[40,8,128]{2,1,0:T(8,128)S(1)}, f32[1,2,3,8,256]{4,3,2,1,0:T(8,128)S(1)}, f32[3,16]{1,0:T(4,128)S(1)}, s32...) custom-call(f32[3,8,32,128]{3,2,1,0:T(8,128)} %vel.3, f32[6,8,32,128]{3,2,1,0:T(8,128)} %stress.3, s32[8,32,128]{2,1,0:T(8,128)} %zones.5, ...), custom_call_target="tpu_custom_call" | custom-call | tf_op jit(solution)/shard_map/pack_rows/pallas_call | solution.py:562
  2.1 3.0 %collective-permute-start = (f32[40,8,128]{2,1,0:T(8,128)S(1)}, f32[40,8,128]{2,1,0:T(8,128)S(1)}, u32[]{:S(2)}, u32[]{:S(2)}) collective-permute-start(f32[40,8,128]{2,1,0:T(8,128)S(1)} %get-tuple-element.44), channel_id=1, source_target_pairs={{0,4},{4,0},{8,12},{12,8},{16,20},{20,16},{24,28},{28,24},{1,5},{5... | collective-permute-start | bytes 491528 | tf_op jit(solution)/shard_map/ppermute | solution.py:579
  5.1 3.6 %collective-permute-start.1 = (f32[40,8,128]{2,1,0:T(8,128)S(1)}, f32[40,8,128]{2,1,0:T(8,128)S(1)}, u32[]{:S(2)}, u32[]{:S(2)}) collective-permute-start(f32[40,8,128]{2,1,0:T(8,128)S(1)} %get-tuple-element.45), channel_id=1, source_target_pairs={{0,28},{4,8},{8,4},{12,16},{16,12},{20,24},{24,20},{28,0},{1,29},{... | collective-permute-start | bytes 491528 | tf_op jit(solution)/shard_map/ppermute | solution.py:578
  8.6 0.0 copy-done.2
  8.6 0.0 copy-done
  8.6 0.0 copy-done.1
  8.6 0.5 %pack_columns.1 = (f32[6,8,40,128]{3,2,1,0:T(8,128)S(1)}, f32[3,8,40,128]{3,2,1,0:T(8,128)S(1)}, f32[96,128]{1,0:T(8,128)S(1)}, f32[96,128]{1,0:T(8,128)S(1)}) custom-call(f32[3,8,32,128]{3,2,1,0:T(8,128)S(1)} %copy-done.1, f32[6,8,32,128]{3,2,1,0:T(8,128)S(1)} %copy-done, s32[8,32,128]{2,1,0:T(8,128)S(1)} %copy-done.2), custom_call_target="tpu_custom_call" | custom-call | tf_op jit(solution)/shard_map/pack_columns/pallas_call | solution.py:580
  9.2 0.1 collective-permute-start.3
  9.3 0.0 copy-start.3
  9.3 1.6 %collective-permute-start.4 = (f32[96,128]{1,0:T(8,128)S(1)}, f32[96,128]{1,0:T(8,128)S(1)}, u32[]{:S(2)}, u32[]{:S(2)}) collective-permute-start(f32[96,128]{1,0:T(8,128)S(1)} %get-tuple-element.53.own_b), channel_id=1, source_target_pairs={{0,3},{1,2},{2,1},{3,0},{4,7},{5,6},{6,5},{7,4},{8,11},{9,10},{10,... | collective-permute-start | bytes 147464 | tf_op jit(solution)/shard_map/ppermute | solution.py:589
  10.9 0.0 copy-done.3
  10.9 0.7 %slices.1 = (s32[16,128]{1,0:T(8,128)S(1)}, f32[4,16,128]{2,1,0:T(8,128)S(1)}, f32[4,16,128]{2,1,0:T(8,128)S(1)}) custom-call(f32[1,2,3,8,256]{4,3,2,1,0:T(8,128)S(1)} %get-tuple-element.46.R, s32[4]{0:T(128)S(1)} %copy-done.3), custom_call_target="tpu_custom_call" | custom-call | tf_op jit(solution)/shard_map/slices/pallas_call | solution.py:596
  11.6 0.1 collective-permute-start.2
  11.6 3.9 %collective-permute-done.2.got = f32[4,16,128]{2,1,0:T(8,128)S(1)} collective-permute-done((f32[4,16,128]{2,1,0:T(8,128)S(1)}, f32[4,16,128]{2,1,0:T(8,128)S(1)}, u32[]{:S(2)}, u32[]{:S(2)}) %collective-permute-start.2) | collective-permute-done | bytes 32800 | tf_op jit(solution)/shard_map/ppermute | solution.py:593
  15.6 0.1 ends.1
  15.7 0.0 collective-permute-done.3.ca
  15.7 0.0 collective-permute-done.4.cb
  15.7 0.0 collective-permute-done.ra
  15.7 0.0 collective-permute-done.1.rb
  15.7 0.2 unpack.1
  15.9 0.1 collective-permute-start.5
  16.0 0.7 %collective-permute-start.6 = (f32[4,8,128]{2,1,0:T(8,128)S(1)}, f32[4,8,128]{2,1,0:T(8,128)S(1)}, u32[]{:S(2)}, u32[]{:S(2)}) collective-permute-start(f32[4,8,128]{2,1,0:T(8,128)S(1)} %get-tuple-element.61.tb), channel_id=1, source_target_pairs={{0,3},{1,2},{2,1},{3,0},{4,7},{5,6},{6,5},{7,4},{8,11},{9,10},{10,... | collective-permute-start | bytes 49160 | tf_op jit(solution)/shard_map/ppermute | solution.py:638
  16.6 0.5 %materials.1 = (f32[8,40,128]{2,1,0:T(8,128)S(1)}, f32[8,40,128]{2,1,0:T(8,128)S(1)}, f32[8,40,128]{2,1,0:T(8,128)S(1)}) custom-call(s32[8,32,128]{2,1,0:T(8,128)S(1)} %copy-done.2, f32[8,8,128]{2,1,0:T(8,128)S(1)} %get-tuple-element.56.zone_tail, f32[3,16]{1,0:T(4,128)S(1)} %get-tuple-element.57.table), custom_call_target="tpu_custom_call" | custom-call | tf_op jit(solution)/shard_map/materials/pallas_call | solution.py:640
  17.1 0.3 %inner.1 = (f32[3,8,40,128]{3,2,1,0:T(8,128)S(1)}, f32[10,40,128]{2,1,0:T(8,128)S(1)}) custom-call(f32[6,8,40,128]{3,2,1,0:T(8,128)S(1)} %get-tuple-element.54.S.S_in, f32[3,8,40,128]{3,2,1,0:T(8,128)S(1)} %get-tuple-element.55.V_in, f32[8,40,128]{2,1,0:T(8,128)S(1)} %get-tuple-element.58.MU, ...), custom_call_target="tpu_custom_call", output_to_operand_aliasing={{0}: (1, {})} | custom-call | tf_op jit(solution)/shard_map/inner/pallas_call | solution.py:648
  17.4 0.0 collective-permute-done.5.tca
  17.4 1.8 %collective-permute-done.6.tcb = f32[4,8,128]{2,1,0:T(8,128)S(1)} collective-permute-done((f32[4,8,128]{2,1,0:T(8,128)S(1)}, f32[4,8,128]{2,1,0:T(8,128)S(1)}, u32[]{:S(2)}, u32[]{:S(2)}) %collective-permute-start.6) | collective-permute-done | bytes 16416 | tf_op jit(solution)/shard_map/ppermute | solution.py:638
  19.2 0.1 collective-permute-start.7
  19.3 2.1 %cone.1 = (f32[6,8,40,128]{3,2,1,0:T(8,128)S(1)}, f32[3,8,40,128]{3,2,1,0:T(8,128)S(1)}, f32[10,40,128]{2,1,0:T(8,128)S(1)}, f32[3,40,128]{2,1,0:T(8,128)S(1)}, ...) custom-call(f32[6,8,40,128]{3,2,1,0:T(8,128)S(1)} %get-tuple-element, ...), custom_call_target="tpu_custom_call", output_to_operand_aliasing={{0}: (0, {}), {1}: (1, {})} | custom-call | tf_op jit(solution)/shard_map/cone/pallas_call | solution.py:668
  21.4 3.7 %all-to-all-start = ((f32[32,2,128]{2,1,0:T(2,128)}), f32[32,2,128]{2,1,0:T(2,128)S(1)}, u32[]{:S(2)}, u32[]{:S(2)}) async-start(f32[32,2,128]{2,1,0:T(2,128)} %get-tuple-element.80), calls=%async_computation | async-start | bytes 65536 | tf_op jit(solution)/shard_map/all_to_all | solution.py:681
  25.1 0.0 collective-permute-done.7
  25.1 1.8 %collective-permute-start.8 = (f32[1,16,128]{2,1,0:T(8,128)S(1)}, f32[1,16,128]{2,1,0:T(8,128)S(1)}, u32[]{:S(2)}, u32[]{:S(2)}) collective-permute-start(f32[1,16,128]{2,1,0:T(8,128)S(1)} %get-tuple-element.82), channel_id=1, source_target_pairs={{0,4},{4,0},{8,12},{12,8},{16,20},{20,16},{24,28},{28,24},{1,5},{5... | collective-permute-start | bytes 24584 | tf_op jit(solution)/shard_map/ppermute | solution.py:593
  27.0 0.8 %upper.1 = (f32[6,8,40,128]{3,2,1,0:T(8,128)S(1)}, f32[3,8,40,128]{3,2,1,0:T(8,128)S(1)}) custom-call(f32[6,8,40,128]{3,2,1,0:T(8,128)S(1)} %get-tuple-element.67.S_in, f32[3,8,40,128]{3,2,1,0:T(8,128)S(1)} %get-tuple-element.68.V_in, f32[8,40,128]{2,1,0:T(8,128)S(1)} %get-tuple-element.63.LAM, ...), custom_call_target="tpu_custom_call", output_to_operand_aliasing={{0}: (0, {}), {1}: (1, {})} | custom-call | tf_op jit(solution)/shard_map/upper/pallas_call | solution.py:682
  27.8 1.1 %collective-permute-done.8.got = f32[1,16,128]{2,1,0:T(8,128)S(1)} collective-permute-done((f32[1,16,128]{2,1,0:T(8,128)S(1)}, f32[1,16,128]{2,1,0:T(8,128)S(1)}, u32[]{:S(2)}, u32[]{:S(2)}) %collective-permute-start.8) | collective-permute-done | bytes 8224 | tf_op jit(solution)/shard_map/ppermute | solution.py:593
  28.8 2.2 %lower.1 = (f32[6,8,40,128]{3,2,1,0:T(8,128)S(1)}, f32[3,8,40,128]{3,2,1,0:T(8,128)S(1)}, f32[10,40,128]{2,1,0:T(8,128)S(1)}, f32[3,8,32,128]{3,2,1,0:T(8,128)}, f32[6,8,32,128]{3,2,1,0:T(8,128)}) custom-call(f32[6,8,40,128]{3,2,1,0:T(8,128)S(1)} %get-tuple-element.72.S_in, ...), custom_call_target="tpu_custom_call", output_to_operand_aliasing={{0}: (0, {}), {1}: (1, {}), {2}: (5, {})} | custom-call | tf_op jit(solution)/shard_map/lower/pallas_call | solution.py:699
  31.0 1.3 %all-to-all-done.shares = f32[32,2,128]{2,1,0:T(2,128)S(1)} async-done(((f32[32,2,128]{2,1,0:T(2,128)}), f32[32,2,128]{2,1,0:T(2,128)S(1)}, u32[]{:S(2)}, u32[]{:S(2)}) %all-to-all-start) | async-done | bytes 32800 | tf_op jit(solution)/shard_map/all_to_all | solution.py:681
  32.3 1.1 %sum_by_building.1 = f32[2,1024]{1,0:T(2,128)} custom-call(f32[32,2,128]{2,1,0:T(2,128)S(1)} %all-to-all-done.shares), custom_call_target="tpu_custom_call" | custom-call | tf_op jit(solution)/shard_map/sum_by_building/pallas_call | solution.py:691
  (4 shorter events, 0.0 us)
Async XLA Ops:
  0.6 8.0 %copy-start.2 = (s32[8,32,128]{2,1,0:T(8,128)S(1)}, s32[8,32,128]{2,1,0:T(8,128)}, u32[]{:S(2)}) copy-start(s32[8,32,128]{2,1,0:T(8,128)} %zones.5) | copy-start | bytes 393220
  0.6 8.0 %copy-start = (f32[6,8,32,128]{3,2,1,0:T(8,128)S(1)}, f32[6,8,32,128]{3,2,1,0:T(8,128)}, u32[]{:S(2)}) copy-start(f32[6,8,32,128]{3,2,1,0:T(8,128)} %stress.3) | copy-start | bytes 2359300
  0.7 8.0 %copy-start.1 = (f32[3,8,32,128]{3,2,1,0:T(8,128)S(1)}, f32[3,8,32,128]{3,2,1,0:T(8,128)}, u32[]{:S(2)}) copy-start(f32[3,8,32,128]{3,2,1,0:T(8,128)} %vel.3) | copy-start | bytes 1179652
  2.1 13.6 %collective-permute-start = (f32[40,8,128]{2,1,0:T(8,128)S(1)}, f32[40,8,128]{2,1,0:T(8,128)S(1)}, u32[]{:S(2)}, u32[]{:S(2)}) collective-permute-start(f32[40,8,128]{2,1,0:T(8,128)S(1)} %get-tuple-element.44), channel_id=1, source_target_pairs={{0,4},{4,0},{8,12},{12,8},{16,20},{20,16},{24,28},{28,24},{1,5},{5... | collective-permute-start | bytes 491528 | tf_op jit(solution)/shard_map/ppermute | solution.py:579
  5.1 10.6 %collective-permute-start.1 = (f32[40,8,128]{2,1,0:T(8,128)S(1)}, f32[40,8,128]{2,1,0:T(8,128)S(1)}, u32[]{:S(2)}, u32[]{:S(2)}) collective-permute-start(f32[40,8,128]{2,1,0:T(8,128)S(1)} %get-tuple-element.45), channel_id=1, source_target_pairs={{0,28},{4,8},{8,4},{12,16},{16,12},{20,24},{24,20},{28,0},{1,29},{... | collective-permute-start | bytes 491528 | tf_op jit(solution)/shard_map/ppermute | solution.py:578
  9.2 6.5 %collective-permute-start.3 = (f32[96,128]{1,0:T(8,128)S(1)}, f32[96,128]{1,0:T(8,128)S(1)}, u32[]{:S(2)}, u32[]{:S(2)}) collective-permute-start(f32[96,128]{1,0:T(8,128)S(1)} %get-tuple-element.52.own_a), channel_id=1, source_target_pairs={{0,1},{1,0},{2,3},{3,2},{4,5},{5,4},{6,7},{7,6},{8,9},{9,8},{10,11... | collective-permute-start | bytes 147464 | tf_op jit(solution)/shard_map/ppermute | solution.py:590
  9.3 1.6 %copy-start.3 = (s32[4]{0:T(128)S(1)}, s32[4]{0:T(128)}, u32[]{:S(2)}) copy-start(s32[4]{0:T(128)} %owner.1) | copy-start | bytes 52
  9.3 6.4 %collective-permute-start.4 = (f32[96,128]{1,0:T(8,128)S(1)}, f32[96,128]{1,0:T(8,128)S(1)}, u32[]{:S(2)}, u32[]{:S(2)}) collective-permute-start(f32[96,128]{1,0:T(8,128)S(1)} %get-tuple-element.53.own_b), channel_id=1, source_target_pairs={{0,3},{1,2},{2,1},{3,0},{4,7},{5,6},{6,5},{7,4},{8,11},{9,10},{10,... | collective-permute-start | bytes 147464 | tf_op jit(solution)/shard_map/ppermute | solution.py:589
  11.6 4.0 %collective-permute-start.2 = (f32[4,16,128]{2,1,0:T(8,128)S(1)}, f32[4,16,128]{2,1,0:T(8,128)S(1)}, u32[]{:S(2)}, u32[]{:S(2)}) collective-permute-start(f32[4,16,128]{2,1,0:T(8,128)S(1)} %get-tuple-element.47), channel_id=1, source_target_pairs={{0,8},{4,12},{8,0},{12,4},{16,24},{20,28},{24,16},{28,20},{1,9},{5... | collective-permute-start | bytes 98312 | tf_op jit(solution)/shard_map/ppermute | solution.py:593
  15.9 1.5 %collective-permute-start.5 = (f32[4,8,128]{2,1,0:T(8,128)S(1)}, f32[4,8,128]{2,1,0:T(8,128)S(1)}, u32[]{:S(2)}, u32[]{:S(2)}) collective-permute-start(f32[4,8,128]{2,1,0:T(8,128)S(1)} %get-tuple-element.60.ta), channel_id=1, source_target_pairs={{0,1},{1,0},{2,3},{3,2},{4,5},{5,4},{6,7},{7,6},{8,9},{9,8},{10,11... | collective-permute-start | bytes 49160 | tf_op jit(solution)/shard_map/ppermute | solution.py:639
  16.0 3.2 %collective-permute-start.6 = (f32[4,8,128]{2,1,0:T(8,128)S(1)}, f32[4,8,128]{2,1,0:T(8,128)S(1)}, u32[]{:S(2)}, u32[]{:S(2)}) collective-permute-start(f32[4,8,128]{2,1,0:T(8,128)S(1)} %get-tuple-element.61.tb), channel_id=1, source_target_pairs={{0,3},{1,2},{2,1},{3,0},{4,7},{5,6},{6,5},{7,4},{8,11},{9,10},{10,... | collective-permute-start | bytes 49160 | tf_op jit(solution)/shard_map/ppermute | solution.py:638
  19.2 5.9 %collective-permute-start.7 = (f32[2,16,128]{2,1,0:T(8,128)S(1)}, f32[2,16,128]{2,1,0:T(8,128)S(1)}, u32[]{:S(2)}, u32[]{:S(2)}) collective-permute-start(f32[2,16,128]{2,1,0:T(8,128)S(1)} %get-tuple-element.77), channel_id=1, source_target_pairs={{0,16},{4,20},{8,24},{12,28},{16,0},{20,4},{24,8},{28,12},{1,17},{... | collective-permute-start | bytes 49160 | tf_op jit(solution)/shard_map/ppermute | solution.py:593
  21.4 10.9 %all-to-all-start = ((f32[32,2,128]{2,1,0:T(2,128)}), f32[32,2,128]{2,1,0:T(2,128)S(1)}, u32[]{:S(2)}, u32[]{:S(2)}) async-start(f32[32,2,128]{2,1,0:T(2,128)} %get-tuple-element.80), calls=%async_computation | async-start | bytes 65536 | tf_op jit(solution)/shard_map/all_to_all | solution.py:681
  25.1 3.7 %collective-permute-start.8 = (f32[1,16,128]{2,1,0:T(8,128)S(1)}, f32[1,16,128]{2,1,0:T(8,128)S(1)}, u32[]{:S(2)}, u32[]{:S(2)}) collective-permute-start(f32[1,16,128]{2,1,0:T(8,128)S(1)} %get-tuple-element.82), channel_id=1, source_target_pairs={{0,4},{4,0},{8,12},{12,8},{16,20},{20,16},{24,28},{28,24},{1,5},{5... | collective-permute-start | bytes 24584 | tf_op jit(solution)/shard_map/ppermute | solution.py:593

commit v4 on v3

--- a/solution.py
+++ b/solution.py
@@ -19,6 +19,9 @@
 HALO = 4
 RING = CX + 2 * HALO
 FIELDS = 10
+WIDE = 3
+ROWS_AT = WIDE * 4 * 8
+ROWS = ROWS_AT + (FIELDS - WIDE) * 3 * 8
 PACKS = 3
 CHUNK = 16
 COLS = PACKS * CX
@@ -62,16 +65,32 @@
     for copy in loads:
         copy.wait()
 
-    for f in range(FIELDS):
+    def tile(f, z, end):
+        return F[end, f, z] if f < 9 else Z[end, z].astype(F32)
+
+    for f in range(WIDE):
         for q in range(NZ // 2):
-            tiles = [F[end, f, z] if f < 9 else Z[end, z].astype(F32) for end in range(2) for z in (2 * q, 2 * q + 1)]
-            first = jnp.where(low, tiles[0], roll(tiles[1], 4, 0))
-            last = jnp.where(low, roll(tiles[3], 4, 0), tiles[2])
-            gxa[f * 4 + q] = jnp.where(even_x, last, first)
-            gxb[f * 4 + q] = jnp.where(even_x, first, last)
-
-
-def cols_kernel(vel, stress, zones, S, V, gya, gyb, sems):
+            first = jnp.where(low, tile(f, 2 * q, 0), roll(tile(f, 2 * q + 1, 0), 4, 0))
+            last = jnp.where(low, roll(tile(f, 2 * q + 1, 1), 4, 0), tile(f, 2 * q, 1))
+            at = 8 * (f * 4 + q)
+            gxa[at:at + 8, :] = jnp.where(even_x, last, first)
+            gxb[at:at + 8, :] = jnp.where(even_x, first, last)
+    for f in range(WIDE, FIELDS):
+        for z in range(NZ):
+            first, last = tile(f, z, 0), roll(tile(f, z, 1), 3, 0)
+            at = pl.ds(ROWS_AT + (f - WIDE) * 24 + z, 3, stride=8)
+            gxa[at, :] = jnp.where(even_x, last, first)[0:3]
+            gxb[at, :] = jnp.where(even_x, first, last)[0:3]
+
+
+def own_band(own, p, at, lasts, firsts):
+    inner = (iota(lasts.shape, 1) // 4) % 4 == 1
+    for s in range(4):
+        if 4 * p + s < FIELDS:
+            own[4 * p + s, at, :] = jnp.where(inner, roll(firsts, -4 * s, 1), roll(lasts, 8 - 4 * s, 1))
+
+
+def cols_kernel(vel, stress, zones, S, V, gya, gyb, own, sems):
     even_y = (lax.axis_index("gy") & 1) == 0
     inner = pl.ds(0, CX)
     loads = [
@@ -101,6 +120,7 @@
                 at = 4 * z + s
                 lasts = jnp.where(slot == at, turned, lasts)
                 firsts = jnp.where(slot == (at + 1) % 32, turned, firsts)
+        own_band(own, p, slice(0, CX), lasts, firsts)
         gya[p * CX:(p + 1) * CX, :] = jnp.where(even_y, lasts, firsts)
         gyb[p * CX:(p + 1) * CX, :] = jnp.where(even_y, firsts, lasts)
 
@@ -148,7 +168,9 @@
         kept_out[k] = held[at + step * bit]
 
 
-def ends_kernel(width, got, kept, source, pair, ta, tb):
+def ends_kernel(width, got, kept, source, gya, gyb, made, pair, ta, tb):
+    ta[0:COLS] = gya[...]
+    tb[0:COLS] = gyb[...]
     even_y = (lax.axis_index("gy") & 1) == 0
     mine = ((source[...] ^ lax.axis_index("gx")) & width) == 0
     lane = iota((8, CY), 1)
@@ -165,11 +187,11 @@
                 idx = jnp.where(here, jnp.where(digit < 8, group * CYC, 96) + col, 0)
                 ends = jnp.sum(jnp.where(here, take(tile, idx), 0.0), axis=0, keepdims=True)
                 tiles[k] = jnp.where(sub == 2 * i + s, jnp.broadcast_to(ends, (8, CY)), tiles[k])
-    ta[...] = jnp.where(even_y, tiles[0], tiles[1])
-    tb[...] = jnp.where(even_y, tiles[1], tiles[0])
-
-
-def edges_kernel(width, quad, tca, tcb, own, sent, kept):
+    ta[COLS:COLS + 8] = jnp.where(even_y, tiles[0], tiles[1])
+    tb[COLS:COLS + 8] = jnp.where(even_y, tiles[1], tiles[0])
+
+
+def edges_kernel(width, quad, ca, cb, token, sent, kept):
     even_y = (lax.axis_index("gy") & 1) == 0
     bit = (lax.axis_index("gx") & width) // width
     beside = iota((1, CY), 1) >= 96
@@ -178,7 +200,7 @@
             at = first + step * side
             out[k] = quad[at]
             for s in range(STEPS):
-                a, b = tca[PACKS, pl.ds(2 * at + s, 1), :], tcb[PACKS, pl.ds(2 * at + s, 1), :]
+                a, b = ca[pl.ds(COLS + 2 * at + s, 1), :], cb[pl.ds(COLS + 2 * at + s, 1), :]
                 for j, ends in enumerate((jnp.where(even_y, b, a), jnp.where(even_y, a, b))):
                     put = j * CXC + 6 + s
                     out[k, put:put + 1, :] = jnp.where(beside, ends, out[k, put:put + 1, :])
@@ -190,12 +212,13 @@
     return [spread[k:k + 1, :] for k in range(3)]
 
 
-def material_kernel(zones, zone_tail, table, LAM, MU, BUOY):
-    columns = [jnp.broadcast_to(row, (RING, CY)) for row in spread_table(table)]
+def material_kernel(zones, table, LAM, MU, BUOY, token):
+    token[...] = jnp.zeros(token.shape, F32)
+    columns = [jnp.broadcast_to(row, (CX, CY)) for row in spread_table(table)]
     for z in range(NZ):
-        ids = jnp.concatenate([zones[z], zone_tail[z].astype(jnp.int32)], axis=0)
+        ids = zones[z]
         for k, ref in enumerate((LAM, MU, BUOY)):
-            ref[z] = take(columns[k], ids)
+            ref[z, 0:CX, :] = take(columns[k], ids)
 
 
 XX, XZ, XY, YY, YZ, ZZ = range(6)
@@ -310,14 +333,42 @@
 
 
 def unpack_kernel(
-    S_in, V_in, ra, rb, ends_a, ends_b, ca, cb,
-    S, V, zone_tail, ta, tb,
+    S_in, V_in, LAM_in, MU_in, BUOY_in, own_in, table, ra, rb,
+    S, V, LAM, MU, BUOY, own, ta, tb, zone_tail,
 ):
     even_x = (lax.axis_index("gx") & 1) == 0
     even_y = (lax.axis_index("gy") & 1) == 0
     low = iota((8, CY), 0) < 4
     slot = iota((8, CY), 1) // HALO
     tail = slice(CX, RING)
+    columns = [jnp.broadcast_to(row, (8, CY)) for row in spread_table(table)]
+
+    def place(f, z, rows, at):
+        if f < 6:
+            S[f, z, CX + at:CX + at + rows.shape[0], :] = rows
+        elif f < 9:
+            V[f - 6, z, CX + at:CX + at + rows.shape[0], :] = rows
+        else:
+            zone_tail[z, at:at + rows.shape[0], :] = rows
+
+    for f in range(WIDE):
+        for q in range(NZ // 2):
+            at = slice(8 * (f * 4 + q), 8 * (f * 4 + q) + 8)
+            after = jnp.where(even_x, ra[at], rb[at])
+            before = jnp.where(even_x, rb[at], ra[at])
+            place(f, 2 * q, jnp.where(low, after, before), 0)
+            place(f, 2 * q + 1, roll(jnp.where(low, before, after), 4, 0), 0)
+    for f in range(WIDE, FIELDS):
+        for z in range(NZ):
+            at = pl.ds(ROWS_AT + (f - WIDE) * 24 + z, 3, stride=8)
+            a, b = ra[at, :], rb[at, :]
+            place(f, z, jnp.zeros((8, CY), F32), 0)
+            place(f, z, jnp.where(even_x, a, b), 0)
+            place(f, z, jnp.where(even_x, b, a), 5)
+    for z in range(NZ):
+        ids = zone_tail[z].astype(jnp.int32)
+        for column, ref in zip(columns, (LAM, MU, BUOY)):
+            ref[z, tail, :] = take(column, ids)
     for p in range(PACKS):
         lasts = jnp.zeros((8, CY), F32)
         firsts = jnp.zeros((8, CY), F32)
@@ -325,40 +376,20 @@
             f = 4 * p + s
             if f >= FIELDS:
                 continue
-            for q in range(NZ // 2):
-                k = f * 4 + q
-                after = jnp.where(even_x, ra[k], rb[k])
-                before = jnp.where(even_x, rb[k], ra[k])
-                both = (jnp.where(low, after, before), roll(jnp.where(low, before, after), 4, 0))
-                for z in (2 * q, 2 * q + 1):
-                    rows = both[z % 2]
-                    turned = roll(rows, 16 * z + 4 * s + 4, 1)
-                    at = 4 * z + s
-                    lasts = jnp.where(slot == at, turned, lasts)
-                    firsts = jnp.where(slot == (at + 1) % 32, turned, firsts)
-                    if f < 6:
-                        S[f, z, tail, :] = rows
-                    elif f < 9:
-                        V[f - 6, z, tail, :] = rows
-                    else:
-                        zone_tail[z] = rows
+            for z in range(NZ):
+                rows = S[f, z, tail, :] if f < 6 else V[f - 6, z, tail, :] if f < 9 else zone_tail[z]
+                turned = roll(rows, 16 * z + 4 * s + 4, 1)
+                at = 4 * z + s
+                lasts = jnp.where(slot == at, turned, lasts)
+                firsts = jnp.where(slot == (at + 1) % 32, turned, firsts)
+        own_band(own, p, tail, lasts, firsts)
         ta[p] = jnp.where(even_y, lasts, firsts)
         tb[p] = jnp.where(even_y, firsts, lasts)
-    ta[PACKS] = ends_a[...]
-    tb[PACKS] = ends_b[...]
-
-
-def inner_kernel(S, V_in, MU, BUOY, own_a, own_b, ta, tb, V, own):
-    even_y = (lax.axis_index("gy") & 1) == 0
-    quarter = (iota((RING, CY), 1) // 4) % 4
-    for p in range(PACKS):
-        at = slice(p * CX, (p + 1) * CX)
-        one, two = jnp.concatenate([own_a[at], ta[p]], axis=0), jnp.concatenate([own_b[at], tb[p]], axis=0)
-        last, first = jnp.where(even_y, one, two), jnp.where(even_y, two, one)
-        for s in range(4):
-            if 4 * p + s < FIELDS:
-                own[4 * p + s] = jnp.where(quarter == 1, roll(first, -4 * s, 1), roll(last, 8 - 4 * s, 1))
+
+
+def inner_kernel(S, V_in, MU, BUOY, V, token):
     velocity_planes(range(0, 5), S, V, MU, BUOY, None, None)
+    token[...] = jnp.zeros(token.shape, F32)
 
 
 def cone_kernel(
@@ -553,7 +584,7 @@
     s_ring = shaped(6, NZ, RING, CY)
     v_ring = shaped(3, NZ, RING, CY)
     m_ring = shaped(NZ, RING, CY)
-    rows = shaped(FIELDS * 4, 8, CY)
+    rows = shaped(ROWS, CY)
     cols = shaped(COLS, CY)
     from_hbm = [
         pltpu.with_memory_space_constraint(x, pltpu.HBM)
@@ -577,17 +608,16 @@
     )(*from_hbm)
     rb = lax.ppermute(gxb, "gx", pairs_far(n_gx))
     ra = lax.ppermute(gxa, "gx", pairs_near(n_gx))
-    S, V, gya, gyb = pl.pallas_call(
+    own = shaped(FIELDS, RING, CY)
+    S, V, gya, gyb, own = pl.pallas_call(
         cols_kernel,
-        out_shape=(s_ring, v_ring, cols, cols),
+        out_shape=(s_ring, v_ring, cols, cols, own),
         in_specs=[vmem] * 3,
-        out_specs=(vmem,) * 4,
+        out_specs=(vmem,) * 5,
         scratch_shapes=[pltpu.SemaphoreType.DMA((2,))],
         compiler_params=params,
         name="pack_columns",
     )(velocity, stress, zones)
-    cb = lax.ppermute(gyb, "gy", pairs_far(n_gy))
-    ca = lax.ppermute(gya, "gy", pairs_near(n_gy))
 
     def across(x, width):
         return lax.ppermute(x, "gx", [(i, i ^ width) for i in range(n_gx)])
@@ -616,44 +646,47 @@
             name="trade",
         )(across(sent, width), kept, source)
         width *= 2
-    tile = shaped(8, CY)
-    quad, ends_a, ends_b = pl.pallas_call(
+    LAM, MU, BUOY, made = pl.pallas_call(
+        material_kernel,
+        out_shape=(m_ring,) * 3 + (shaped(8, CY),),
+        in_specs=[vmem] * 2,
+        out_specs=(vmem,) * 4,
+        compiler_params=params,
+        name="materials",
+    )(zones, zone_table)
+    message = shaped(COLS + 8, CY)
+    quad, message_a, message_b = pl.pallas_call(
         functools.partial(ends_kernel, width),
-        out_shape=(shaped(4, CHUNK, CY), tile, tile),
-        in_specs=[vmem] * 3,
+        out_shape=(shaped(4, CHUNK, CY), message, message),
+        in_specs=[vmem] * 5 + [anywhere],
         out_specs=(vmem,) * 3,
         compiler_params=params,
         name="ends",
-    )(across(sent, width), kept, source)
-    ends = shaped(PACKS + 1, 8, CY)
-    S, V, zone_tail, ta, tb = pl.pallas_call(
+    )(across(sent, width), kept, source, gya, gyb, made)
+    cb = lax.ppermute(message_b, "gy", pairs_far(n_gy))
+    ca = lax.ppermute(message_a, "gy", pairs_near(n_gy))
+    ends = shaped(PACKS, 8, CY)
+    S, V, LAM, MU, BUOY, own, ta, tb = pl.pallas_call(
         unpack_kernel,
-        out_shape=(s_ring, v_ring, shaped(NZ, 8, CY), ends, ends),
-        in_specs=[vmem] * 6 + [anywhere] * 2,
-        out_specs=(vmem,) * 5,
-        input_output_aliases={0: 0, 1: 1},
+        out_shape=(s_ring, v_ring, m_ring, m_ring, m_ring, shaped(FIELDS, RING, CY), ends, ends),
+        in_specs=[vmem] * 9,
+        out_specs=(vmem,) * 8,
+        scratch_shapes=[pltpu.VMEM((NZ, 8, CY), F32)],
+        input_output_aliases={k: k for k in range(6)},
         compiler_params=params,
         name="unpack",
-    )(S, V, ra, rb, ends_a, ends_b, ca, cb)
+    )(S, V, LAM, MU, BUOY, own, zone_table, ra, rb)
     tcb = lax.ppermute(tb, "gy", pairs_far(n_gy))
     tca = lax.ppermute(ta, "gy", pairs_near(n_gy))
-    LAM, MU, BUOY = pl.pallas_call(
-        material_kernel,
-        out_shape=(m_ring,) * 3,
-        in_specs=[vmem] * 3,
-        out_specs=(vmem,) * 3,
-        compiler_params=params,
-        name="materials",
-    )(zones, zone_tail, zone_table)
-    V, own = pl.pallas_call(
+    V, token = pl.pallas_call(
         inner_kernel,
-        out_shape=(v_ring, shaped(FIELDS, RING, CY)),
-        in_specs=[vmem] * 8,
+        out_shape=(v_ring, shaped(8, CY)),
+        in_specs=[vmem] * 4,
         out_specs=(vmem,) * 2,
         input_output_aliases={1: 0},
         compiler_params=params,
         name="inner",
-    )(S, V, MU, BUOY, gya, gyb, ta, tb)
+    )(S, V, MU, BUOY)
     two = shaped(2, CHUNK, CY)
     width *= 2
     sent, kept = pl.pallas_call(
@@ -663,7 +696,7 @@
         out_specs=(vmem,) * 2,
         compiler_params=params,
         name="edges",
-    )(quad, tca, tcb, own)
+    )(quad, ca, cb, token)
     band = shaped(3, RING, CY)
     S, V, BF, BM, BV, BW, shares = pl.pallas_call(
         cone_kernel,

time: 33.6 us -> 32.7 us (0.973)
  waiting for transfers between devices: 8.08 us -> 7.17 us
    ppermute x3, waiting for transfers between devices: 4.98 us -> 3.75 us  [across(): return lax.ppermute(x, 'gx', [(i, i ^ width) for i in range(n_gx)])]
    ppermute x2, waiting for transfers between devices: 0.01 us -> 0.71 us  [the longest x1 0.7 us: body(): cb = lax.ppermute(message_b, 'gy', pairs_far(n_gy))]
    ppermute x1, waiting for transfers between devices: 1.76 us -> 1.38 us  [body(): tcb = lax.ppermute(tb, 'gy', pairs_far(n_gy))]
  transfers between devices with their start and end apart: 10 -> 10, of which waited for: 4 -> 5; matrix products, arithmetic and copies ran while one was open for 0% -> 0% of each run, Pallas kernels for 21% -> 23%
where the time goes in v4:
time: 32.7 us; the launch traced here: 32.5 us
  starting transfers between devices  14.5 us (44%)
  Pallas kernels  10.1 us (31%)
  waiting for transfers between devices  7.17 us (22%)
  between operations  0.8 us (2%)
    ppermute x3, waiting for transfers between devices, across(): return lax.ppermute(x, 'gx', [(i, i ^ width) for i in range(n_gx)])  3.75 us
    ppermute x1, starting transfers between devices, body(): rb = lax.ppermute(gxb, 'gx', pairs_far(n_gx))  3.57 us
    all_to_all x1, starting transfers between devices, body(): every = lax.all_to_all(shares, ('gx', 'gy'), 0, 0)  3.37 us
    ppermute x1, starting transfers between devices, body(): ra = lax.ppermute(gxa, 'gx', pairs_near(n_gx))  3 us
    pallas_call x1, Pallas kernels, body(): pl.pallas_call(lower_kernel, out_shape=(s_ring, v_ring, shaped(FIELDS, RI...  2.16 us
    ppermute x3, starting transfers between devices, across(): return lax.ppermute(x, 'gx', [(i, i ^ width) for i in range(n_gx)])  2.1 us
    pallas_call x1, Pallas kernels, body(): pl.pallas_call(cone_kernel, out_shape=(s_ring, v_ring, shaped(FIELDS, RIN...  2.07 us
    ppermute x1, starting transfers between devices, body(): cb = lax.ppermute(message_b, 'gy', pairs_far(n_gy))  1.64 us
  transfers between devices with their start and end apart: 10, of which 5 were waited for; matrix products, arithmetic and copies ran while one was open for 0% of the time, Pallas kernels for 23%

profile of v4, /device:TPU:0, one launch (start us, length us, event | category | flops | bytes accessed | tf_op | source)
XLA Modules:
  0.0 32.5 jit_solution(12868997607981997114)
XLA Ops:
  0.6 0.0 copy-start
  0.6 0.0 copy-start.1
  0.7 0.0 copy-start.2
  0.7 1.4 %pack_rows.1 = (f32[264,128]{1,0:T(8,128)S(1)}, f32[264,128]{1,0:T(8,128)S(1)}, f32[1,2,3,8,256]{4,3,2,1,0:T(8,128)S(1)}, f32[3,16]{1,0:T(4,128)S(1)}, s32[1,1,64]{2,1,0:T(1,128)S(1)}, /*index=5*/s32[1,1,64]{2,1,0:T(1,128)S(1)}) custom-call(f32[3,8,32,128]{3,2,1,0:T(8,128)} %vel.3, f32[6,8,32,128]{3,2,1,0:T(8,128)} %stress.3, s32[8,32,128]{2,1,0:T(8,128)} %zones.5, ...), custom_call_target="tpu_custom_call" | custom-call | tf_op jit(solution)/shard_map/pack_rows/pallas_call | solution.py:593
  2.1 3.0 %collective-permute-start = (f32[264,128]{1,0:T(8,128)S(1)}, f32[264,128]{1,0:T(8,128)S(1)}, u32[]{:S(2)}, u32[]{:S(2)}) collective-permute-start(f32[264,128]{1,0:T(8,128)S(1)} %get-tuple-element.54), channel_id=1, source_target_pairs={{0,4},{4,0},{8,12},{12,8},{16,20},{20,16},{24,28},{28,24},{1,5},{5... | collective-permute-start | bytes 405512 | tf_op jit(solution)/shard_map/ppermute | solution.py:610
  5.1 0.0 copy-start.3
  5.1 3.6 %collective-permute-start.1 = (f32[264,128]{1,0:T(8,128)S(1)}, f32[264,128]{1,0:T(8,128)S(1)}, u32[]{:S(2)}, u32[]{:S(2)}) collective-permute-start(f32[264,128]{1,0:T(8,128)S(1)} %get-tuple-element.55), channel_id=1, source_target_pairs={{0,28},{4,8},{8,4},{12,16},{16,12},{20,24},{24,20},{28,0},{1,29},{... | collective-permute-start | bytes 405512 | tf_op jit(solution)/shard_map/ppermute | solution.py:609
  8.7 0.0 copy-done.3
  8.7 0.7 %slices.1 = (s32[16,128]{1,0:T(8,128)S(1)}, f32[4,16,128]{2,1,0:T(8,128)S(1)}, f32[4,16,128]{2,1,0:T(8,128)S(1)}) custom-call(f32[1,2,3,8,256]{4,3,2,1,0:T(8,128)S(1)} %get-tuple-element.63.R, s32[4]{0:T(128)S(1)} %copy-done.3), custom_call_target="tpu_custom_call" | custom-call | tf_op jit(solution)/shard_map/slices/pallas_call | solution.py:626
  9.3 0.1 collective-permute-start.2
  9.4 0.0 copy-done
  9.4 0.0 copy-done.1
  9.4 0.0 copy-done.2
  9.4 0.8 %pack_columns.1 = (f32[6,8,40,128]{3,2,1,0:T(8,128)S(1)}, f32[3,8,40,128]{3,2,1,0:T(8,128)S(1)}, f32[96,128]{1,0:T(8,128)S(1)}, f32[96,128]{1,0:T(8,128)S(1)}, f32[10,40,128]{2,1,0:T(8,128)S(1)}) custom-call(f32[3,8,32,128]{3,2,1,0:T(8,128)S(1)} %copy-done.1, f32[6,8,32,128]{3,2,1,0:T(8,128)S(1)} %copy-done, s32[8,32,128]{2,1,0:T(8,128)S(1)} %copy-done.2), custom_call_target="tpu_custom_call" | custom-call | tf_op jit(solution)/shard_map/pack_columns/pallas_call | solution.py:612
  10.2 0.4 %materials.1 = (f32[8,40,128]{2,1,0:T(8,128)S(1)}, f32[8,40,128]{2,1,0:T(8,128)S(1)}, f32[8,40,128]{2,1,0:T(8,128)S(1)}, f32[8,128]{1,0:T(8,128)S(1)}) custom-call(s32[8,32,128]{2,1,0:T(8,128)S(1)} %copy-done.2, f32[3,16]{1,0:T(4,128)S(1)} %get-tuple-element.49.table), custom_call_target="tpu_custom_call" | custom-call | tf_op jit(solution)/shard_map/materials/pallas_call | solution.py:649
  10.6 2.7 %collective-permute-done.2.got = f32[4,16,128]{2,1,0:T(8,128)S(1)} collective-permute-done((f32[4,16,128]{2,1,0:T(8,128)S(1)}, f32[4,16,128]{2,1,0:T(8,128)S(1)}, u32[]{:S(2)}, u32[]{:S(2)}) %collective-permute-start.2) | collective-permute-done | bytes 32800 | tf_op jit(solution)/shard_map/ppermute | solution.py:623
  13.3 0.1 ends.1
  13.4 0.1 collective-permute-start.3
  13.5 1.6 %collective-permute-start.4 = (f32[104,128]{1,0:T(8,128)S(1)}, f32[104,128]{1,0:T(8,128)S(1)}, u32[]{:S(2)}, u32[]{:S(2)}) collective-permute-start(f32[104,128]{1,0:T(8,128)S(1)} %get-tuple-element.71), channel_id=1, source_target_pairs={{0,3},{1,2},{2,1},{3,0},{4,7},{5,6},{6,5},{7,4},{8,11},{9,10},{10,... | collective-permute-start | bytes 159752 | tf_op jit(solution)/shard_map/ppermute | solution.py:666
  15.1 0.0 collective-permute-done.ra
  15.1 0.0 collective-permute-done.1.rb
  15.1 0.3 %unpack.1 = (f32[6,8,40,128]{3,2,1,0:T(8,128)S(1)}, f32[3,8,40,128]{3,2,1,0:T(8,128)S(1)}, f32[8,40,128]{2,1,0:T(8,128)S(1)}, f32[8,40,128]{2,1,0:T(8,128)S(1)},...) custom-call(f32[6,8,40,128]{3,2,1,0:T(8,128)S(1)} %get-tuple-element, ...), custom_call_target="tpu_custom_call", output_to_operand_aliasing={{0}: (0, {}), {1}: (1, {}), {2}: (2, {}), {3}: (3, {}), {4}... | custom-call | tf_op jit(solution)/shard_map/unpack/pallas_call | solution.py:669
  15.5 0.1 collective-permute-start.5
  15.6 0.6 %collective-permute-start.6 = (f32[3,8,128]{2,1,0:T(8,128)S(1)}, f32[3,8,128]{2,1,0:T(8,128)S(1)}, u32[]{:S(2)}, u32[]{:S(2)}) collective-permute-start(f32[3,8,128]{2,1,0:T(8,128)S(1)} %get-tuple-element.73), channel_id=1, source_target_pairs={{0,3},{1,2},{2,1},{3,0},{4,7},{5,6},{6,5},{7,4},{8,11},{9,10},{10,... | collective-permute-start | bytes 36872 | tf_op jit(solution)/shard_map/ppermute | solution.py:679
  16.2 0.2 inner.1
  16.4 0.0 collective-permute-done.3.ca
  16.4 0.7 %collective-permute-done.4.cb = f32[104,128]{1,0:T(8,128)S(1)} collective-permute-done((f32[104,128]{1,0:T(8,128)S(1)}, f32[104,128]{1,0:T(8,128)S(1)}, u32[]{:S(2)}, u32[]{:S(2)}) %collective-permute-start.4) | collective-permute-done | bytes 53280 | tf_op jit(solution)/shard_map/ppermute | solution.py:666
  17.1 0.2 collective-permute-start.7
  17.4 0.0 collective-permute-done.5.tca
  17.4 1.4 %collective-permute-done.6.tcb = f32[3,8,128]{2,1,0:T(8,128)S(1)} collective-permute-done((f32[3,8,128]{2,1,0:T(8,128)S(1)}, f32[3,8,128]{2,1,0:T(8,128)S(1)}, u32[]{:S(2)}, u32[]{:S(2)}) %collective-permute-start.6) | collective-permute-done | bytes 12320 | tf_op jit(solution)/shard_map/ppermute | solution.py:679
  18.7 2.1 %cone.1 = (f32[6,8,40,128]{3,2,1,0:T(8,128)S(1)}, f32[3,8,40,128]{3,2,1,0:T(8,128)S(1)}, f32[10,40,128]{2,1,0:T(8,128)S(1)}, f32[3,40,128]{2,1,0:T(8,128)S(1)}, ...) custom-call(f32[6,8,40,128]{3,2,1,0:T(8,128)S(1)} %get-tuple-element, ...), custom_call_target="tpu_custom_call", output_to_operand_aliasing={{0}: (0, {}), {1}: (1, {})} | custom-call | tf_op jit(solution)/shard_map/cone/pallas_call | solution.py:701
  20.8 3.4 %all-to-all-start = ((f32[32,2,128]{2,1,0:T(2,128)}), f32[32,2,128]{2,1,0:T(2,128)S(1)}, u32[]{:S(2)}, u32[]{:S(2)}) async-start(f32[32,2,128]{2,1,0:T(2,128)} %get-tuple-element.90), calls=%async_computation | async-start | bytes 65536 | tf_op jit(solution)/shard_map/all_to_all | solution.py:714
  24.2 0.0 collective-permute-done.7
  24.2 1.8 %collective-permute-start.8 = (f32[1,16,128]{2,1,0:T(8,128)S(1)}, f32[1,16,128]{2,1,0:T(8,128)S(1)}, u32[]{:S(2)}, u32[]{:S(2)}) collective-permute-start(f32[1,16,128]{2,1,0:T(8,128)S(1)} %get-tuple-element.92), channel_id=1, source_target_pairs={{0,4},{4,0},{8,12},{12,8},{16,20},{20,16},{24,28},{28,24},{1,5},{5... | collective-permute-start | bytes 24584 | tf_op jit(solution)/shard_map/ppermute | solution.py:623
  26.1 0.8 %upper.1 = (f32[6,8,40,128]{3,2,1,0:T(8,128)S(1)}, f32[3,8,40,128]{3,2,1,0:T(8,128)S(1)}) custom-call(f32[6,8,40,128]{3,2,1,0:T(8,128)S(1)} %get-tuple-element.76.S_in, f32[3,8,40,128]{3,2,1,0:T(8,128)S(1)} %get-tuple-element.77.V_in, f32[8,40,128]{2,1,0:T(8,128)S(1)} %get-tuple-element.61.LAM, ...), custom_call_target="tpu_custom_call", output_to_operand_aliasing={{0}: (0, {}), {1}: (1, {})} | custom-call | tf_op jit(solution)/shard_map/upper/pallas_call | solution.py:715
  26.9 1.1 %collective-permute-done.8.got = f32[1,16,128]{2,1,0:T(8,128)S(1)} collective-permute-done((f32[1,16,128]{2,1,0:T(8,128)S(1)}, f32[1,16,128]{2,1,0:T(8,128)S(1)}, u32[]{:S(2)}, u32[]{:S(2)}) %collective-permute-start.8) | collective-permute-done | bytes 8224 | tf_op jit(solution)/shard_map/ppermute | solution.py:623
  27.9 2.2 %lower.1 = (f32[6,8,40,128]{3,2,1,0:T(8,128)S(1)}, f32[3,8,40,128]{3,2,1,0:T(8,128)S(1)}, f32[10,40,128]{2,1,0:T(8,128)S(1)}, f32[3,8,32,128]{3,2,1,0:T(8,128)}, f32[6,8,32,128]{3,2,1,0:T(8,128)}) custom-call(f32[6,8,40,128]{3,2,1,0:T(8,128)S(1)} %get-tuple-element.81.S_in, ...), custom_call_target="tpu_custom_call", output_to_operand_aliasing={{0}: (0, {}), {1}: (1, {}), {2}: (5, {})} | custom-call | tf_op jit(solution)/shard_map/lower/pallas_call | solution.py:732
  30.1 1.3 %all-to-all-done.shares = f32[32,2,128]{2,1,0:T(2,128)S(1)} async-done(((f32[32,2,128]{2,1,0:T(2,128)}), f32[32,2,128]{2,1,0:T(2,128)S(1)}, u32[]{:S(2)}, u32[]{:S(2)}) %all-to-all-start) | async-done | bytes 32800 | tf_op jit(solution)/shard_map/all_to_all | solution.py:714
  31.4 1.1 %sum_by_building.1 = f32[2,1024]{1,0:T(2,128)} custom-call(f32[32,2,128]{2,1,0:T(2,128)S(1)} %all-to-all-done.shares), custom_call_target="tpu_custom_call" | custom-call | tf_op jit(solution)/shard_map/sum_by_building/pallas_call | solution.py:724
  (4 shorter events, 0.0 us)
Async XLA Ops:
  0.6 8.8 %copy-start = (f32[6,8,32,128]{3,2,1,0:T(8,128)S(1)}, f32[6,8,32,128]{3,2,1,0:T(8,128)}, u32[]{:S(2)}) copy-start(f32[6,8,32,128]{3,2,1,0:T(8,128)} %stress.3) | copy-start | bytes 2359300
  0.6 8.8 %copy-start.1 = (f32[3,8,32,128]{3,2,1,0:T(8,128)S(1)}, f32[3,8,32,128]{3,2,1,0:T(8,128)}, u32[]{:S(2)}) copy-start(f32[3,8,32,128]{3,2,1,0:T(8,128)} %vel.3) | copy-start | bytes 1179652
  0.7 8.8 %copy-start.2 = (s32[8,32,128]{2,1,0:T(8,128)S(1)}, s32[8,32,128]{2,1,0:T(8,128)}, u32[]{:S(2)}) copy-start(s32[8,32,128]{2,1,0:T(8,128)} %zones.5) | copy-start | bytes 393220
  2.1 13.1 %collective-permute-start = (f32[264,128]{1,0:T(8,128)S(1)}, f32[264,128]{1,0:T(8,128)S(1)}, u32[]{:S(2)}, u32[]{:S(2)}) collective-permute-start(f32[264,128]{1,0:T(8,128)S(1)} %get-tuple-element.54), channel_id=1, source_target_pairs={{0,4},{4,0},{8,12},{12,8},{16,20},{20,16},{24,28},{28,24},{1,5},{5... | collective-permute-start | bytes 405512 | tf_op jit(solution)/shard_map/ppermute | solution.py:610
  5.1 3.6 %copy-start.3 = (s32[4]{0:T(128)S(1)}, s32[4]{0:T(128)}, u32[]{:S(2)}) copy-start(s32[4]{0:T(128)} %owner.1) | copy-start | bytes 52
  5.1 10.1 %collective-permute-start.1 = (f32[264,128]{1,0:T(8,128)S(1)}, f32[264,128]{1,0:T(8,128)S(1)}, u32[]{:S(2)}, u32[]{:S(2)}) collective-permute-start(f32[264,128]{1,0:T(8,128)S(1)} %get-tuple-element.55), channel_id=1, source_target_pairs={{0,28},{4,8},{8,4},{12,16},{16,12},{20,24},{24,20},{28,0},{1,29},{... | collective-permute-start | bytes 405512 | tf_op jit(solution)/shard_map/ppermute | solution.py:609
  9.3 4.0 %collective-permute-start.2 = (f32[4,16,128]{2,1,0:T(8,128)S(1)}, f32[4,16,128]{2,1,0:T(8,128)S(1)}, u32[]{:S(2)}, u32[]{:S(2)}) collective-permute-start(f32[4,16,128]{2,1,0:T(8,128)S(1)} %get-tuple-element.64), channel_id=1, source_target_pairs={{0,8},{4,12},{8,0},{12,4},{16,24},{20,28},{24,16},{28,20},{1,9},{5... | collective-permute-start | bytes 98312 | tf_op jit(solution)/shard_map/ppermute | solution.py:623
  13.4 3.0 %collective-permute-start.3 = (f32[104,128]{1,0:T(8,128)S(1)}, f32[104,128]{1,0:T(8,128)S(1)}, u32[]{:S(2)}, u32[]{:S(2)}) collective-permute-start(f32[104,128]{1,0:T(8,128)S(1)} %get-tuple-element.70), channel_id=1, source_target_pairs={{0,1},{1,0},{2,3},{3,2},{4,5},{5,4},{6,7},{7,6},{8,9},{9,8},{10,11... | collective-permute-start | bytes 159752 | tf_op jit(solution)/shard_map/ppermute | solution.py:667
  13.5 3.6 %collective-permute-start.4 = (f32[104,128]{1,0:T(8,128)S(1)}, f32[104,128]{1,0:T(8,128)S(1)}, u32[]{:S(2)}, u32[]{:S(2)}) collective-permute-start(f32[104,128]{1,0:T(8,128)S(1)} %get-tuple-element.71), channel_id=1, source_target_pairs={{0,3},{1,2},{2,1},{3,0},{4,7},{5,6},{6,5},{7,4},{8,11},{9,10},{10,... | collective-permute-start | bytes 159752 | tf_op jit(solution)/shard_map/ppermute | solution.py:666
  15.5 1.9 %collective-permute-start.5 = (f32[3,8,128]{2,1,0:T(8,128)S(1)}, f32[3,8,128]{2,1,0:T(8,128)S(1)}, u32[]{:S(2)}, u32[]{:S(2)}) collective-permute-start(f32[3,8,128]{2,1,0:T(8,128)S(1)} %get-tuple-element.72), channel_id=1, source_target_pairs={{0,1},{1,0},{2,3},{3,2},{4,5},{5,4},{6,7},{7,6},{8,9},{9,8},{10,11... | collective-permute-start | bytes 36872 | tf_op jit(solution)/shard_map/ppermute | solution.py:680
  15.6 3.1 %collective-permute-start.6 = (f32[3,8,128]{2,1,0:T(8,128)S(1)}, f32[3,8,128]{2,1,0:T(8,128)S(1)}, u32[]{:S(2)}, u32[]{:S(2)}) collective-permute-start(f32[3,8,128]{2,1,0:T(8,128)S(1)} %get-tuple-element.73), channel_id=1, source_target_pairs={{0,3},{1,2},{2,1},{3,0},{4,7},{5,6},{6,5},{7,4},{8,11},{9,10},{10,... | collective-permute-start | bytes 36872 | tf_op jit(solution)/shard_map/ppermute | solution.py:679
  17.1 7.0 %collective-permute-start.7 = (f32[2,16,128]{2,1,0:T(8,128)S(1)}, f32[2,16,128]{2,1,0:T(8,128)S(1)}, u32[]{:S(2)}, u32[]{:S(2)}) collective-permute-start(f32[2,16,128]{2,1,0:T(8,128)S(1)} %get-tuple-element.87), channel_id=1, source_target_pairs={{0,16},{4,20},{8,24},{12,28},{16,0},{20,4},{24,8},{28,12},{1,17},{... | collective-permute-start | bytes 49160 | tf_op jit(solution)/shard_map/ppermute | solution.py:623
  20.8 10.6 %all-to-all-start = ((f32[32,2,128]{2,1,0:T(2,128)}), f32[32,2,128]{2,1,0:T(2,128)S(1)}, u32[]{:S(2)}, u32[]{:S(2)}) async-start(f32[32,2,128]{2,1,0:T(2,128)} %get-tuple-element.90), calls=%async_computation | async-start | bytes 65536 | tf_op jit(solution)/shard_map/all_to_all | solution.py:714
  24.2 3.7 %collective-permute-start.8 = (f32[1,16,128]{2,1,0:T(8,128)S(1)}, f32[1,16,128]{2,1,0:T(8,128)S(1)}, u32[]{:S(2)}, u32[]{:S(2)}) collective-permute-start(f32[1,16,128]{2,1,0:T(8,128)S(1)} %get-tuple-element.92), channel_id=1, source_target_pairs={{0,4},{4,0},{8,12},{12,8},{16,20},{20,16},{24,28},{28,24},{1,5},{5... | collective-permute-start | bytes 24584 | tf_op jit(solution)/shard_map/ppermute | solution.py:623

commit v5 on v4

--- a/solution.py
+++ b/solution.py
@@ -47,8 +47,8 @@
 
 
 def rows_kernel(
-    vel, stress, zones, regional_in, table_in, building_in, block_in,
-    gxa, gxb, regional, table, building, block, F, Z, sems,
+    n_gy, vel, stress, zones, regional_in, table_in, building_in, block_in, owner_in,
+    gxa, gxb, regional, table, building, block, source, F, Z, owner, sems,
 ):
     even_x = (lax.axis_index("gx") & 1) == 0
     low = iota((8, CY), 0) < 4
@@ -58,7 +58,7 @@
         loads.append(pltpu.make_async_copy(stress.at[:, :, rows, :], F.at[end, pl.ds(0, 6)], sems.at[3 * end]))
         loads.append(pltpu.make_async_copy(vel.at[:, :, rows, :], F.at[end, pl.ds(6, 3)], sems.at[3 * end + 1]))
         loads.append(pltpu.make_async_copy(zones.at[:, rows, :], Z.at[end], sems.at[3 * end + 2]))
-    small = ((regional_in, regional), (table_in, table), (building_in, building), (block_in, block))
+    small = ((owner_in, owner), (regional_in, regional), (table_in, table), (building_in, building), (block_in, block))
     loads += [pltpu.make_async_copy(src, dst, sems.at[6 + k]) for k, (src, dst) in enumerate(small)]
     for copy in loads:
         copy.start()
@@ -67,6 +67,12 @@
 
     def tile(f, z, end):
         return F[end, f, z] if f < 9 else Z[end, z].astype(F32)
+
+    gy = lax.axis_index("gy")
+    row = iota((CHUNK, CY), 0)
+    edge = (iota((CHUNK, CY), 1) >= 96) & ((row & 7) >= 6)
+    sides = jnp.where(row < CXC, owner[(gy + n_gy - 1) % n_gy], owner[(gy + 1) % n_gy])
+    source[...] = jnp.where(edge, sides, owner[gy])
 
     for f in range(WIDE):
         for q in range(NZ // 2):
@@ -132,12 +138,7 @@
     return [(4 * (k // 2) + k % 2, 2) for k in range(count // 2)]
 
 
-def slices_kernel(n_gx, n_gy, R, owner, source, sent, kept, slices):
-    gy = lax.axis_index("gy")
-    row = iota((CHUNK, CY), 0)
-    edge = (iota((CHUNK, CY), 1) >= 96) & ((row & 7) >= 6)
-    sides = jnp.where(row < CXC, owner[(gy + n_gy - 1) % n_gy], owner[(gy + 1) % n_gy])
-    source[...] = jnp.where(edge, sides, owner[gy])
+def slices_kernel(n_gx, R, sent, kept, slices):
     part = iota((n_gx, CY), 1) // CYC
     for s in range(STEPS):
         halves = [[R[0, s, c, :, t * CY:(t + 1) * CY] for t in range(2)] for c in range(3)]
@@ -258,29 +259,37 @@
     return {f: jnp.where(lane % 16 == 2, roll(band[f], -10, 1), band[f]) for f in fields}
 
 
-def velocity_planes(planes, S, V, MU, BUOY, band, drm):
+ALL = (XX, XZ, XY, YY, YZ, ZZ)
+FLAT, STEEP = (XX, XY), (XZ, YZ)
+
+
+def moving(planes, first):
+    return [(z, (0, 1) if (z % 2 == 0) == first else (2,)) for z in planes]
+
+
+def every(planes):
+    return [(z, (0, 1, 2)) for z in planes]
+
+
+def velocity_planes(parts, S, V, MU, BUOY, band, drm):
     seam = {XY: None, YY: None, YZ: None} if band is None else seams(band, (XY, YY, YZ))
-    for z in planes:
-        sxy, sxz, syz = S[XY, z], S[XZ, z], S[YZ, z]
-        force = [
-            dx(S[XX, z]) + dy(sxy, seam[XY], z) + dz(S, XZ, z),
-            dx(sxy) + dy(S[YY, z], seam[YY], z) + dz(S, YZ, z),
-            dx(sxz) + dy(syz, seam[YZ], z) + dz(S, ZZ, z),
-        ]
-        if z == NZ - 1:
-            force = [force[c] + (20.0 * MU[z]) * drm(c, 0) for c in range(3)]
-        for c in range(3):
-            V[c, z] = V[c, z] + BUOY[z] * force[c]
-
-
-def velocity_seams(planes, V, BUOY, band):
+    for z, comps in parts:
+        for c in comps:
+            x, y, vert = ((XX, XY, XZ), (XY, YY, YZ), (XZ, YZ, ZZ))[c]
+            force = dx(S[x, z]) + dy(S[y, z], seam[y], z) + dz(S, vert, z)
+            if z == NZ - 1:
+                force = force + (20.0 * MU[z]) * drm(c, 0)
+            V[c, z] = V[c, z] + BUOY[z] * force
+
+
+def velocity_seams(parts, V, BUOY, band):
     lane = iota((RING, CY), 1)
     sign = jnp.where(lane == 0, -1.0, jnp.where(lane == CY - 1, 1.0, 0.0))
     seam = seams(band, (XY, YY, YZ))
-    for z in planes:
+    for z, comps in parts:
         scale = BUOY[z] * sign
-        for c, f in enumerate((XY, YY, YZ)):
-            V[c, z] = V[c, z] + scale * roll(seam[f], -(16 * z + 3), 1)
+        for c in comps:
+            V[c, z] = V[c, z] + scale * roll(seam[(XY, YY, YZ)[c]], -(16 * z + 3), 1)
 
 
 def velocity_band(band, new, BM, drm):
@@ -329,11 +338,8 @@
     new[YZ] = band[YZ] + mu * (band_dz(vy) + band_dy(vz))
 
 
-ALL = (XX, XZ, XY, YY, YZ, ZZ)
-
-
 def unpack_kernel(
-    S_in, V_in, LAM_in, MU_in, BUOY_in, own_in, table, ra, rb,
+    S_in, V_in, LAM_in, MU_in, BUOY_in, own_in, table, rb, ra,
     S, V, LAM, MU, BUOY, own, ta, tb, zone_tail,
 ):
     even_x = (lax.axis_index("gx") & 1) == 0
@@ -388,7 +394,7 @@
 
 
 def inner_kernel(S, V_in, MU, BUOY, V, token):
-    velocity_planes(range(0, 5), S, V, MU, BUOY, None, None)
+    velocity_planes(moving(range(0, 5), True), S, V, MU, BUOY, None, None)
     token[...] = jnp.zeros(token.shape, F32)
 
 
@@ -417,15 +423,15 @@
     for k in range(3):
         BM[k] = take(jnp.broadcast_to(columns[k], (RING, CY)), ids)
 
-    velocity_seams(range(0, 5), V, BUOY, BF)
+    velocity_seams(moving(range(0, 5), True), V, BUOY, BF)
     velocity_band(BF, BW, BM, None)
     for c in range(3):
         BV[c] = BW[6 + c]
     seam = seams(BW, (6, 7, 8))
     for z in range(0, 4):
-        stress_plane(z, seam, S, V, LAM, MU, ALL)
+        stress_plane(z, seam, S, V, LAM, MU, (FLAT, STEEP)[z % 2])
     stress_band(BF, BW, BM)
-    velocity_planes(range(0, 3), S, V, MU, BUOY, BW, None)
+    velocity_planes(moving(range(0, 3), True), S, V, MU, BUOY, BW, None)
     velocity_band(BW, BW, BM, None)
     stress_plane(1, seams(BW, (8,)), S, V, LAM, MU, (XZ, YZ))
 
@@ -448,14 +454,14 @@
 
 
 def upper_kernel(S_in, V_in, LAM, MU, BUOY, BF, BV, BW, S, V):
-    velocity_planes(range(5, 7), S, V, MU, BUOY, BF, None)
+    velocity_planes(moving(range(0, 5), False) + every(range(5, 7)), S, V, MU, BUOY, BF, None)
     seam = {6 + c: value for c, value in seams(BV, range(3)).items()}
-    for z in range(4, 6):
-        stress_plane(z, seam, S, V, LAM, MU, ALL)
-    velocity_planes(range(3, 5), S, V, MU, BUOY, BW, None)
+    for z in range(0, 6):
+        stress_plane(z, seam, S, V, LAM, MU, ALL if z > 3 else (STEEP, FLAT)[z % 2])
+    velocity_planes(moving(range(0, 3), False) + every(range(3, 5)), S, V, MU, BUOY, BW, None)
     seam = seams(BW, (6, 7, 8))
     for z in range(0, 4):
-        stress_plane(z, seam, S, V, LAM, MU, (XX, XY) if z == 1 else ALL)
+        stress_plane(z, seam, S, V, LAM, MU, FLAT if z == 1 else ALL)
 
 
 def lower_kernel(
@@ -502,13 +508,13 @@
     def drm(step):
         return lambda c, k: DRM[step, c, k]
 
-    velocity_planes(range(7, NZ), S, V, MU, BUOY, BF, drm(0))
+    velocity_planes(every(range(7, NZ)), S, V, MU, BUOY, BF, drm(0))
     velocity_band(BF, BF, BM, drm(0))
     seam = seams(BF, (6, 7, 8))
     for z in range(6, NZ):
         stress_plane(z, seam, S, V, LAM, MU, ALL)
     stress_band(BF, BF, BM)
-    velocity_planes(range(5, NZ), S, V, MU, BUOY, BF, drm(1))
+    velocity_planes(every(range(5, NZ)), S, V, MU, BUOY, BF, drm(1))
     velocity_band(BF, BF, BM, drm(1))
     save(V, vel_out, 5, NZ - 5)
     seam = seams(BF, (6, 7, 8))
@@ -588,20 +594,21 @@
     cols = shaped(COLS, CY)
     from_hbm = [
         pltpu.with_memory_space_constraint(x, pltpu.HBM)
-        for x in (velocity, stress, zones, regional, zone_table, building, block)
+        for x in (velocity, stress, zones, regional, zone_table, building, block, owner)
     ]
-    gxa, gxb, regional, zone_table, building, block = pl.pallas_call(
-        rows_kernel,
+    gxa, gxb, regional, zone_table, building, block, source = pl.pallas_call(
+        functools.partial(rows_kernel, n_gy),
         out_shape=(
             rows, rows, whole(regional.shape, F32), whole(zone_table.shape, F32),
-            whole(building.shape, jnp.int32), whole(block.shape, jnp.int32),
+            whole(building.shape, jnp.int32), whole(block.shape, jnp.int32), whole((CHUNK, CY), jnp.int32),
         ),
-        in_specs=[hbm] * 7,
-        out_specs=(vmem,) * 6,
+        in_specs=[hbm] * 8,
+        out_specs=(vmem,) * 7,
         scratch_shapes=[
             pltpu.VMEM((2, 9, NZ, 8, CY), F32),
             pltpu.VMEM((2, NZ, 8, CY), jnp.int32),
-            pltpu.SemaphoreType.DMA((10,)),
+            pltpu.SMEM(owner.shape, jnp.int32),
+            pltpu.SemaphoreType.DMA((11,)),
         ],
         compiler_params=params,
         name="pack_rows",
@@ -623,15 +630,15 @@
         return lax.ppermute(x, "gx", [(i, i ^ width) for i in range(n_gx)])
 
     half = shaped(n_gx // 2, CHUNK, CY)
-    source, sent, kept = pl.pallas_call(
-        functools.partial(slices_kernel, n_gx, n_gy),
-        out_shape=(whole((CHUNK, CY), jnp.int32), half, half),
-        in_specs=[vmem, pl.BlockSpec(memory_space=pltpu.SMEM)],
-        out_specs=(vmem,) * 3,
+    sent, kept = pl.pallas_call(
+        functools.partial(slices_kernel, n_gx),
+        out_shape=(half, half),
+        in_specs=[vmem],
+        out_specs=(vmem,) * 2,
         scratch_shapes=[pltpu.VMEM((n_gx * CHUNK, CY), F32)],
         compiler_params=params,
         name="slices",
-    )(regional, owner)
+    )(regional)
     width = 2
     while 4 * width < n_gx:
         count = sent.shape[0]
@@ -675,7 +682,7 @@
         input_output_aliases={k: k for k in range(6)},
         compiler_params=params,
         name="unpack",
-    )(S, V, LAM, MU, BUOY, own, zone_table, ra, rb)
+    )(S, V, LAM, MU, BUOY, own, zone_table, rb, ra)
     tcb = lax.ppermute(tb, "gy", pairs_far(n_gy))
     tca = lax.ppermute(ta, "gy", pairs_near(n_gy))
     V, token = pl.pallas_call(
@@ -711,7 +718,7 @@
     odd = (gx & 1) != 0
     sent, kept = jnp.where(odd, held[0], held[1])[None], jnp.where(odd, held[1], held[0])[None]
     got = across(sent, 1)
-    every = lax.all_to_all(shares, ("gx", "gy"), 0, 0)
+    gathered = lax.all_to_all(shares, ("gx", "gy"), 0, 0)
     S, V = pl.pallas_call(
         upper_kernel,
         out_shape=(s_ring, v_ring),
@@ -728,7 +735,7 @@
         out_specs=vmem,
         compiler_params=params,
         name="sum_by_building",
-    )(every)
+    )(gathered)
     _, _, _, vel_out, stress_out = pl.pallas_call(
         lower_kernel,
         out_shape=(s_ring, v_ring, shaped(FIELDS, RING, CY), shaped(*velocity.shape), shaped(*stress.shape)),

time: 32.7 us -> 32.3 us (0.988)
  starting transfers between devices: 14.5 us -> 16 us
  waiting for transfers between devices: 7.17 us -> 5.84 us
  Pallas kernels: 10.1 us -> 9.5 us
    ppermute x1, starting transfers between devices: 3 us -> 0.01 us  [body(): ra = lax.ppermute(gxa, 'gx', pairs_near(n_gx))]
    ppermute x1, starting transfers between devices: 3.57 us -> 6.04 us  [body(): rb = lax.ppermute(gxb, 'gx', pairs_far(n_gx))]
    ppermute x1, starting transfers between devices: 0.57 us -> 1.64 us  [body(): tcb = lax.ppermute(tb, 'gy', pairs_far(n_gy))]
    ppermute x1, waiting for transfers between devices: 1.38 us -> 0.56 us  [body(): tcb = lax.ppermute(tb, 'gy', pairs_far(n_gy))]
    ppermute x1, waiting for transfers between devices: 0.7 us -> 0.01 us  [body(): cb = lax.ppermute(message_b, 'gy', pairs_far(n_gy))]
    ppermute x3, starting transfers between devices: 2.1 us -> 2.75 us  [across(): return lax.ppermute(x, 'gx', [(i, i ^ width) for i in range(n_gx)])]
    ppermute x1, waiting for transfers between devices: 0.01 us -> 0.54 us  [body(): ra = lax.ppermute(gxa, 'gx', pairs_near(n_gx))]
    pallas_call x2, Pallas kernels: 2.06 us -> 1.54 us  [the longest x1 1.42 us: body(): pl.pallas_call(functools.partial(rows_kernel, n_gy), out_shape=(rows, row...]
  transfers between devices with their start and end apart: 10 -> 10, of which waited for: 5 -> 5; matrix products, arithmetic and copies ran while one was open for 0% -> 0% of each run, Pallas kernels for 23% -> 22%
where the time goes in v5:
time: 32.3 us; the launch traced here: 32.1 us
  starting transfers between devices  16 us (50%)
  Pallas kernels  9.5 us (29%)
  waiting for transfers between devices  5.84 us (18%)
  between operations  0.79 us (2%)
    ppermute x1, starting transfers between devices, body(): rb = lax.ppermute(gxb, 'gx', pairs_far(n_gx))  6.04 us
    all_to_all x1, starting transfers between devices, body(): gathered = lax.all_to_all(shares, ('gx', 'gy'), 0, 0)  3.76 us
    ppermute x3, waiting for transfers between devices, across(): return lax.ppermute(x, 'gx', [(i, i ^ width) for i in range(n_gx)])  3.41 us
    ppermute x3, starting transfers between devices, across(): return lax.ppermute(x, 'gx', [(i, i ^ width) for i in range(n_gx)])  2.75 us
    pallas_call x1, Pallas kernels, body(): pl.pallas_call(lower_kernel, out_shape=(s_ring, v_ring, shaped(FIELDS, RI...  2.16 us
    pallas_call x1, Pallas kernels, body(): pl.pallas_call(cone_kernel, out_shape=(s_ring, v_ring, shaped(FIELDS, RIN...  1.79 us
    ppermute x1, starting transfers between devices, body(): cb = lax.ppermute(message_b, 'gy', pairs_far(n_gy))  1.64 us
    ppermute x1, starting transfers between devices, body(): tcb = lax.ppermute(tb, 'gy', pairs_far(n_gy))  1.64 us
  transfers between devices with their start and end apart: 10, of which 5 were waited for; matrix products, arithmetic and copies ran while one was open for 0% of the time, Pallas kernels for 22%

profile of v5, /device:TPU:0, one launch (start us, length us, event | category | flops | bytes accessed | tf_op | source)
XLA Modules:
  0.0 32.1 jit_solution(12398970005006204181)
XLA Ops:
  0.6 0.0 copy-start
  0.6 0.0 copy-start.1
  0.7 0.0 copy-start.2
  0.7 1.4 %pack_rows.1 = (f32[264,128]{1,0:T(8,128)S(1)}, f32[264,128]{1,0:T(8,128)S(1)}, f32[1,2,3,8,256]{4,3,2,1,0:T(8,128)S(1)}, f32[3,16]{1,0:T(4,128)S(1)}, s32[1,1,6...) custom-call(f32[3,8,32,128]{3,2,1,0:T(8,128)} %vel.3, f32[6,8,32,128]{3,2,1,0:T(8,128)} %stress.3, ...), custom_call_target="tpu_custom_call" | custom-call | tf_op jit(solution)/shard_map/pack_rows/pallas_call | solution.py:599
  2.1 6.0 %collective-permute-start = (f32[264,128]{1,0:T(8,128)S(1)}, f32[264,128]{1,0:T(8,128)S(1)}, u32[]{:S(2)}, u32[]{:S(2)}) collective-permute-start(f32[264,128]{1,0:T(8,128)S(1)} %get-tuple-element.54), channel_id=1, source_target_pairs={{0,28},{4,8},{8,4},{12,16},{16,12},{20,24},{24,20},{28,0},{1,29},{... | collective-permute-start | bytes 405512 | tf_op jit(solution)/shard_map/ppermute | solution.py:616
  8.1 0.0 collective-permute-start.1
  8.1 0.1 slices.1
  8.3 0.1 collective-permute-start.2
  8.4 0.0 copy-done
  8.4 0.0 copy-done.1
  8.4 0.0 copy-done.2
  8.4 0.8 %pack_columns.1 = (f32[6,8,40,128]{3,2,1,0:T(8,128)S(1)}, f32[3,8,40,128]{3,2,1,0:T(8,128)S(1)}, f32[96,128]{1,0:T(8,128)S(1)}, f32[96,128]{1,0:T(8,128)S(1)}, f32[10,40,128]{2,1,0:T(8,128)S(1)}) custom-call(f32[3,8,32,128]{3,2,1,0:T(8,128)S(1)} %copy-done.1, f32[6,8,32,128]{3,2,1,0:T(8,128)S(1)} %copy-done, s32[8,32,128]{2,1,0:T(8,128)S(1)} %copy-done.2), custom_call_target="tpu_custom_call" | custom-call | tf_op jit(solution)/shard_map/pack_columns/pallas_call | solution.py:619
  9.2 0.4 %materials.1 = (f32[8,40,128]{2,1,0:T(8,128)S(1)}, f32[8,40,128]{2,1,0:T(8,128)S(1)}, f32[8,40,128]{2,1,0:T(8,128)S(1)}, f32[8,128]{1,0:T(8,128)S(1)}) custom-call(s32[8,32,128]{2,1,0:T(8,128)S(1)} %copy-done.2, f32[3,16]{1,0:T(4,128)S(1)} %get-tuple-element.49.table), custom_call_target="tpu_custom_call" | custom-call | tf_op jit(solution)/shard_map/materials/pallas_call | solution.py:656
  9.6 2.6 %collective-permute-done.2.got = f32[4,16,128]{2,1,0:T(8,128)S(1)} collective-permute-done((f32[4,16,128]{2,1,0:T(8,128)S(1)}, f32[4,16,128]{2,1,0:T(8,128)S(1)}, u32[]{:S(2)}, u32[]{:S(2)}) %collective-permute-start.2) | collective-permute-done | bytes 32800 | tf_op jit(solution)/shard_map/ppermute | solution.py:630
  12.2 0.1 ends.1
  12.4 0.1 collective-permute-start.3
  12.4 1.6 %collective-permute-start.4 = (f32[104,128]{1,0:T(8,128)S(1)}, f32[104,128]{1,0:T(8,128)S(1)}, u32[]{:S(2)}, u32[]{:S(2)}) collective-permute-start(f32[104,128]{1,0:T(8,128)S(1)} %get-tuple-element.71), channel_id=1, source_target_pairs={{0,3},{1,2},{2,1},{3,0},{4,7},{5,6},{6,5},{7,4},{8,11},{9,10},{10,... | collective-permute-start | bytes 159752 | tf_op jit(solution)/shard_map/ppermute | solution.py:673
  14.1 0.0 collective-permute-done.rb
  14.1 0.5 %collective-permute-done.1.ra = f32[264,128]{1,0:T(8,128)S(1)} collective-permute-done((f32[264,128]{1,0:T(8,128)S(1)}, f32[264,128]{1,0:T(8,128)S(1)}, u32[]{:S(2)}, u32[]{:S(2)}) %collective-permute-start.1) | collective-permute-done | bytes 135200 | tf_op jit(solution)/shard_map/ppermute | solution.py:617
  14.6 0.3 %unpack.1 = (f32[6,8,40,128]{3,2,1,0:T(8,128)S(1)}, f32[3,8,40,128]{3,2,1,0:T(8,128)S(1)}, f32[8,40,128]{2,1,0:T(8,128)S(1)}, f32[8,40,128]{2,1,0:T(8,128)S(1)},...) custom-call(f32[6,8,40,128]{3,2,1,0:T(8,128)S(1)} %get-tuple-element, ...), custom_call_target="tpu_custom_call", output_to_operand_aliasing={{0}: (0, {}), {1}: (1, {}), {2}: (2, {}), {3}: (3, {}), {4}... | custom-call | tf_op jit(solution)/shard_map/unpack/pallas_call | solution.py:676
  14.9 0.1 collective-permute-start.5
  15.0 1.6 %collective-permute-start.6 = (f32[3,8,128]{2,1,0:T(8,128)S(1)}, f32[3,8,128]{2,1,0:T(8,128)S(1)}, u32[]{:S(2)}, u32[]{:S(2)}) collective-permute-start(f32[3,8,128]{2,1,0:T(8,128)S(1)} %get-tuple-element.73), channel_id=1, source_target_pairs={{0,3},{1,2},{2,1},{3,0},{4,7},{5,6},{6,5},{7,4},{8,11},{9,10},{10,... | collective-permute-start | bytes 36872 | tf_op jit(solution)/shard_map/ppermute | solution.py:686
  16.7 0.2 inner.1
  16.8 0.0 collective-permute-done.3.ca
  16.8 0.0 collective-permute-done.4.cb
  16.9 0.8 %collective-permute-start.7 = (f32[2,16,128]{2,1,0:T(8,128)S(1)}, f32[2,16,128]{2,1,0:T(8,128)S(1)}, u32[]{:S(2)}, u32[]{:S(2)}) collective-permute-start(f32[2,16,128]{2,1,0:T(8,128)S(1)} %get-tuple-element.87), channel_id=1, source_target_pairs={{0,16},{4,20},{8,24},{12,28},{16,0},{20,4},{24,8},{28,12},{1,17},{... | collective-permute-start | bytes 49160 | tf_op jit(solution)/shard_map/ppermute | solution.py:630
  17.7 0.0 collective-permute-done.5.tca
  17.7 0.6 %collective-permute-done.6.tcb = f32[3,8,128]{2,1,0:T(8,128)S(1)} collective-permute-done((f32[3,8,128]{2,1,0:T(8,128)S(1)}, f32[3,8,128]{2,1,0:T(8,128)S(1)}, u32[]{:S(2)}, u32[]{:S(2)}) %collective-permute-start.6) | collective-permute-done | bytes 12320 | tf_op jit(solution)/shard_map/ppermute | solution.py:686
  18.2 1.8 %cone.1 = (f32[6,8,40,128]{3,2,1,0:T(8,128)S(1)}, f32[3,8,40,128]{3,2,1,0:T(8,128)S(1)}, f32[10,40,128]{2,1,0:T(8,128)S(1)}, f32[3,40,128]{2,1,0:T(8,128)S(1)}, ...) custom-call(f32[6,8,40,128]{3,2,1,0:T(8,128)S(1)} %get-tuple-element, ...), custom_call_target="tpu_custom_call", output_to_operand_aliasing={{0}: (0, {}), {1}: (1, {})} | custom-call | tf_op jit(solution)/shard_map/cone/pallas_call | solution.py:708
  20.0 3.8 %all-to-all-start = ((f32[32,2,128]{2,1,0:T(2,128)}), f32[32,2,128]{2,1,0:T(2,128)S(1)}, u32[]{:S(2)}, u32[]{:S(2)}) async-start(f32[32,2,128]{2,1,0:T(2,128)} %get-tuple-element.90), calls=%async_computation | async-start | bytes 65536 | tf_op jit(solution)/shard_map/all_to_all | solution.py:721
  23.8 0.0 collective-permute-done.7
  23.8 1.8 %collective-permute-start.8 = (f32[1,16,128]{2,1,0:T(8,128)S(1)}, f32[1,16,128]{2,1,0:T(8,128)S(1)}, u32[]{:S(2)}, u32[]{:S(2)}) collective-permute-start(f32[1,16,128]{2,1,0:T(8,128)S(1)} %get-tuple-element.92), channel_id=1, source_target_pairs={{0,4},{4,0},{8,12},{12,8},{16,20},{20,16},{24,28},{28,24},{1,5},{5... | collective-permute-start | bytes 24584 | tf_op jit(solution)/shard_map/ppermute | solution.py:630
  25.6 1.1 %upper.1 = (f32[6,8,40,128]{3,2,1,0:T(8,128)S(1)}, f32[3,8,40,128]{3,2,1,0:T(8,128)S(1)}) custom-call(f32[6,8,40,128]{3,2,1,0:T(8,128)S(1)} %get-tuple-element.76.S_in, f32[3,8,40,128]{3,2,1,0:T(8,128)S(1)} %get-tuple-element.77.V_in, f32[8,40,128]{2,1,0:T(8,128)S(1)} %get-tuple-element.61.LAM, ...), custom_call_target="tpu_custom_call", output_to_operand_aliasing={{0}: (0, {}), {1}: (1, {})} | custom-call | tf_op jit(solution)/shard_map/upper/pallas_call | solution.py:722
  26.7 0.8 %collective-permute-done.8.got = f32[1,16,128]{2,1,0:T(8,128)S(1)} collective-permute-done((f32[1,16,128]{2,1,0:T(8,128)S(1)}, f32[1,16,128]{2,1,0:T(8,128)S(1)}, u32[]{:S(2)}, u32[]{:S(2)}) %collective-permute-start.8) | collective-permute-done | bytes 8224 | tf_op jit(solution)/shard_map/ppermute | solution.py:630
  27.5 2.2 %lower.1 = (f32[6,8,40,128]{3,2,1,0:T(8,128)S(1)}, f32[3,8,40,128]{3,2,1,0:T(8,128)S(1)}, f32[10,40,128]{2,1,0:T(8,128)S(1)}, f32[3,8,32,128]{3,2,1,0:T(8,128)}, f32[6,8,32,128]{3,2,1,0:T(8,128)}) custom-call(f32[6,8,40,128]{3,2,1,0:T(8,128)S(1)} %get-tuple-element.81.S_in, ...), custom_call_target="tpu_custom_call", output_to_operand_aliasing={{0}: (0, {}), {1}: (1, {}), {2}: (5, {})} | custom-call | tf_op jit(solution)/shard_map/lower/pallas_call | solution.py:739
  29.7 1.3 %all-to-all-done.shares = f32[32,2,128]{2,1,0:T(2,128)S(1)} async-done(((f32[32,2,128]{2,1,0:T(2,128)}), f32[32,2,128]{2,1,0:T(2,128)S(1)}, u32[]{:S(2)}, u32[]{:S(2)}) %all-to-all-start) | async-done | bytes 32800 | tf_op jit(solution)/shard_map/all_to_all | solution.py:721
  31.0 1.1 %sum_by_building.1 = f32[2,1024]{1,0:T(2,128)} custom-call(f32[32,2,128]{2,1,0:T(2,128)S(1)} %all-to-all-done.shares), custom_call_target="tpu_custom_call" | custom-call | tf_op jit(solution)/shard_map/sum_by_building/pallas_call | solution.py:731
  (4 shorter events, 0.0 us)
Async XLA Ops:
  0.6 7.8 %copy-start = (f32[6,8,32,128]{3,2,1,0:T(8,128)S(1)}, f32[6,8,32,128]{3,2,1,0:T(8,128)}, u32[]{:S(2)}) copy-start(f32[6,8,32,128]{3,2,1,0:T(8,128)} %stress.3) | copy-start | bytes 2359300
  0.6 7.8 %copy-start.1 = (f32[3,8,32,128]{3,2,1,0:T(8,128)S(1)}, f32[3,8,32,128]{3,2,1,0:T(8,128)}, u32[]{:S(2)}) copy-start(f32[3,8,32,128]{3,2,1,0:T(8,128)} %vel.3) | copy-start | bytes 1179652
  0.7 7.8 %copy-start.2 = (s32[8,32,128]{2,1,0:T(8,128)S(1)}, s32[8,32,128]{2,1,0:T(8,128)}, u32[]{:S(2)}) copy-start(s32[8,32,128]{2,1,0:T(8,128)} %zones.5) | copy-start | bytes 393220
  2.1 12.0 %collective-permute-start = (f32[264,128]{1,0:T(8,128)S(1)}, f32[264,128]{1,0:T(8,128)S(1)}, u32[]{:S(2)}, u32[]{:S(2)}) collective-permute-start(f32[264,128]{1,0:T(8,128)S(1)} %get-tuple-element.54), channel_id=1, source_target_pairs={{0,28},{4,8},{8,4},{12,16},{16,12},{20,24},{24,20},{28,0},{1,29},{... | collective-permute-start | bytes 405512 | tf_op jit(solution)/shard_map/ppermute | solution.py:616
  8.1 6.5 %collective-permute-start.1 = (f32[264,128]{1,0:T(8,128)S(1)}, f32[264,128]{1,0:T(8,128)S(1)}, u32[]{:S(2)}, u32[]{:S(2)}) collective-permute-start(f32[264,128]{1,0:T(8,128)S(1)} %get-tuple-element.55), channel_id=1, source_target_pairs={{0,4},{4,0},{8,12},{12,8},{16,20},{20,16},{24,28},{28,24},{1,5},{5... | collective-permute-start | bytes 405512 | tf_op jit(solution)/shard_map/ppermute | solution.py:617
  8.3 4.0 %collective-permute-start.2 = (f32[4,16,128]{2,1,0:T(8,128)S(1)}, f32[4,16,128]{2,1,0:T(8,128)S(1)}, u32[]{:S(2)}, u32[]{:S(2)}) collective-permute-start(f32[4,16,128]{2,1,0:T(8,128)S(1)} %get-tuple-element.64), channel_id=1, source_target_pairs={{0,8},{4,12},{8,0},{12,4},{16,24},{20,28},{24,16},{28,20},{1,9},{5... | collective-permute-start | bytes 98312 | tf_op jit(solution)/shard_map/ppermute | solution.py:630
  12.4 4.5 %collective-permute-start.3 = (f32[104,128]{1,0:T(8,128)S(1)}, f32[104,128]{1,0:T(8,128)S(1)}, u32[]{:S(2)}, u32[]{:S(2)}) collective-permute-start(f32[104,128]{1,0:T(8,128)S(1)} %get-tuple-element.70), channel_id=1, source_target_pairs={{0,1},{1,0},{2,3},{3,2},{4,5},{5,4},{6,7},{7,6},{8,9},{9,8},{10,11... | collective-permute-start | bytes 159752 | tf_op jit(solution)/shard_map/ppermute | solution.py:674
  12.4 4.4 %collective-permute-start.4 = (f32[104,128]{1,0:T(8,128)S(1)}, f32[104,128]{1,0:T(8,128)S(1)}, u32[]{:S(2)}, u32[]{:S(2)}) collective-permute-start(f32[104,128]{1,0:T(8,128)S(1)} %get-tuple-element.71), channel_id=1, source_target_pairs={{0,3},{1,2},{2,1},{3,0},{4,7},{5,6},{6,5},{7,4},{8,11},{9,10},{10,... | collective-permute-start | bytes 159752 | tf_op jit(solution)/shard_map/ppermute | solution.py:673
  14.9 2.7 %collective-permute-start.5 = (f32[3,8,128]{2,1,0:T(8,128)S(1)}, f32[3,8,128]{2,1,0:T(8,128)S(1)}, u32[]{:S(2)}, u32[]{:S(2)}) collective-permute-start(f32[3,8,128]{2,1,0:T(8,128)S(1)} %get-tuple-element.72), channel_id=1, source_target_pairs={{0,1},{1,0},{2,3},{3,2},{4,5},{5,4},{6,7},{7,6},{8,9},{9,8},{10,11... | collective-permute-start | bytes 36872 | tf_op jit(solution)/shard_map/ppermute | solution.py:687
  15.0 3.2 %collective-permute-start.6 = (f32[3,8,128]{2,1,0:T(8,128)S(1)}, f32[3,8,128]{2,1,0:T(8,128)S(1)}, u32[]{:S(2)}, u32[]{:S(2)}) collective-permute-start(f32[3,8,128]{2,1,0:T(8,128)S(1)} %get-tuple-element.73), channel_id=1, source_target_pairs={{0,3},{1,2},{2,1},{3,0},{4,7},{5,6},{6,5},{7,4},{8,11},{9,10},{10,... | collective-permute-start | bytes 36872 | tf_op jit(solution)/shard_map/ppermute | solution.py:686
  16.9 6.9 %collective-permute-start.7 = (f32[2,16,128]{2,1,0:T(8,128)S(1)}, f32[2,16,128]{2,1,0:T(8,128)S(1)}, u32[]{:S(2)}, u32[]{:S(2)}) collective-permute-start(f32[2,16,128]{2,1,0:T(8,128)S(1)} %get-tuple-element.87), channel_id=1, source_target_pairs={{0,16},{4,20},{8,24},{12,28},{16,0},{20,4},{24,8},{28,12},{1,17},{... | collective-permute-start | bytes 49160 | tf_op jit(solution)/shard_map/ppermute | solution.py:630
  20.0 11.0 %all-to-all-start = ((f32[32,2,128]{2,1,0:T(2,128)}), f32[32,2,128]{2,1,0:T(2,128)S(1)}, u32[]{:S(2)}, u32[]{:S(2)}) async-start(f32[32,2,128]{2,1,0:T(2,128)} %get-tuple-element.90), calls=%async_computation | async-start | bytes 65536 | tf_op jit(solution)/shard_map/all_to_all | solution.py:721
  23.8 3.7 %collective-permute-start.8 = (f32[1,16,128]{2,1,0:T(8,128)S(1)}, f32[1,16,128]{2,1,0:T(8,128)S(1)}, u32[]{:S(2)}, u32[]{:S(2)}) collective-permute-start(f32[1,16,128]{2,1,0:T(8,128)S(1)} %get-tuple-element.92), channel_id=1, source_target_pairs={{0,4},{4,0},{8,12},{12,8},{16,20},{20,16},{24,28},{28,24},{1,5},{5... | collective-permute-start | bytes 24584 | tf_op jit(solution)/shard_map/ppermute | solution.py:630

commit v6 on v5

--- a/solution.py
+++ b/solution.py
@@ -53,11 +53,11 @@
     even_x = (lax.axis_index("gx") & 1) == 0
     low = iota((8, CY), 0) < 4
     loads = []
-    for end, at in enumerate((0, CX - 8)):
-        rows = pl.ds(at, 8)
-        loads.append(pltpu.make_async_copy(stress.at[:, :, rows, :], F.at[end, pl.ds(0, 6)], sems.at[3 * end]))
-        loads.append(pltpu.make_async_copy(vel.at[:, :, rows, :], F.at[end, pl.ds(6, 3)], sems.at[3 * end + 1]))
-        loads.append(pltpu.make_async_copy(zones.at[:, rows, :], Z.at[end], sems.at[3 * end + 2]))
+    for end, at in enumerate((0, CX - HALO)):
+        rows, to = pl.ds(at, HALO), pl.ds(HALO * end, HALO)
+        loads.append(pltpu.make_async_copy(stress.at[:, :, rows, :], F.at[end, pl.ds(0, 6), :, to], sems.at[3 * end]))
+        loads.append(pltpu.make_async_copy(vel.at[:, :, rows, :], F.at[end, pl.ds(6, 3), :, to], sems.at[3 * end + 1]))
+        loads.append(pltpu.make_async_copy(zones.at[:, rows, :], Z.at[end, :, to], sems.at[3 * end + 2]))
     small = ((owner_in, owner), (regional_in, regional), (table_in, table), (building_in, building), (block_in, block))
     loads += [pltpu.make_async_copy(src, dst, sems.at[6 + k]) for k, (src, dst) in enumerate(small)]
     for copy in loads:
@@ -192,8 +192,27 @@
     tb[COLS:COLS + 8] = jnp.where(even_y, tiles[1], tiles[0])
 
 
-def edges_kernel(width, quad, ca, cb, token, sent, kept):
+def band_rows(BF, BM, own, table, left, right, p, at):
+    quarter = (iota(left.shape, 1) // 4) % 4
+    for s in range(4):
+        f = 4 * p + s
+        if f < FIELDS:
+            BF[f, at, :] = jnp.where(
+                quarter == 0, roll(left, -4 * s, 1),
+                jnp.where(quarter == 3, roll(right, 8 - 4 * s, 1), own[f, at, :]),
+            )
+        if f == FIELDS - 1:
+            ids = BF[f, at, :].astype(jnp.int32)
+            for k, column in enumerate(spread_table(table)):
+                BM[k, at, :] = take(jnp.broadcast_to(column, left.shape), ids)
+
+
+def edges_kernel(width, quad, cb, ca, token, own, table, sent, kept, BF, BM):
     even_y = (lax.axis_index("gy") & 1) == 0
+    for p in range(PACKS):
+        at = slice(p * CX, (p + 1) * CX)
+        left, right = jnp.where(even_y, cb[at], ca[at]), jnp.where(even_y, ca[at], cb[at])
+        band_rows(BF, BM, own, table, left, right, p, slice(0, CX))
     bit = (lax.axis_index("gx") & width) // width
     beside = iota((1, CY), 1) >= 96
     for k, (first, step) in enumerate(split(4)):
@@ -399,29 +418,15 @@
 
 
 def cone_kernel(
-    S_in, V_in, LAM, MU, BUOY, table, own, ca, cb, tca, tcb, building, block,
+    S_in, V_in, LAM, MU, BUOY, BF_in, BM_in, table, own, tcb, tca, building, block,
     S, V, BF, BM, BV, BW, shares,
 ):
     even_y = (lax.axis_index("gy") & 1) == 0
     lane8 = iota((8, CY), 1)
     sub8 = iota((8, CY), 0)
-    quarter = (iota((RING, CY), 1) // 4) % 4
-    columns = spread_table(table)
-
     for p in range(PACKS):
-        at = slice(p * CX, (p + 1) * CX)
-        one, two = jnp.concatenate([ca[at], tca[p]], axis=0), jnp.concatenate([cb[at], tcb[p]], axis=0)
-        from_right, from_left = jnp.where(even_y, one, two), jnp.where(even_y, two, one)
-        for s in range(4):
-            f = 4 * p + s
-            if f < FIELDS:
-                BF[f] = jnp.where(
-                    quarter == 0, roll(from_left, -4 * s, 1),
-                    jnp.where(quarter == 3, roll(from_right, 8 - 4 * s, 1), own[f]),
-                )
-    ids = BF[9].astype(jnp.int32)
-    for k in range(3):
-        BM[k] = take(jnp.broadcast_to(columns[k], (RING, CY)), ids)
+        left, right = jnp.where(even_y, tcb[p], tca[p]), jnp.where(even_y, tca[p], tcb[p])
+        band_rows(BF, BM, own, table, left, right, p, slice(CX, RING))
 
     velocity_seams(moving(range(0, 5), True), V, BUOY, BF)
     velocity_band(BF, BW, BM, None)
@@ -527,32 +532,32 @@
 
 def sum_kernel(n, shares, out):
     half = n // 2
+    n_high = BUILDINGS // CY
     low = iota((half, CY), 1) < FP_DEV
     values = shares[:, 0, :]
     names = shares[:, 1, :].astype(jnp.int32)
-    entry = [
+    names = jnp.where(low, names[:half], names[half:])
+    high, names = names // CY, names % CY
+    pieces = []
+    for rest in (
         jnp.where(low, values[:half], roll(values[half:], FP_DEV, 1)),
         jnp.where(low, roll(values[:half], FP_DEV, 1), values[half:]),
-    ]
-    names = jnp.where(low, names[:half], names[half:])
-    high = names // CY
-    names = names % CY
-    n_high = BUILDINGS // CY
+    ):
+        for _ in range(3):
+            piece = rest.astype(jnp.bfloat16).astype(F32)
+            rest = rest - piece
+            pieces.append(piece)
     rows = iota((n_high, CY), 0)
     wanted = iota((CY, CY), 0)
-    acc = jnp.zeros((6 * n_high, CY), F32)
+    left, hot = [], []
     for k in range(half):
-        hot = (jnp.broadcast_to(names[k:k + 1], (CY, CY)) == wanted).astype(F32).astype(jnp.bfloat16)
         here = jnp.broadcast_to(high[k:k + 1], (n_high, CY)) == rows
-        left = []
-        for c in range(2):
-            rest = jnp.where(here, jnp.broadcast_to(entry[c][k:k + 1], (n_high, CY)), 0.0)
-            for _ in range(3):
-                piece = rest.astype(jnp.bfloat16)
-                rest = rest - piece.astype(F32)
-                left.append(piece.astype(F32))
-        left = jnp.concatenate(left, axis=0).astype(jnp.bfloat16)
-        acc = acc + lax.dot_general(left, hot, (((1,), (1,)), ((), ())), preferred_element_type=F32)
+        parts = [jnp.where(here, jnp.broadcast_to(piece[k:k + 1], (n_high, CY)), 0.0) for piece in pieces]
+        left.append(jnp.concatenate(parts, axis=0).astype(jnp.bfloat16))
+        hot.append((jnp.broadcast_to(names[k:k + 1], (CY, CY)) == wanted).astype(F32).astype(jnp.bfloat16))
+    acc = lax.dot_general(
+        jnp.concatenate(left, axis=1), jnp.concatenate(hot, axis=1), (((1,), (1,)), ((), ())), preferred_element_type=F32,
+    )
     sums = []
     for c in range(2):
         base = 3 * c * n_high
@@ -695,25 +700,25 @@
         name="inner",
     )(S, V, MU, BUOY)
     two = shaped(2, CHUNK, CY)
+    band = shaped(3, RING, CY)
     width *= 2
-    sent, kept = pl.pallas_call(
+    sent, kept, BF, BM = pl.pallas_call(
         functools.partial(edges_kernel, width),
-        out_shape=(two, two),
-        in_specs=[vmem] * 3 + [anywhere],
-        out_specs=(vmem,) * 2,
+        out_shape=(two, two, shaped(FIELDS, RING, CY), band),
+        in_specs=[vmem] * 3 + [anywhere] + [vmem] * 2,
+        out_specs=(vmem,) * 4,
         compiler_params=params,
         name="edges",
-    )(quad, ca, cb, token)
-    band = shaped(3, RING, CY)
+    )(quad, cb, ca, token, own, zone_table)
     S, V, BF, BM, BV, BW, shares = pl.pallas_call(
         cone_kernel,
         out_shape=(s_ring, v_ring, shaped(FIELDS, RING, CY), band, band, shaped(9, RING, CY), shaped(n, 2, CY)),
         in_specs=[vmem] * 13,
         out_specs=(vmem,) * 7,
-        input_output_aliases={0: 0, 1: 1},
+        input_output_aliases={0: 0, 1: 1, 5: 2, 6: 3},
         compiler_params=params,
         name="cone",
-    )(S, V, LAM, MU, BUOY, zone_table, own, ca, cb, tca, tcb, building, block)
+    )(S, V, LAM, MU, BUOY, BF, BM, zone_table, own, tcb, tca, building, block)
     held = jnp.where(((source ^ gx) & width) == 0, kept, across(sent, width))
     odd = (gx & 1) != 0
     sent, kept = jnp.where(odd, held[0], held[1])[None], jnp.where(odd, held[1], held[0])[None]

time: 32.3 us -> 31.8 us (0.985)
    ppermute x1, starting transfers between devices: 1.64 us -> 0.07 us  [body(): cb = lax.ppermute(message_b, 'gy', pairs_far(n_gy))]
    ppermute x1, starting transfers between devices: 0.07 us -> 1.62 us  [body(): ca = lax.ppermute(message_a, 'gy', pairs_near(n_gy))]
    ppermute x1, starting transfers between devices: 1.64 us -> 0.87 us  [body(): tcb = lax.ppermute(tb, 'gy', pairs_far(n_gy))]
    ppermute x1, starting transfers between devices: 0.07 us -> 0.83 us  [body(): tca = lax.ppermute(ta, 'gy', pairs_near(n_gy))]
where the time goes in v6:
time: 31.8 us; the launch traced here: 31.6 us
  starting transfers between devices  16 us (50%)
  Pallas kernels  9.19 us (29%)
  waiting for transfers between devices  5.67 us (18%)
  between operations  0.78 us (2%)
    ppermute x1, starting transfers between devices, body(): rb = lax.ppermute(gxb, 'gx', pairs_far(n_gx))  6.04 us
    all_to_all x1, starting transfers between devices, body(): gathered = lax.all_to_all(shares, ('gx', 'gy'), 0, 0)  3.77 us
    ppermute x3, waiting for transfers between devices, across(): return lax.ppermute(x, 'gx', [(i, i ^ width) for i in range(n_gx)])  3.41 us
    ppermute x3, starting transfers between devices, across(): return lax.ppermute(x, 'gx', [(i, i ^ width) for i in range(n_gx)])  2.75 us
    pallas_call x1, Pallas kernels, body(): pl.pallas_call(lower_kernel, out_shape=(s_ring, v_ring, shaped(FIELDS, RI...  2.16 us
    ppermute x1, starting transfers between devices, body(): ca = lax.ppermute(message_a, 'gy', pairs_near(n_gy))  1.62 us
    pallas_call x1, Pallas kernels, body(): pl.pallas_call(cone_kernel, out_shape=(s_ring, v_ring, shaped(FIELDS, RIN...  1.61 us
    all_to_all x1, waiting for transfers between devices, body(): gathered = lax.all_to_all(shares, ('gx', 'gy'), 0, 0)  1.33 us
  transfers between devices with their start and end apart: 10, of which 5 were waited for; matrix products, arithmetic and copies ran while one was open for 0% of the time, Pallas kernels for 22%

profile of v6, /device:TPU:0, one launch (start us, length us, event | category | flops | bytes accessed | tf_op | source)
XLA Modules:
  0.0 31.6 jit_solution(11220232271411919024)
XLA Ops:
  0.6 0.0 copy-start
  0.6 0.0 copy-start.1
  0.7 0.0 copy-start.2
  0.7 1.3 %pack_rows.1 = (f32[264,128]{1,0:T(8,128)S(1)}, f32[264,128]{1,0:T(8,128)S(1)}, f32[1,2,3,8,256]{4,3,2,1,0:T(8,128)S(1)}, f32[3,16]{1,0:T(4,128)S(1)}, s32[1,1,6...) custom-call(f32[3,8,32,128]{3,2,1,0:T(8,128)} %vel.3, f32[6,8,32,128]{3,2,1,0:T(8,128)} %stress.3, ...), custom_call_target="tpu_custom_call" | custom-call | tf_op jit(solution)/shard_map/pack_rows/pallas_call | solution.py:604
  1.9 6.0 %collective-permute-start = (f32[264,128]{1,0:T(8,128)S(1)}, f32[264,128]{1,0:T(8,128)S(1)}, u32[]{:S(2)}, u32[]{:S(2)}) collective-permute-start(f32[264,128]{1,0:T(8,128)S(1)} %get-tuple-element.56), channel_id=1, source_target_pairs={{0,28},{4,8},{8,4},{12,16},{16,12},{20,24},{24,20},{28,0},{1,29},{... | collective-permute-start | bytes 405512 | tf_op jit(solution)/shard_map/ppermute | solution.py:621
  8.0 0.0 collective-permute-start.1
  8.0 0.1 slices.1
  8.1 0.1 collective-permute-start.2
  8.2 0.0 copy-done
  8.2 0.0 copy-done.1
  8.3 0.0 copy-done.2
  8.3 0.8 %pack_columns.1 = (f32[6,8,40,128]{3,2,1,0:T(8,128)S(1)}, f32[3,8,40,128]{3,2,1,0:T(8,128)S(1)}, f32[96,128]{1,0:T(8,128)S(1)}, f32[96,128]{1,0:T(8,128)S(1)}, f32[10,40,128]{2,1,0:T(8,128)S(1)}) custom-call(f32[3,8,32,128]{3,2,1,0:T(8,128)S(1)} %copy-done.1, f32[6,8,32,128]{3,2,1,0:T(8,128)S(1)} %copy-done, s32[8,32,128]{2,1,0:T(8,128)S(1)} %copy-done.2), custom_call_target="tpu_custom_call" | custom-call | tf_op jit(solution)/shard_map/pack_columns/pallas_call | solution.py:624
  9.1 0.4 %materials.1 = (f32[8,40,128]{2,1,0:T(8,128)S(1)}, f32[8,40,128]{2,1,0:T(8,128)S(1)}, f32[8,40,128]{2,1,0:T(8,128)S(1)}, f32[8,128]{1,0:T(8,128)S(1)}) custom-call(s32[8,32,128]{2,1,0:T(8,128)S(1)} %copy-done.2, f32[3,16]{1,0:T(4,128)S(1)} %get-tuple-element.51.table), custom_call_target="tpu_custom_call" | custom-call | tf_op jit(solution)/shard_map/materials/pallas_call | solution.py:661
  9.5 2.6 %collective-permute-done.2.got = f32[4,16,128]{2,1,0:T(8,128)S(1)} collective-permute-done((f32[4,16,128]{2,1,0:T(8,128)S(1)}, f32[4,16,128]{2,1,0:T(8,128)S(1)}, u32[]{:S(2)}, u32[]{:S(2)}) %collective-permute-start.2) | collective-permute-done | bytes 32800 | tf_op jit(solution)/shard_map/ppermute | solution.py:635
  12.1 0.1 ends.1
  12.2 0.1 collective-permute-start.3
  12.3 1.6 %collective-permute-start.4 = (f32[104,128]{1,0:T(8,128)S(1)}, f32[104,128]{1,0:T(8,128)S(1)}, u32[]{:S(2)}, u32[]{:S(2)}) collective-permute-start(f32[104,128]{1,0:T(8,128)S(1)} %get-tuple-element.73), channel_id=1, source_target_pairs={{0,1},{1,0},{2,3},{3,2},{4,5},{5,4},{6,7},{7,6},{8,9},{9,8},{10,11... | collective-permute-start | bytes 159752 | tf_op jit(solution)/shard_map/ppermute | solution.py:679
  13.9 0.0 collective-permute-done.rb
  13.9 0.6 %collective-permute-done.1.ra = f32[264,128]{1,0:T(8,128)S(1)} collective-permute-done((f32[264,128]{1,0:T(8,128)S(1)}, f32[264,128]{1,0:T(8,128)S(1)}, u32[]{:S(2)}, u32[]{:S(2)}) %collective-permute-start.1) | collective-permute-done | bytes 135200 | tf_op jit(solution)/shard_map/ppermute | solution.py:622
  14.5 0.3 %unpack.1 = (f32[6,8,40,128]{3,2,1,0:T(8,128)S(1)}, f32[3,8,40,128]{3,2,1,0:T(8,128)S(1)}, f32[8,40,128]{2,1,0:T(8,128)S(1)}, f32[8,40,128]{2,1,0:T(8,128)S(1)},...) custom-call(f32[6,8,40,128]{3,2,1,0:T(8,128)S(1)} %get-tuple-element, ...), custom_call_target="tpu_custom_call", output_to_operand_aliasing={{0}: (0, {}), {1}: (1, {}), {2}: (2, {}), {3}: (3, {}), {4}... | custom-call | tf_op jit(solution)/shard_map/unpack/pallas_call | solution.py:681
  14.8 0.9 %collective-permute-start.5 = (f32[3,8,128]{2,1,0:T(8,128)S(1)}, f32[3,8,128]{2,1,0:T(8,128)S(1)}, u32[]{:S(2)}, u32[]{:S(2)}) collective-permute-start(f32[3,8,128]{2,1,0:T(8,128)S(1)} %get-tuple-element.78), channel_id=1, source_target_pairs={{0,3},{1,2},{2,1},{3,0},{4,7},{5,6},{6,5},{7,4},{8,11},{9,10},{10,... | collective-permute-start | bytes 36872 | tf_op jit(solution)/shard_map/ppermute | solution.py:691
  15.7 0.8 %collective-permute-start.6 = (f32[3,8,128]{2,1,0:T(8,128)S(1)}, f32[3,8,128]{2,1,0:T(8,128)S(1)}, u32[]{:S(2)}, u32[]{:S(2)}) collective-permute-start(f32[3,8,128]{2,1,0:T(8,128)S(1)} %get-tuple-element.79), channel_id=1, source_target_pairs={{0,1},{1,0},{2,3},{3,2},{4,5},{5,4},{6,7},{7,6},{8,9},{9,8},{10,11... | collective-permute-start | bytes 36872 | tf_op jit(solution)/shard_map/ppermute | solution.py:692
  16.5 0.2 inner.1
  16.6 0.0 collective-permute-done.3.cb
  16.7 0.0 collective-permute-done.4.ca
  16.7 0.2 edges.1
  16.9 0.8 %collective-permute-start.7 = (f32[2,16,128]{2,1,0:T(8,128)S(1)}, f32[2,16,128]{2,1,0:T(8,128)S(1)}, u32[]{:S(2)}, u32[]{:S(2)}) collective-permute-start(f32[2,16,128]{2,1,0:T(8,128)S(1)} %get-tuple-element.91), channel_id=1, source_target_pairs={{0,16},{4,20},{8,24},{12,28},{16,0},{20,4},{24,8},{28,12},{1,17},{... | collective-permute-start | bytes 49160 | tf_op jit(solution)/shard_map/ppermute | solution.py:635
  17.7 0.4 %collective-permute-done.5.tcb = f32[3,8,128]{2,1,0:T(8,128)S(1)} collective-permute-done((f32[3,8,128]{2,1,0:T(8,128)S(1)}, f32[3,8,128]{2,1,0:T(8,128)S(1)}, u32[]{:S(2)}, u32[]{:S(2)}) %collective-permute-start.5) | collective-permute-done | bytes 12320 | tf_op jit(solution)/shard_map/ppermute | solution.py:691
  18.0 0.0 collective-permute-done.6.tca
  18.0 1.6 %cone.1 = (f32[6,8,40,128]{3,2,1,0:T(8,128)S(1)}, f32[3,8,40,128]{3,2,1,0:T(8,128)S(1)}, f32[10,40,128]{2,1,0:T(8,128)S(1)}, f32[3,40,128]{2,1,0:T(8,128)S(1)}, ...) custom-call(f32[6,8,40,128]{3,2,1,0:T(8,128)S(1)} %get-tuple-element, ...), custom_call_target="tpu_custom_call", output_to_operand_aliasing={{0}: (0, {}), {1}: (1, {}), {2}: (5, {}), {3}: (6, {})} | custom-call | tf_op jit(solution)/shard_map/cone/pallas_call | solution.py:713
  19.6 3.8 %all-to-all-start = ((f32[32,2,128]{2,1,0:T(2,128)}), f32[32,2,128]{2,1,0:T(2,128)S(1)}, u32[]{:S(2)}, u32[]{:S(2)}) async-start(f32[32,2,128]{2,1,0:T(2,128)} %get-tuple-element.94), calls=%async_computation | async-start | bytes 65536 | tf_op jit(solution)/shard_map/all_to_all | solution.py:726
  23.4 0.0 collective-permute-done.7
  23.5 1.8 %collective-permute-start.8 = (f32[1,16,128]{2,1,0:T(8,128)S(1)}, f32[1,16,128]{2,1,0:T(8,128)S(1)}, u32[]{:S(2)}, u32[]{:S(2)}) collective-permute-start(f32[1,16,128]{2,1,0:T(8,128)S(1)} %get-tuple-element.96), channel_id=1, source_target_pairs={{0,4},{4,0},{8,12},{12,8},{16,20},{20,16},{24,28},{28,24},{1,5},{5... | collective-permute-start | bytes 24584 | tf_op jit(solution)/shard_map/ppermute | solution.py:635
  25.3 1.1 %upper.1 = (f32[6,8,40,128]{3,2,1,0:T(8,128)S(1)}, f32[3,8,40,128]{3,2,1,0:T(8,128)S(1)}) custom-call(f32[6,8,40,128]{3,2,1,0:T(8,128)S(1)} %get-tuple-element.82.S_in, f32[3,8,40,128]{3,2,1,0:T(8,128)S(1)} %get-tuple-element.83.V_in, f32[8,40,128]{2,1,0:T(8,128)S(1)} %get-tuple-element.63.LAM, ...), custom_call_target="tpu_custom_call", output_to_operand_aliasing={{0}: (0, {}), {1}: (1, {})} | custom-call | tf_op jit(solution)/shard_map/upper/pallas_call | solution.py:727
  26.4 0.8 %collective-permute-done.8.got = f32[1,16,128]{2,1,0:T(8,128)S(1)} collective-permute-done((f32[1,16,128]{2,1,0:T(8,128)S(1)}, f32[1,16,128]{2,1,0:T(8,128)S(1)}, u32[]{:S(2)}, u32[]{:S(2)}) %collective-permute-start.8) | collective-permute-done | bytes 8224 | tf_op jit(solution)/shard_map/ppermute | solution.py:635
  27.2 2.2 %lower.1 = (f32[6,8,40,128]{3,2,1,0:T(8,128)S(1)}, f32[3,8,40,128]{3,2,1,0:T(8,128)S(1)}, f32[10,40,128]{2,1,0:T(8,128)S(1)}, f32[3,8,32,128]{3,2,1,0:T(8,128)}, f32[6,8,32,128]{3,2,1,0:T(8,128)}) custom-call(f32[6,8,40,128]{3,2,1,0:T(8,128)S(1)} %get-tuple-element.87.S_in, ...), custom_call_target="tpu_custom_call", output_to_operand_aliasing={{0}: (0, {}), {1}: (1, {}), {2}: (5, {})} | custom-call | tf_op jit(solution)/shard_map/lower/pallas_call | solution.py:744
  29.3 1.3 %all-to-all-done.shares = f32[32,2,128]{2,1,0:T(2,128)S(1)} async-done(((f32[32,2,128]{2,1,0:T(2,128)}), f32[32,2,128]{2,1,0:T(2,128)S(1)}, u32[]{:S(2)}, u32[]{:S(2)}) %all-to-all-start) | async-done | bytes 32800 | tf_op jit(solution)/shard_map/all_to_all | solution.py:726
  30.7 1.0 %sum_by_building.1 = f32[2,1024]{1,0:T(2,128)} custom-call(f32[32,2,128]{2,1,0:T(2,128)S(1)} %all-to-all-done.shares), custom_call_target="tpu_custom_call" | custom-call | tf_op jit(solution)/shard_map/sum_by_building/pallas_call | solution.py:736
  (3 shorter events, 0.0 us)
Async XLA Ops:
  0.6 7.6 %copy-start = (f32[6,8,32,128]{3,2,1,0:T(8,128)S(1)}, f32[6,8,32,128]{3,2,1,0:T(8,128)}, u32[]{:S(2)}) copy-start(f32[6,8,32,128]{3,2,1,0:T(8,128)} %stress.3) | copy-start | bytes 2359300
  0.6 7.6 %copy-start.1 = (f32[3,8,32,128]{3,2,1,0:T(8,128)S(1)}, f32[3,8,32,128]{3,2,1,0:T(8,128)}, u32[]{:S(2)}) copy-start(f32[3,8,32,128]{3,2,1,0:T(8,128)} %vel.3) | copy-start | bytes 1179652
  0.7 7.6 %copy-start.2 = (s32[8,32,128]{2,1,0:T(8,128)S(1)}, s32[8,32,128]{2,1,0:T(8,128)}, u32[]{:S(2)}) copy-start(s32[8,32,128]{2,1,0:T(8,128)} %zones.5) | copy-start | bytes 393220
  1.9 12.0 %collective-permute-start = (f32[264,128]{1,0:T(8,128)S(1)}, f32[264,128]{1,0:T(8,128)S(1)}, u32[]{:S(2)}, u32[]{:S(2)}) collective-permute-start(f32[264,128]{1,0:T(8,128)S(1)} %get-tuple-element.56), channel_id=1, source_target_pairs={{0,28},{4,8},{8,4},{12,16},{16,12},{20,24},{24,20},{28,0},{1,29},{... | collective-permute-start | bytes 405512 | tf_op jit(solution)/shard_map/ppermute | solution.py:621
  8.0 6.5 %collective-permute-start.1 = (f32[264,128]{1,0:T(8,128)S(1)}, f32[264,128]{1,0:T(8,128)S(1)}, u32[]{:S(2)}, u32[]{:S(2)}) collective-permute-start(f32[264,128]{1,0:T(8,128)S(1)} %get-tuple-element.57), channel_id=1, source_target_pairs={{0,4},{4,0},{8,12},{12,8},{16,20},{20,16},{24,28},{28,24},{1,5},{5... | collective-permute-start | bytes 405512 | tf_op jit(solution)/shard_map/ppermute | solution.py:622
  8.1 4.0 %collective-permute-start.2 = (f32[4,16,128]{2,1,0:T(8,128)S(1)}, f32[4,16,128]{2,1,0:T(8,128)S(1)}, u32[]{:S(2)}, u32[]{:S(2)}) collective-permute-start(f32[4,16,128]{2,1,0:T(8,128)S(1)} %get-tuple-element.65), channel_id=1, source_target_pairs={{0,8},{4,12},{8,0},{12,4},{16,24},{20,28},{24,16},{28,20},{1,9},{5... | collective-permute-start | bytes 98312 | tf_op jit(solution)/shard_map/ppermute | solution.py:635
  12.2 4.5 %collective-permute-start.3 = (f32[104,128]{1,0:T(8,128)S(1)}, f32[104,128]{1,0:T(8,128)S(1)}, u32[]{:S(2)}, u32[]{:S(2)}) collective-permute-start(f32[104,128]{1,0:T(8,128)S(1)} %get-tuple-element.72), channel_id=1, source_target_pairs={{0,3},{1,2},{2,1},{3,0},{4,7},{5,6},{6,5},{7,4},{8,11},{9,10},{10,... | collective-permute-start | bytes 159752 | tf_op jit(solution)/shard_map/ppermute | solution.py:678
  12.3 4.4 %collective-permute-start.4 = (f32[104,128]{1,0:T(8,128)S(1)}, f32[104,128]{1,0:T(8,128)S(1)}, u32[]{:S(2)}, u32[]{:S(2)}) collective-permute-start(f32[104,128]{1,0:T(8,128)S(1)} %get-tuple-element.73), channel_id=1, source_target_pairs={{0,1},{1,0},{2,3},{3,2},{4,5},{5,4},{6,7},{7,6},{8,9},{9,8},{10,11... | collective-permute-start | bytes 159752 | tf_op jit(solution)/shard_map/ppermute | solution.py:679
  14.8 3.2 %collective-permute-start.5 = (f32[3,8,128]{2,1,0:T(8,128)S(1)}, f32[3,8,128]{2,1,0:T(8,128)S(1)}, u32[]{:S(2)}, u32[]{:S(2)}) collective-permute-start(f32[3,8,128]{2,1,0:T(8,128)S(1)} %get-tuple-element.78), channel_id=1, source_target_pairs={{0,3},{1,2},{2,1},{3,0},{4,7},{5,6},{6,5},{7,4},{8,11},{9,10},{10,... | collective-permute-start | bytes 36872 | tf_op jit(solution)/shard_map/ppermute | solution.py:691
  15.7 2.4 %collective-permute-start.6 = (f32[3,8,128]{2,1,0:T(8,128)S(1)}, f32[3,8,128]{2,1,0:T(8,128)S(1)}, u32[]{:S(2)}, u32[]{:S(2)}) collective-permute-start(f32[3,8,128]{2,1,0:T(8,128)S(1)} %get-tuple-element.79), channel_id=1, source_target_pairs={{0,1},{1,0},{2,3},{3,2},{4,5},{5,4},{6,7},{7,6},{8,9},{9,8},{10,11... | collective-permute-start | bytes 36872 | tf_op jit(solution)/shard_map/ppermute | solution.py:692
  16.9 6.5 %collective-permute-start.7 = (f32[2,16,128]{2,1,0:T(8,128)S(1)}, f32[2,16,128]{2,1,0:T(8,128)S(1)}, u32[]{:S(2)}, u32[]{:S(2)}) collective-permute-start(f32[2,16,128]{2,1,0:T(8,128)S(1)} %get-tuple-element.91), channel_id=1, source_target_pairs={{0,16},{4,20},{8,24},{12,28},{16,0},{20,4},{24,8},{28,12},{1,17},{... | collective-permute-start | bytes 49160 | tf_op jit(solution)/shard_map/ppermute | solution.py:635
  19.6 11.0 %all-to-all-start = ((f32[32,2,128]{2,1,0:T(2,128)}), f32[32,2,128]{2,1,0:T(2,128)S(1)}, u32[]{:S(2)}, u32[]{:S(2)}) async-start(f32[32,2,128]{2,1,0:T(2,128)} %get-tuple-element.94), calls=%async_computation | async-start | bytes 65536 | tf_op jit(solution)/shard_map/all_to_all | solution.py:726
  23.5 3.7 %collective-permute-start.8 = (f32[1,16,128]{2,1,0:T(8,128)S(1)}, f32[1,16,128]{2,1,0:T(8,128)S(1)}, u32[]{:S(2)}, u32[]{:S(2)}) collective-permute-start(f32[1,16,128]{2,1,0:T(8,128)S(1)} %get-tuple-element.96), channel_id=1, source_target_pairs={{0,4},{4,0},{8,12},{12,8},{16,20},{20,16},{24,28},{28,24},{1,5},{5... | collective-permute-start | bytes 24584 | tf_op jit(solution)/shard_map/ppermute | solution.py:635

commit v7 on v6

--- a/solution.py
+++ b/solution.py
@@ -20,8 +20,8 @@
 RING = CX + 2 * HALO
 FIELDS = 10
 WIDE = 3
-ROWS_AT = WIDE * 4 * 8
-ROWS = ROWS_AT + (FIELDS - WIDE) * 3 * 8
+WIDE_AT = (FIELDS - WIDE) * 3 * 8
+ROWS = WIDE_AT + WIDE * 4 * 8
 PACKS = 3
 CHUNK = 16
 COLS = PACKS * CX
@@ -78,13 +78,13 @@
         for q in range(NZ // 2):
             first = jnp.where(low, tile(f, 2 * q, 0), roll(tile(f, 2 * q + 1, 0), 4, 0))
             last = jnp.where(low, roll(tile(f, 2 * q + 1, 1), 4, 0), tile(f, 2 * q, 1))
-            at = 8 * (f * 4 + q)
+            at = WIDE_AT + 8 * (f * 4 + q)
             gxa[at:at + 8, :] = jnp.where(even_x, last, first)
             gxb[at:at + 8, :] = jnp.where(even_x, first, last)
     for f in range(WIDE, FIELDS):
         for z in range(NZ):
             first, last = tile(f, z, 0), roll(tile(f, z, 1), 3, 0)
-            at = pl.ds(ROWS_AT + (f - WIDE) * 24 + z, 3, stride=8)
+            at = pl.ds((f - WIDE) * 24 + z, 3, stride=8)
             gxa[at, :] = jnp.where(even_x, last, first)[0:3]
             gxb[at, :] = jnp.where(even_x, first, last)[0:3]
 
@@ -368,28 +368,28 @@
     tail = slice(CX, RING)
     columns = [jnp.broadcast_to(row, (8, CY)) for row in spread_table(table)]
 
-    def place(f, z, rows, at):
+    def place(f, z, rows):
         if f < 6:
-            S[f, z, CX + at:CX + at + rows.shape[0], :] = rows
+            S[f, z, tail, :] = rows
         elif f < 9:
-            V[f - 6, z, CX + at:CX + at + rows.shape[0], :] = rows
+            V[f - 6, z, tail, :] = rows
         else:
-            zone_tail[z, at:at + rows.shape[0], :] = rows
+            zone_tail[z] = rows
 
     for f in range(WIDE):
         for q in range(NZ // 2):
-            at = slice(8 * (f * 4 + q), 8 * (f * 4 + q) + 8)
+            at = slice(WIDE_AT + 8 * (f * 4 + q), WIDE_AT + 8 * (f * 4 + q) + 8)
             after = jnp.where(even_x, ra[at], rb[at])
             before = jnp.where(even_x, rb[at], ra[at])
-            place(f, 2 * q, jnp.where(low, after, before), 0)
-            place(f, 2 * q + 1, roll(jnp.where(low, before, after), 4, 0), 0)
+            place(f, 2 * q, jnp.where(low, after, before))
+            place(f, 2 * q + 1, roll(jnp.where(low, before, after), 4, 0))
+    sub = iota((8, CY), 0)
     for f in range(WIDE, FIELDS):
         for z in range(NZ):
-            at = pl.ds(ROWS_AT + (f - WIDE) * 24 + z, 3, stride=8)
+            at = pl.ds((f - WIDE) * 24 + z, 8, stride=8)
             a, b = ra[at, :], rb[at, :]
-            place(f, z, jnp.zeros((8, CY), F32), 0)
-            place(f, z, jnp.where(even_x, a, b), 0)
-            place(f, z, jnp.where(even_x, b, a), 5)
+            after, before = jnp.where(even_x, a, b), roll(jnp.where(even_x, b, a), 5, 0)
+            place(f, z, jnp.where(sub < 3, after, jnp.where(sub >= 5, before, 0.0)))
     for z in range(NZ):
         ids = zone_tail[z].astype(jnp.int32)
         for column, ref in zip(columns, (LAM, MU, BUOY)):

time: 31.8 us -> 31.8 us (level)
  no operation moved by 1% of the time
where the time goes in v7:
time: 31.8 us; the launch traced here: 31.6 us
  starting transfers between devices  16 us (50%)
  Pallas kernels  9.18 us (29%)
  waiting for transfers between devices  5.66 us (18%)
  between operations  0.78 us (2%)
    ppermute x1, starting transfers between devices, body(): rb = lax.ppermute(gxb, 'gx', pairs_far(n_gx))  6.04 us
    all_to_all x1, starting transfers between devices, body(): gathered = lax.all_to_all(shares, ('gx', 'gy'), 0, 0)  3.78 us
    ppermute x3, waiting for transfers between devices, across(): return lax.ppermute(x, 'gx', [(i, i ^ width) for i in range(n_gx)])  3.41 us
    ppermute x3, starting transfers between devices, across(): return lax.ppermute(x, 'gx', [(i, i ^ width) for i in range(n_gx)])  2.76 us
    pallas_call x1, Pallas kernels, body(): pl.pallas_call(lower_kernel, out_shape=(s_ring, v_ring, shaped(FIELDS, RI...  2.16 us
    ppermute x1, starting transfers between devices, body(): ca = lax.ppermute(message_a, 'gy', pairs_near(n_gy))  1.62 us
    pallas_call x1, Pallas kernels, body(): pl.pallas_call(cone_kernel, out_shape=(s_ring, v_ring, shaped(FIELDS, RIN...  1.61 us
    all_to_all x1, waiting for transfers between devices, body(): gathered = lax.all_to_all(shares, ('gx', 'gy'), 0, 0)  1.33 us
  transfers between devices with their start and end apart: 10, of which 5 were waited for; matrix products, arithmetic and copies ran while one was open for 0% of the time, Pallas kernels for 22%

profile of v7, /device:TPU:0, one launch (start us, length us, event | category | flops | bytes accessed | tf_op | source)
XLA Modules:
  0.0 31.6 jit_solution(15095759922842496055)
XLA Ops:
  0.6 0.0 copy-start
  0.6 0.0 copy-start.1
  0.7 0.0 copy-start.2
  0.7 1.3 %pack_rows.1 = (f32[264,128]{1,0:T(8,128)S(1)}, f32[264,128]{1,0:T(8,128)S(1)}, f32[1,2,3,8,256]{4,3,2,1,0:T(8,128)S(1)}, f32[3,16]{1,0:T(4,128)S(1)}, s32[1,1,6...) custom-call(f32[3,8,32,128]{3,2,1,0:T(8,128)} %vel.3, f32[6,8,32,128]{3,2,1,0:T(8,128)} %stress.3, ...), custom_call_target="tpu_custom_call" | custom-call | tf_op jit(solution)/shard_map/pack_rows/pallas_call | solution.py:604
  1.9 6.0 %collective-permute-start = (f32[264,128]{1,0:T(8,128)S(1)}, f32[264,128]{1,0:T(8,128)S(1)}, u32[]{:S(2)}, u32[]{:S(2)}) collective-permute-start(f32[264,128]{1,0:T(8,128)S(1)} %get-tuple-element.56), channel_id=1, source_target_pairs={{0,28},{4,8},{8,4},{12,16},{16,12},{20,24},{24,20},{28,0},{1,29},{... | collective-permute-start | bytes 405512 | tf_op jit(solution)/shard_map/ppermute | solution.py:621
  8.0 0.0 collective-permute-start.1
  8.0 0.1 slices.1
  8.1 0.1 collective-permute-start.2
  8.2 0.0 copy-done
  8.2 0.0 copy-done.1
  8.3 0.0 copy-done.2
  8.3 0.8 %pack_columns.1 = (f32[6,8,40,128]{3,2,1,0:T(8,128)S(1)}, f32[3,8,40,128]{3,2,1,0:T(8,128)S(1)}, f32[96,128]{1,0:T(8,128)S(1)}, f32[96,128]{1,0:T(8,128)S(1)}, f32[10,40,128]{2,1,0:T(8,128)S(1)}) custom-call(f32[3,8,32,128]{3,2,1,0:T(8,128)S(1)} %copy-done.1, f32[6,8,32,128]{3,2,1,0:T(8,128)S(1)} %copy-done, s32[8,32,128]{2,1,0:T(8,128)S(1)} %copy-done.2), custom_call_target="tpu_custom_call" | custom-call | tf_op jit(solution)/shard_map/pack_columns/pallas_call | solution.py:624
  9.1 0.4 %materials.1 = (f32[8,40,128]{2,1,0:T(8,128)S(1)}, f32[8,40,128]{2,1,0:T(8,128)S(1)}, f32[8,40,128]{2,1,0:T(8,128)S(1)}, f32[8,128]{1,0:T(8,128)S(1)}) custom-call(s32[8,32,128]{2,1,0:T(8,128)S(1)} %copy-done.2, f32[3,16]{1,0:T(4,128)S(1)} %get-tuple-element.51.table), custom_call_target="tpu_custom_call" | custom-call | tf_op jit(solution)/shard_map/materials/pallas_call | solution.py:661
  9.5 2.6 %collective-permute-done.2.got = f32[4,16,128]{2,1,0:T(8,128)S(1)} collective-permute-done((f32[4,16,128]{2,1,0:T(8,128)S(1)}, f32[4,16,128]{2,1,0:T(8,128)S(1)}, u32[]{:S(2)}, u32[]{:S(2)}) %collective-permute-start.2) | collective-permute-done | bytes 32800 | tf_op jit(solution)/shard_map/ppermute | solution.py:635
  12.1 0.1 ends.1
  12.2 0.1 collective-permute-start.3
  12.3 1.6 %collective-permute-start.4 = (f32[104,128]{1,0:T(8,128)S(1)}, f32[104,128]{1,0:T(8,128)S(1)}, u32[]{:S(2)}, u32[]{:S(2)}) collective-permute-start(f32[104,128]{1,0:T(8,128)S(1)} %get-tuple-element.73), channel_id=1, source_target_pairs={{0,1},{1,0},{2,3},{3,2},{4,5},{5,4},{6,7},{7,6},{8,9},{9,8},{10,11... | collective-permute-start | bytes 159752 | tf_op jit(solution)/shard_map/ppermute | solution.py:679
  13.9 0.0 collective-permute-done.rb
  13.9 0.6 %collective-permute-done.1.ra = f32[264,128]{1,0:T(8,128)S(1)} collective-permute-done((f32[264,128]{1,0:T(8,128)S(1)}, f32[264,128]{1,0:T(8,128)S(1)}, u32[]{:S(2)}, u32[]{:S(2)}) %collective-permute-start.1) | collective-permute-done | bytes 135200 | tf_op jit(solution)/shard_map/ppermute | solution.py:622
  14.5 0.3 %unpack.1 = (f32[6,8,40,128]{3,2,1,0:T(8,128)S(1)}, f32[3,8,40,128]{3,2,1,0:T(8,128)S(1)}, f32[8,40,128]{2,1,0:T(8,128)S(1)}, f32[8,40,128]{2,1,0:T(8,128)S(1)},...) custom-call(f32[6,8,40,128]{3,2,1,0:T(8,128)S(1)} %get-tuple-element, ...), custom_call_target="tpu_custom_call", output_to_operand_aliasing={{0}: (0, {}), {1}: (1, {}), {2}: (2, {}), {3}: (3, {}), {4}... | custom-call | tf_op jit(solution)/shard_map/unpack/pallas_call | solution.py:681
  14.8 0.9 %collective-permute-start.5 = (f32[3,8,128]{2,1,0:T(8,128)S(1)}, f32[3,8,128]{2,1,0:T(8,128)S(1)}, u32[]{:S(2)}, u32[]{:S(2)}) collective-permute-start(f32[3,8,128]{2,1,0:T(8,128)S(1)} %get-tuple-element.78), channel_id=1, source_target_pairs={{0,3},{1,2},{2,1},{3,0},{4,7},{5,6},{6,5},{7,4},{8,11},{9,10},{10,... | collective-permute-start | bytes 36872 | tf_op jit(solution)/shard_map/ppermute | solution.py:691
  15.6 0.8 %collective-permute-start.6 = (f32[3,8,128]{2,1,0:T(8,128)S(1)}, f32[3,8,128]{2,1,0:T(8,128)S(1)}, u32[]{:S(2)}, u32[]{:S(2)}) collective-permute-start(f32[3,8,128]{2,1,0:T(8,128)S(1)} %get-tuple-element.79), channel_id=1, source_target_pairs={{0,1},{1,0},{2,3},{3,2},{4,5},{5,4},{6,7},{7,6},{8,9},{9,8},{10,11... | collective-permute-start | bytes 36872 | tf_op jit(solution)/shard_map/ppermute | solution.py:692
  16.5 0.2 inner.1
  16.6 0.0 collective-permute-done.3.cb
  16.6 0.0 collective-permute-done.4.ca
  16.7 0.2 edges.1
  16.9 0.8 %collective-permute-start.7 = (f32[2,16,128]{2,1,0:T(8,128)S(1)}, f32[2,16,128]{2,1,0:T(8,128)S(1)}, u32[]{:S(2)}, u32[]{:S(2)}) collective-permute-start(f32[2,16,128]{2,1,0:T(8,128)S(1)} %get-tuple-element.91), channel_id=1, source_target_pairs={{0,16},{4,20},{8,24},{12,28},{16,0},{20,4},{24,8},{28,12},{1,17},{... | collective-permute-start | bytes 49160 | tf_op jit(solution)/shard_map/ppermute | solution.py:635
  17.7 0.4 %collective-permute-done.5.tcb = f32[3,8,128]{2,1,0:T(8,128)S(1)} collective-permute-done((f32[3,8,128]{2,1,0:T(8,128)S(1)}, f32[3,8,128]{2,1,0:T(8,128)S(1)}, u32[]{:S(2)}, u32[]{:S(2)}) %collective-permute-start.5) | collective-permute-done | bytes 12320 | tf_op jit(solution)/shard_map/ppermute | solution.py:691
  18.0 0.0 collective-permute-done.6.tca
  18.0 1.6 %cone.1 = (f32[6,8,40,128]{3,2,1,0:T(8,128)S(1)}, f32[3,8,40,128]{3,2,1,0:T(8,128)S(1)}, f32[10,40,128]{2,1,0:T(8,128)S(1)}, f32[3,40,128]{2,1,0:T(8,128)S(1)}, ...) custom-call(f32[6,8,40,128]{3,2,1,0:T(8,128)S(1)} %get-tuple-element, ...), custom_call_target="tpu_custom_call", output_to_operand_aliasing={{0}: (0, {}), {1}: (1, {}), {2}: (5, {}), {3}: (6, {})} | custom-call | tf_op jit(solution)/shard_map/cone/pallas_call | solution.py:713
  19.6 3.8 %all-to-all-start = ((f32[32,2,128]{2,1,0:T(2,128)}), f32[32,2,128]{2,1,0:T(2,128)S(1)}, u32[]{:S(2)}, u32[]{:S(2)}) async-start(f32[32,2,128]{2,1,0:T(2,128)} %get-tuple-element.94), calls=%async_computation | async-start | bytes 65536 | tf_op jit(solution)/shard_map/all_to_all | solution.py:726
  23.4 0.0 collective-permute-done.7
  23.5 1.8 %collective-permute-start.8 = (f32[1,16,128]{2,1,0:T(8,128)S(1)}, f32[1,16,128]{2,1,0:T(8,128)S(1)}, u32[]{:S(2)}, u32[]{:S(2)}) collective-permute-start(f32[1,16,128]{2,1,0:T(8,128)S(1)} %get-tuple-element.96), channel_id=1, source_target_pairs={{0,4},{4,0},{8,12},{12,8},{16,20},{20,16},{24,28},{28,24},{1,5},{5... | collective-permute-start | bytes 24584 | tf_op jit(solution)/shard_map/ppermute | solution.py:635
  25.3 1.1 %upper.1 = (f32[6,8,40,128]{3,2,1,0:T(8,128)S(1)}, f32[3,8,40,128]{3,2,1,0:T(8,128)S(1)}) custom-call(f32[6,8,40,128]{3,2,1,0:T(8,128)S(1)} %get-tuple-element.82.S_in, f32[3,8,40,128]{3,2,1,0:T(8,128)S(1)} %get-tuple-element.83.V_in, f32[8,40,128]{2,1,0:T(8,128)S(1)} %get-tuple-element.63.LAM, ...), custom_call_target="tpu_custom_call", output_to_operand_aliasing={{0}: (0, {}), {1}: (1, {})} | custom-call | tf_op jit(solution)/shard_map/upper/pallas_call | solution.py:727
  26.4 0.8 %collective-permute-done.8.got = f32[1,16,128]{2,1,0:T(8,128)S(1)} collective-permute-done((f32[1,16,128]{2,1,0:T(8,128)S(1)}, f32[1,16,128]{2,1,0:T(8,128)S(1)}, u32[]{:S(2)}, u32[]{:S(2)}) %collective-permute-start.8) | collective-permute-done | bytes 8224 | tf_op jit(solution)/shard_map/ppermute | solution.py:635
  27.2 2.2 %lower.1 = (f32[6,8,40,128]{3,2,1,0:T(8,128)S(1)}, f32[3,8,40,128]{3,2,1,0:T(8,128)S(1)}, f32[10,40,128]{2,1,0:T(8,128)S(1)}, f32[3,8,32,128]{3,2,1,0:T(8,128)}, f32[6,8,32,128]{3,2,1,0:T(8,128)}) custom-call(f32[6,8,40,128]{3,2,1,0:T(8,128)S(1)} %get-tuple-element.87.S_in, ...), custom_call_target="tpu_custom_call", output_to_operand_aliasing={{0}: (0, {}), {1}: (1, {}), {2}: (5, {})} | custom-call | tf_op jit(solution)/shard_map/lower/pallas_call | solution.py:744
  29.3 1.3 %all-to-all-done.shares = f32[32,2,128]{2,1,0:T(2,128)S(1)} async-done(((f32[32,2,128]{2,1,0:T(2,128)}), f32[32,2,128]{2,1,0:T(2,128)S(1)}, u32[]{:S(2)}, u32[]{:S(2)}) %all-to-all-start) | async-done | bytes 32800 | tf_op jit(solution)/shard_map/all_to_all | solution.py:726
  30.7 1.0 %sum_by_building.1 = f32[2,1024]{1,0:T(2,128)} custom-call(f32[32,2,128]{2,1,0:T(2,128)S(1)} %all-to-all-done.shares), custom_call_target="tpu_custom_call" | custom-call | tf_op jit(solution)/shard_map/sum_by_building/pallas_call | solution.py:736
  (3 shorter events, 0.0 us)
Async XLA Ops:
  0.6 7.6 %copy-start = (f32[6,8,32,128]{3,2,1,0:T(8,128)S(1)}, f32[6,8,32,128]{3,2,1,0:T(8,128)}, u32[]{:S(2)}) copy-start(f32[6,8,32,128]{3,2,1,0:T(8,128)} %stress.3) | copy-start | bytes 2359300
  0.6 7.6 %copy-start.1 = (f32[3,8,32,128]{3,2,1,0:T(8,128)S(1)}, f32[3,8,32,128]{3,2,1,0:T(8,128)}, u32[]{:S(2)}) copy-start(f32[3,8,32,128]{3,2,1,0:T(8,128)} %vel.3) | copy-start | bytes 1179652
  0.7 7.6 %copy-start.2 = (s32[8,32,128]{2,1,0:T(8,128)S(1)}, s32[8,32,128]{2,1,0:T(8,128)}, u32[]{:S(2)}) copy-start(s32[8,32,128]{2,1,0:T(8,128)} %zones.5) | copy-start | bytes 393220
  1.9 12.0 %collective-permute-start = (f32[264,128]{1,0:T(8,128)S(1)}, f32[264,128]{1,0:T(8,128)S(1)}, u32[]{:S(2)}, u32[]{:S(2)}) collective-permute-start(f32[264,128]{1,0:T(8,128)S(1)} %get-tuple-element.56), channel_id=1, source_target_pairs={{0,28},{4,8},{8,4},{12,16},{16,12},{20,24},{24,20},{28,0},{1,29},{... | collective-permute-start | bytes 405512 | tf_op jit(solution)/shard_map/ppermute | solution.py:621
  8.0 6.5 %collective-permute-start.1 = (f32[264,128]{1,0:T(8,128)S(1)}, f32[264,128]{1,0:T(8,128)S(1)}, u32[]{:S(2)}, u32[]{:S(2)}) collective-permute-start(f32[264,128]{1,0:T(8,128)S(1)} %get-tuple-element.57), channel_id=1, source_target_pairs={{0,4},{4,0},{8,12},{12,8},{16,20},{20,16},{24,28},{28,24},{1,5},{5... | collective-permute-start | bytes 405512 | tf_op jit(solution)/shard_map/ppermute | solution.py:622
  8.1 4.0 %collective-permute-start.2 = (f32[4,16,128]{2,1,0:T(8,128)S(1)}, f32[4,16,128]{2,1,0:T(8,128)S(1)}, u32[]{:S(2)}, u32[]{:S(2)}) collective-permute-start(f32[4,16,128]{2,1,0:T(8,128)S(1)} %get-tuple-element.65), channel_id=1, source_target_pairs={{0,8},{4,12},{8,0},{12,4},{16,24},{20,28},{24,16},{28,20},{1,9},{5... | collective-permute-start | bytes 98312 | tf_op jit(solution)/shard_map/ppermute | solution.py:635
  12.2 4.4 %collective-permute-start.3 = (f32[104,128]{1,0:T(8,128)S(1)}, f32[104,128]{1,0:T(8,128)S(1)}, u32[]{:S(2)}, u32[]{:S(2)}) collective-permute-start(f32[104,128]{1,0:T(8,128)S(1)} %get-tuple-element.72), channel_id=1, source_target_pairs={{0,3},{1,2},{2,1},{3,0},{4,7},{5,6},{6,5},{7,4},{8,11},{9,10},{10,... | collective-permute-start | bytes 159752 | tf_op jit(solution)/shard_map/ppermute | solution.py:678
  12.3 4.4 %collective-permute-start.4 = (f32[104,128]{1,0:T(8,128)S(1)}, f32[104,128]{1,0:T(8,128)S(1)}, u32[]{:S(2)}, u32[]{:S(2)}) collective-permute-start(f32[104,128]{1,0:T(8,128)S(1)} %get-tuple-element.73), channel_id=1, source_target_pairs={{0,1},{1,0},{2,3},{3,2},{4,5},{5,4},{6,7},{7,6},{8,9},{9,8},{10,11... | collective-permute-start | bytes 159752 | tf_op jit(solution)/shard_map/ppermute | solution.py:679
  14.8 3.2 %collective-permute-start.5 = (f32[3,8,128]{2,1,0:T(8,128)S(1)}, f32[3,8,128]{2,1,0:T(8,128)S(1)}, u32[]{:S(2)}, u32[]{:S(2)}) collective-permute-start(f32[3,8,128]{2,1,0:T(8,128)S(1)} %get-tuple-element.78), channel_id=1, source_target_pairs={{0,3},{1,2},{2,1},{3,0},{4,7},{5,6},{6,5},{7,4},{8,11},{9,10},{10,... | collective-permute-start | bytes 36872 | tf_op jit(solution)/shard_map/ppermute | solution.py:691
  15.6 2.4 %collective-permute-start.6 = (f32[3,8,128]{2,1,0:T(8,128)S(1)}, f32[3,8,128]{2,1,0:T(8,128)S(1)}, u32[]{:S(2)}, u32[]{:S(2)}) collective-permute-start(f32[3,8,128]{2,1,0:T(8,128)S(1)} %get-tuple-element.79), channel_id=1, source_target_pairs={{0,1},{1,0},{2,3},{3,2},{4,5},{5,4},{6,7},{7,6},{8,9},{9,8},{10,11... | collective-permute-start | bytes 36872 | tf_op jit(solution)/shard_map/ppermute | solution.py:692
  16.9 6.5 %collective-permute-start.7 = (f32[2,16,128]{2,1,0:T(8,128)S(1)}, f32[2,16,128]{2,1,0:T(8,128)S(1)}, u32[]{:S(2)}, u32[]{:S(2)}) collective-permute-start(f32[2,16,128]{2,1,0:T(8,128)S(1)} %get-tuple-element.91), channel_id=1, source_target_pairs={{0,16},{4,20},{8,24},{12,28},{16,0},{20,4},{24,8},{28,12},{1,17},{... | collective-permute-start | bytes 49160 | tf_op jit(solution)/shard_map/ppermute | solution.py:635
  19.6 11.0 %all-to-all-start = ((f32[32,2,128]{2,1,0:T(2,128)}), f32[32,2,128]{2,1,0:T(2,128)S(1)}, u32[]{:S(2)}, u32[]{:S(2)}) async-start(f32[32,2,128]{2,1,0:T(2,128)} %get-tuple-element.94), calls=%async_computation | async-start | bytes 65536 | tf_op jit(solution)/shard_map/all_to_all | solution.py:726
  23.5 3.7 %collective-permute-start.8 = (f32[1,16,128]{2,1,0:T(8,128)S(1)}, f32[1,16,128]{2,1,0:T(8,128)S(1)}, u32[]{:S(2)}, u32[]{:S(2)}) collective-permute-start(f32[1,16,128]{2,1,0:T(8,128)S(1)} %get-tuple-element.96), channel_id=1, source_target_pairs={{0,4},{4,0},{8,12},{12,8},{16,20},{20,16},{24,28},{28,24},{1,5},{5... | collective-permute-start | bytes 24584 | tf_op jit(solution)/shard_map/ppermute | solution.py:635

commit v8 on v7

--- a/solution.py
+++ b/solution.py
@@ -311,17 +311,13 @@
             V[c, z] = V[c, z] + scale * roll(seam[(XY, YY, YZ)[c]], -(16 * z + 3), 1)
 
 
-def velocity_band(band, new, BM, drm):
-    sxy, sxz, syz = band[XY], band[XZ], band[YZ]
-    force = [
-        dx(band[XX]) + band_dy(sxy) + band_dz(sxz),
-        dx(sxy) + band_dy(band[YY]) + band_dz(syz),
-        dx(sxz) + band_dy(syz) + band_dz(band[ZZ]),
-    ]
-    for c in range(3):
+def velocity_band(band, new, BM, drm, comps=(0, 1, 2)):
+    for c in comps:
+        x, y, vert = ((XX, XY, XZ), (XY, YY, YZ), (XZ, YZ, ZZ))[c]
+        force = dx(band[x]) + band_dy(band[y]) + band_dz(band[vert])
         if drm is not None:
-            force[c] = force[c] + (20.0 * BM[1]) * drm(c, 1)
-        new[6 + c] = band[6 + c] + BM[2] * force[c]
+            force = force + (20.0 * BM[1]) * drm(c, 1)
+        new[6 + c] = band[6 + c] + BM[2] * force
 
 
 def stress_plane(z, seam, S, V, LAM, MU, fields):
@@ -437,7 +433,7 @@
         stress_plane(z, seam, S, V, LAM, MU, (FLAT, STEEP)[z % 2])
     stress_band(BF, BW, BM)
     velocity_planes(moving(range(0, 3), True), S, V, MU, BUOY, BW, None)
-    velocity_band(BW, BW, BM, None)
+    velocity_band(BW, BW, BM, None, (2,))
     stress_plane(1, seams(BW, (8,)), S, V, LAM, MU, (XZ, YZ))
 
     total = jnp.zeros((8, CY), F32)
@@ -458,12 +454,13 @@
     shares[...] = jnp.broadcast_to(message[None], shares.shape)
 
 
-def upper_kernel(S_in, V_in, LAM, MU, BUOY, BF, BV, BW, S, V):
+def upper_kernel(S_in, V_in, LAM, MU, BUOY, BF, BM, BV, BW_in, S, V, BW):
     velocity_planes(moving(range(0, 5), False) + every(range(5, 7)), S, V, MU, BUOY, BF, None)
     seam = {6 + c: value for c, value in seams(BV, range(3)).items()}
     for z in range(0, 6):
         stress_plane(z, seam, S, V, LAM, MU, ALL if z > 3 else (STEEP, FLAT)[z % 2])
     velocity_planes(moving(range(0, 3), False) + every(range(3, 5)), S, V, MU, BUOY, BW, None)
+    velocity_band(BW, BW, BM, None, (0, 1))
     seam = seams(BW, (6, 7, 8))
     for z in range(0, 4):
         stress_plane(z, seam, S, V, LAM, MU, FLAT if z == 1 else ALL)
@@ -724,15 +721,15 @@
     sent, kept = jnp.where(odd, held[0], held[1])[None], jnp.where(odd, held[1], held[0])[None]
     got = across(sent, 1)
     gathered = lax.all_to_all(shares, ("gx", "gy"), 0, 0)
-    S, V = pl.pallas_call(
+    S, V, _ = pl.pallas_call(
         upper_kernel,
-        out_shape=(s_ring, v_ring),
-        in_specs=[vmem] * 8,
-        out_specs=(vmem,) * 2,
-        input_output_aliases={0: 0, 1: 1},
+        out_shape=(s_ring, v_ring, shaped(9, RING, CY)),
+        in_specs=[vmem] * 9,
+        out_specs=(vmem,) * 3,
+        input_output_aliases={0: 0, 1: 1, 8: 2},
         compiler_params=params,
         name="upper",
-    )(S, V, LAM, MU, BUOY, BF, BV, BW)
+    )(S, V, LAM, MU, BUOY, BF, BM, BV, BW)
     shear = pl.pallas_call(
         functools.partial(sum_kernel, n),
         out_shape=shaped(2, BUILDINGS),

time: 31.8 us -> 31.8 us (level)
  no operation moved by 1% of the time
where the time goes in v8:
time: 31.8 us; the launch traced here: 31.6 us
  starting transfers between devices  16 us (50%)
  Pallas kernels  9.23 us (29%)
  waiting for transfers between devices  5.56 us (17%)
  between operations  0.78 us (2%)
    ppermute x1, starting transfers between devices, body(): rb = lax.ppermute(gxb, 'gx', pairs_far(n_gx))  6.04 us
    all_to_all x1, starting transfers between devices, body(): gathered = lax.all_to_all(shares, ('gx', 'gy'), 0, 0)  3.78 us
    ppermute x3, waiting for transfers between devices, across(): return lax.ppermute(x, 'gx', [(i, i ^ width) for i in range(n_gx)])  3.31 us
    ppermute x3, starting transfers between devices, across(): return lax.ppermute(x, 'gx', [(i, i ^ width) for i in range(n_gx)])  2.76 us
    pallas_call x1, Pallas kernels, body(): pl.pallas_call(lower_kernel, out_shape=(s_ring, v_ring, shaped(FIELDS, RI...  2.16 us
    ppermute x1, starting transfers between devices, body(): ca = lax.ppermute(message_a, 'gy', pairs_near(n_gy))  1.62 us
    pallas_call x1, Pallas kernels, body(): pl.pallas_call(cone_kernel, out_shape=(s_ring, v_ring, shaped(FIELDS, RIN...  1.55 us
    all_to_all x1, waiting for transfers between devices, body(): gathered = lax.all_to_all(shares, ('gx', 'gy'), 0, 0)  1.33 us
  transfers between devices with their start and end apart: 10, of which 5 were waited for; matrix products, arithmetic and copies ran while one was open for 0% of the time, Pallas kernels for 22%

profile of v8, /device:TPU:0, one launch (start us, length us, event | category | flops | bytes accessed | tf_op | source)
XLA Modules:
  0.0 31.6 jit_solution(6143744221038386416)
XLA Ops:
  0.6 0.0 copy-start
  0.6 0.0 copy-start.1
  0.7 0.0 copy-start.2
  0.7 1.3 %pack_rows.1 = (f32[264,128]{1,0:T(8,128)S(1)}, f32[264,128]{1,0:T(8,128)S(1)}, f32[1,2,3,8,256]{4,3,2,1,0:T(8,128)S(1)}, f32[3,16]{1,0:T(4,128)S(1)}, s32[1,1,6...) custom-call(f32[3,8,32,128]{3,2,1,0:T(8,128)} %vel.3, f32[6,8,32,128]{3,2,1,0:T(8,128)} %stress.3, ...), custom_call_target="tpu_custom_call" | custom-call | tf_op jit(solution)/shard_map/pack_rows/pallas_call | solution.py:601
  1.9 6.0 %collective-permute-start = (f32[264,128]{1,0:T(8,128)S(1)}, f32[264,128]{1,0:T(8,128)S(1)}, u32[]{:S(2)}, u32[]{:S(2)}) collective-permute-start(f32[264,128]{1,0:T(8,128)S(1)} %get-tuple-element.56), channel_id=1, source_target_pairs={{0,28},{4,8},{8,4},{12,16},{16,12},{20,24},{24,20},{28,0},{1,29},{... | collective-permute-start | bytes 405512 | tf_op jit(solution)/shard_map/ppermute | solution.py:618
  8.0 0.0 collective-permute-start.1
  8.0 0.1 slices.1
  8.1 0.1 collective-permute-start.2
  8.2 0.0 copy-done
  8.2 0.0 copy-done.1
  8.3 0.0 copy-done.2
  8.3 0.8 %pack_columns.1 = (f32[6,8,40,128]{3,2,1,0:T(8,128)S(1)}, f32[3,8,40,128]{3,2,1,0:T(8,128)S(1)}, f32[96,128]{1,0:T(8,128)S(1)}, f32[96,128]{1,0:T(8,128)S(1)}, f32[10,40,128]{2,1,0:T(8,128)S(1)}) custom-call(f32[3,8,32,128]{3,2,1,0:T(8,128)S(1)} %copy-done.1, f32[6,8,32,128]{3,2,1,0:T(8,128)S(1)} %copy-done, s32[8,32,128]{2,1,0:T(8,128)S(1)} %copy-done.2), custom_call_target="tpu_custom_call" | custom-call | tf_op jit(solution)/shard_map/pack_columns/pallas_call | solution.py:621
  9.1 0.4 %materials.1 = (f32[8,40,128]{2,1,0:T(8,128)S(1)}, f32[8,40,128]{2,1,0:T(8,128)S(1)}, f32[8,40,128]{2,1,0:T(8,128)S(1)}, f32[8,128]{1,0:T(8,128)S(1)}) custom-call(s32[8,32,128]{2,1,0:T(8,128)S(1)} %copy-done.2, f32[3,16]{1,0:T(4,128)S(1)} %get-tuple-element.51.table), custom_call_target="tpu_custom_call" | custom-call | tf_op jit(solution)/shard_map/materials/pallas_call | solution.py:658
  9.5 2.6 %collective-permute-done.2.got = f32[4,16,128]{2,1,0:T(8,128)S(1)} collective-permute-done((f32[4,16,128]{2,1,0:T(8,128)S(1)}, f32[4,16,128]{2,1,0:T(8,128)S(1)}, u32[]{:S(2)}, u32[]{:S(2)}) %collective-permute-start.2) | collective-permute-done | bytes 32800 | tf_op jit(solution)/shard_map/ppermute | solution.py:632
  12.1 0.1 ends.1
  12.2 0.1 collective-permute-start.3
  12.3 1.6 %collective-permute-start.4 = (f32[104,128]{1,0:T(8,128)S(1)}, f32[104,128]{1,0:T(8,128)S(1)}, u32[]{:S(2)}, u32[]{:S(2)}) collective-permute-start(f32[104,128]{1,0:T(8,128)S(1)} %get-tuple-element.73), channel_id=1, source_target_pairs={{0,1},{1,0},{2,3},{3,2},{4,5},{5,4},{6,7},{7,6},{8,9},{9,8},{10,11... | collective-permute-start | bytes 159752 | tf_op jit(solution)/shard_map/ppermute | solution.py:676
  13.9 0.0 collective-permute-done.rb
  13.9 0.6 %collective-permute-done.1.ra = f32[264,128]{1,0:T(8,128)S(1)} collective-permute-done((f32[264,128]{1,0:T(8,128)S(1)}, f32[264,128]{1,0:T(8,128)S(1)}, u32[]{:S(2)}, u32[]{:S(2)}) %collective-permute-start.1) | collective-permute-done | bytes 135200 | tf_op jit(solution)/shard_map/ppermute | solution.py:619
  14.5 0.3 %unpack.1 = (f32[6,8,40,128]{3,2,1,0:T(8,128)S(1)}, f32[3,8,40,128]{3,2,1,0:T(8,128)S(1)}, f32[8,40,128]{2,1,0:T(8,128)S(1)}, f32[8,40,128]{2,1,0:T(8,128)S(1)},...) custom-call(f32[6,8,40,128]{3,2,1,0:T(8,128)S(1)} %get-tuple-element, ...), custom_call_target="tpu_custom_call", output_to_operand_aliasing={{0}: (0, {}), {1}: (1, {}), {2}: (2, {}), {3}: (3, {}), {4}... | custom-call | tf_op jit(solution)/shard_map/unpack/pallas_call | solution.py:678
  14.8 0.9 %collective-permute-start.5 = (f32[3,8,128]{2,1,0:T(8,128)S(1)}, f32[3,8,128]{2,1,0:T(8,128)S(1)}, u32[]{:S(2)}, u32[]{:S(2)}) collective-permute-start(f32[3,8,128]{2,1,0:T(8,128)S(1)} %get-tuple-element.78), channel_id=1, source_target_pairs={{0,3},{1,2},{2,1},{3,0},{4,7},{5,6},{6,5},{7,4},{8,11},{9,10},{10,... | collective-permute-start | bytes 36872 | tf_op jit(solution)/shard_map/ppermute | solution.py:688
  15.6 0.8 %collective-permute-start.6 = (f32[3,8,128]{2,1,0:T(8,128)S(1)}, f32[3,8,128]{2,1,0:T(8,128)S(1)}, u32[]{:S(2)}, u32[]{:S(2)}) collective-permute-start(f32[3,8,128]{2,1,0:T(8,128)S(1)} %get-tuple-element.79), channel_id=1, source_target_pairs={{0,1},{1,0},{2,3},{3,2},{4,5},{5,4},{6,7},{7,6},{8,9},{9,8},{10,11... | collective-permute-start | bytes 36872 | tf_op jit(solution)/shard_map/ppermute | solution.py:689
  16.5 0.2 inner.1
  16.6 0.0 collective-permute-done.3.cb
  16.6 0.0 collective-permute-done.4.ca
  16.7 0.2 edges.1
  16.9 0.8 %collective-permute-start.7 = (f32[2,16,128]{2,1,0:T(8,128)S(1)}, f32[2,16,128]{2,1,0:T(8,128)S(1)}, u32[]{:S(2)}, u32[]{:S(2)}) collective-permute-start(f32[2,16,128]{2,1,0:T(8,128)S(1)} %get-tuple-element.91), channel_id=1, source_target_pairs={{0,16},{4,20},{8,24},{12,28},{16,0},{20,4},{24,8},{28,12},{1,17},{... | collective-permute-start | bytes 49160 | tf_op jit(solution)/shard_map/ppermute | solution.py:632
  17.7 0.4 %collective-permute-done.5.tcb = f32[3,8,128]{2,1,0:T(8,128)S(1)} collective-permute-done((f32[3,8,128]{2,1,0:T(8,128)S(1)}, f32[3,8,128]{2,1,0:T(8,128)S(1)}, u32[]{:S(2)}, u32[]{:S(2)}) %collective-permute-start.5) | collective-permute-done | bytes 12320 | tf_op jit(solution)/shard_map/ppermute | solution.py:688
  18.0 0.0 collective-permute-done.6.tca
  18.0 1.5 %cone.1 = (f32[6,8,40,128]{3,2,1,0:T(8,128)S(1)}, f32[3,8,40,128]{3,2,1,0:T(8,128)S(1)}, f32[10,40,128]{2,1,0:T(8,128)S(1)}, f32[3,40,128]{2,1,0:T(8,128)S(1)}, ...) custom-call(f32[6,8,40,128]{3,2,1,0:T(8,128)S(1)} %get-tuple-element, ...), custom_call_target="tpu_custom_call", output_to_operand_aliasing={{0}: (0, {}), {1}: (1, {}), {2}: (5, {}), {3}: (6, {})} | custom-call | tf_op jit(solution)/shard_map/cone/pallas_call | solution.py:710
  19.6 3.8 %all-to-all-start = ((f32[32,2,128]{2,1,0:T(2,128)}), f32[32,2,128]{2,1,0:T(2,128)S(1)}, u32[]{:S(2)}, u32[]{:S(2)}) async-start(f32[32,2,128]{2,1,0:T(2,128)} %get-tuple-element.94), calls=%async_computation | async-start | bytes 65536 | tf_op jit(solution)/shard_map/all_to_all | solution.py:723
  23.4 0.0 collective-permute-done.7
  23.4 1.8 %collective-permute-start.8 = (f32[1,16,128]{2,1,0:T(8,128)S(1)}, f32[1,16,128]{2,1,0:T(8,128)S(1)}, u32[]{:S(2)}, u32[]{:S(2)}) collective-permute-start(f32[1,16,128]{2,1,0:T(8,128)S(1)} %get-tuple-element.96), channel_id=1, source_target_pairs={{0,4},{4,0},{8,12},{12,8},{16,20},{20,16},{24,28},{28,24},{1,5},{5... | collective-permute-start | bytes 24584 | tf_op jit(solution)/shard_map/ppermute | solution.py:632
  25.2 1.2 %upper.1 = (f32[6,8,40,128]{3,2,1,0:T(8,128)S(1)}, f32[3,8,40,128]{3,2,1,0:T(8,128)S(1)}, f32[9,40,128]{2,1,0:T(8,128)S(1)}) custom-call(f32[6,8,40,128]{3,2,1,0:T(8,128)S(1)} %get-tuple-element.82.S_in, f32[3,8,40,128]{3,2,1,0:T(8,128)S(1)} %get-tuple-element.83.V_in, ...), custom_call_target="tpu_custom_call", output_to_operand_aliasing={{0}: (0, {}), {1}: (1, {}), {2}: (8, {})} | custom-call | tf_op jit(solution)/shard_map/upper/pallas_call | solution.py:724
  26.4 0.7 %collective-permute-done.8.got = f32[1,16,128]{2,1,0:T(8,128)S(1)} collective-permute-done((f32[1,16,128]{2,1,0:T(8,128)S(1)}, f32[1,16,128]{2,1,0:T(8,128)S(1)}, u32[]{:S(2)}, u32[]{:S(2)}) %collective-permute-start.8) | collective-permute-done | bytes 8224 | tf_op jit(solution)/shard_map/ppermute | solution.py:632
  27.1 2.2 %lower.1 = (f32[6,8,40,128]{3,2,1,0:T(8,128)S(1)}, f32[3,8,40,128]{3,2,1,0:T(8,128)S(1)}, f32[10,40,128]{2,1,0:T(8,128)S(1)}, f32[3,8,32,128]{3,2,1,0:T(8,128)}, f32[6,8,32,128]{3,2,1,0:T(8,128)}) custom-call(f32[6,8,40,128]{3,2,1,0:T(8,128)S(1)} %get-tuple-element.88.S_in, ...), custom_call_target="tpu_custom_call", output_to_operand_aliasing={{0}: (0, {}), {1}: (1, {}), {2}: (5, {})} | custom-call | tf_op jit(solution)/shard_map/lower/pallas_call | solution.py:741
  29.3 1.3 %all-to-all-done.shares = f32[32,2,128]{2,1,0:T(2,128)S(1)} async-done(((f32[32,2,128]{2,1,0:T(2,128)}), f32[32,2,128]{2,1,0:T(2,128)S(1)}, u32[]{:S(2)}, u32[]{:S(2)}) %all-to-all-start) | async-done | bytes 32800 | tf_op jit(solution)/shard_map/all_to_all | solution.py:723
  30.6 1.0 %sum_by_building.1 = f32[2,1024]{1,0:T(2,128)} custom-call(f32[32,2,128]{2,1,0:T(2,128)S(1)} %all-to-all-done.shares), custom_call_target="tpu_custom_call" | custom-call | tf_op jit(solution)/shard_map/sum_by_building/pallas_call | solution.py:733
  (3 shorter events, 0.0 us)
Async XLA Ops:
  0.6 7.6 %copy-start = (f32[6,8,32,128]{3,2,1,0:T(8,128)S(1)}, f32[6,8,32,128]{3,2,1,0:T(8,128)}, u32[]{:S(2)}) copy-start(f32[6,8,32,128]{3,2,1,0:T(8,128)} %stress.3) | copy-start | bytes 2359300
  0.6 7.6 %copy-start.1 = (f32[3,8,32,128]{3,2,1,0:T(8,128)S(1)}, f32[3,8,32,128]{3,2,1,0:T(8,128)}, u32[]{:S(2)}) copy-start(f32[3,8,32,128]{3,2,1,0:T(8,128)} %vel.3) | copy-start | bytes 1179652
  0.7 7.6 %copy-start.2 = (s32[8,32,128]{2,1,0:T(8,128)S(1)}, s32[8,32,128]{2,1,0:T(8,128)}, u32[]{:S(2)}) copy-start(s32[8,32,128]{2,1,0:T(8,128)} %zones.5) | copy-start | bytes 393220
  1.9 12.0 %collective-permute-start = (f32[264,128]{1,0:T(8,128)S(1)}, f32[264,128]{1,0:T(8,128)S(1)}, u32[]{:S(2)}, u32[]{:S(2)}) collective-permute-start(f32[264,128]{1,0:T(8,128)S(1)} %get-tuple-element.56), channel_id=1, source_target_pairs={{0,28},{4,8},{8,4},{12,16},{16,12},{20,24},{24,20},{28,0},{1,29},{... | collective-permute-start | bytes 405512 | tf_op jit(solution)/shard_map/ppermute | solution.py:618
  8.0 6.5 %collective-permute-start.1 = (f32[264,128]{1,0:T(8,128)S(1)}, f32[264,128]{1,0:T(8,128)S(1)}, u32[]{:S(2)}, u32[]{:S(2)}) collective-permute-start(f32[264,128]{1,0:T(8,128)S(1)} %get-tuple-element.57), channel_id=1, source_target_pairs={{0,4},{4,0},{8,12},{12,8},{16,20},{20,16},{24,28},{28,24},{1,5},{5... | collective-permute-start | bytes 405512 | tf_op jit(solution)/shard_map/ppermute | solution.py:619
  8.1 4.0 %collective-permute-start.2 = (f32[4,16,128]{2,1,0:T(8,128)S(1)}, f32[4,16,128]{2,1,0:T(8,128)S(1)}, u32[]{:S(2)}, u32[]{:S(2)}) collective-permute-start(f32[4,16,128]{2,1,0:T(8,128)S(1)} %get-tuple-element.65), channel_id=1, source_target_pairs={{0,8},{4,12},{8,0},{12,4},{16,24},{20,28},{24,16},{28,20},{1,9},{5... | collective-permute-start | bytes 98312 | tf_op jit(solution)/shard_map/ppermute | solution.py:632
  12.2 4.4 %collective-permute-start.3 = (f32[104,128]{1,0:T(8,128)S(1)}, f32[104,128]{1,0:T(8,128)S(1)}, u32[]{:S(2)}, u32[]{:S(2)}) collective-permute-start(f32[104,128]{1,0:T(8,128)S(1)} %get-tuple-element.72), channel_id=1, source_target_pairs={{0,3},{1,2},{2,1},{3,0},{4,7},{5,6},{6,5},{7,4},{8,11},{9,10},{10,... | collective-permute-start | bytes 159752 | tf_op jit(solution)/shard_map/ppermute | solution.py:675
  12.3 4.4 %collective-permute-start.4 = (f32[104,128]{1,0:T(8,128)S(1)}, f32[104,128]{1,0:T(8,128)S(1)}, u32[]{:S(2)}, u32[]{:S(2)}) collective-permute-start(f32[104,128]{1,0:T(8,128)S(1)} %get-tuple-element.73), channel_id=1, source_target_pairs={{0,1},{1,0},{2,3},{3,2},{4,5},{5,4},{6,7},{7,6},{8,9},{9,8},{10,11... | collective-permute-start | bytes 159752 | tf_op jit(solution)/shard_map/ppermute | solution.py:676
  14.8 3.2 %collective-permute-start.5 = (f32[3,8,128]{2,1,0:T(8,128)S(1)}, f32[3,8,128]{2,1,0:T(8,128)S(1)}, u32[]{:S(2)}, u32[]{:S(2)}) collective-permute-start(f32[3,8,128]{2,1,0:T(8,128)S(1)} %get-tuple-element.78), channel_id=1, source_target_pairs={{0,3},{1,2},{2,1},{3,0},{4,7},{5,6},{6,5},{7,4},{8,11},{9,10},{10,... | collective-permute-start | bytes 36872 | tf_op jit(solution)/shard_map/ppermute | solution.py:688
  15.6 2.4 %collective-permute-start.6 = (f32[3,8,128]{2,1,0:T(8,128)S(1)}, f32[3,8,128]{2,1,0:T(8,128)S(1)}, u32[]{:S(2)}, u32[]{:S(2)}) collective-permute-start(f32[3,8,128]{2,1,0:T(8,128)S(1)} %get-tuple-element.79), channel_id=1, source_target_pairs={{0,1},{1,0},{2,3},{3,2},{4,5},{5,4},{6,7},{7,6},{8,9},{9,8},{10,11... | collective-permute-start | bytes 36872 | tf_op jit(solution)/shard_map/ppermute | solution.py:689
  16.9 6.5 %collective-permute-start.7 = (f32[2,16,128]{2,1,0:T(8,128)S(1)}, f32[2,16,128]{2,1,0:T(8,128)S(1)}, u32[]{:S(2)}, u32[]{:S(2)}) collective-permute-start(f32[2,16,128]{2,1,0:T(8,128)S(1)} %get-tuple-element.91), channel_id=1, source_target_pairs={{0,16},{4,20},{8,24},{12,28},{16,0},{20,4},{24,8},{28,12},{1,17},{... | collective-permute-start | bytes 49160 | tf_op jit(solution)/shard_map/ppermute | solution.py:632
  19.6 11.0 %all-to-all-start = ((f32[32,2,128]{2,1,0:T(2,128)}), f32[32,2,128]{2,1,0:T(2,128)S(1)}, u32[]{:S(2)}, u32[]{:S(2)}) async-start(f32[32,2,128]{2,1,0:T(2,128)} %get-tuple-element.94), calls=%async_computation | async-start | bytes 65536 | tf_op jit(solution)/shard_map/all_to_all | solution.py:723
  23.4 3.7 %collective-permute-start.8 = (f32[1,16,128]{2,1,0:T(8,128)S(1)}, f32[1,16,128]{2,1,0:T(8,128)S(1)}, u32[]{:S(2)}, u32[]{:S(2)}) collective-permute-start(f32[1,16,128]{2,1,0:T(8,128)S(1)} %get-tuple-element.96), channel_id=1, source_target_pairs={{0,4},{4,0},{8,12},{12,8},{16,20},{20,16},{24,28},{28,24},{1,5},{5... | collective-permute-start | bytes 24584 | tf_op jit(solution)/shard_map/ppermute | solution.py:632

commit v9 on v8

--- a/solution.py
+++ b/solution.py
@@ -339,13 +339,14 @@
         S[YZ, z] = S[YZ, z] + mu * (dz(V, 1, z) + dy(vz, seam[8], z))
 
 
-def stress_band(band, new, BM):
+def stress_band(band, new, BM, keep_xx=True):
     vx, vy, vz = new[6], new[7], new[8]
     lam, mu = BM[0], BM[1]
     xx, yy, zz = dx(vx), band_dy(vy), band_dz(vz)
     theta = lam * (xx + yy + zz)
     two = mu + mu
-    new[XX] = band[XX] + (theta + two * xx)
+    if keep_xx:
+        new[XX] = band[XX] + (theta + two * xx)
     new[YY] = band[YY] + (theta + two * yy)
     new[ZZ] = band[ZZ] + (theta + two * zz)
     new[XZ] = band[XZ] + mu * (band_dz(vx) + dx(vz))
@@ -431,7 +432,7 @@
     seam = seams(BW, (6, 7, 8))
     for z in range(0, 4):
         stress_plane(z, seam, S, V, LAM, MU, (FLAT, STEEP)[z % 2])
-    stress_band(BF, BW, BM)
+    stress_band(BF, BW, BM, False)
     velocity_planes(moving(range(0, 3), True), S, V, MU, BUOY, BW, None)
     velocity_band(BW, BW, BM, None, (2,))
     stress_plane(1, seams(BW, (8,)), S, V, LAM, MU, (XZ, YZ))
@@ -460,6 +461,9 @@
     for z in range(0, 6):
         stress_plane(z, seam, S, V, LAM, MU, ALL if z > 3 else (STEEP, FLAT)[z % 2])
     velocity_planes(moving(range(0, 3), False) + every(range(3, 5)), S, V, MU, BUOY, BW, None)
+    vx, vy, vz = BV[0], BV[1], BV[2]
+    xx, yy, zz = dx(vx), band_dy(vy), band_dz(vz)
+    BW[XX] = BF[XX] + (BM[0] * (xx + yy + zz) + (BM[1] + BM[1]) * xx)
     velocity_band(BW, BW, BM, None, (0, 1))
     seam = seams(BW, (6, 7, 8))
     for z in range(0, 4):

time: 31.8 us -> 31.8 us (level)
  no operation moved by 1% of the time
where the time goes in v9:
time: 31.8 us; the launch traced here: 31.6 us
  starting transfers between devices  16 us (50%)
  Pallas kernels  9.25 us (29%)
  waiting for transfers between devices  5.54 us (17%)
  between operations  0.78 us (2%)
    ppermute x1, starting transfers between devices, body(): rb = lax.ppermute(gxb, 'gx', pairs_far(n_gx))  6.04 us
    all_to_all x1, starting transfers between devices, body(): gathered = lax.all_to_all(shares, ('gx', 'gy'), 0, 0)  3.78 us
    ppermute x3, waiting for transfers between devices, across(): return lax.ppermute(x, 'gx', [(i, i ^ width) for i in range(n_gx)])  3.29 us
    ppermute x3, starting transfers between devices, across(): return lax.ppermute(x, 'gx', [(i, i ^ width) for i in range(n_gx)])  2.76 us
    pallas_call x1, Pallas kernels, body(): pl.pallas_call(lower_kernel, out_shape=(s_ring, v_ring, shaped(FIELDS, RI...  2.16 us
    ppermute x1, starting transfers between devices, body(): ca = lax.ppermute(message_a, 'gy', pairs_near(n_gy))  1.62 us
    pallas_call x1, Pallas kernels, body(): pl.pallas_call(cone_kernel, out_shape=(s_ring, v_ring, shaped(FIELDS, RIN...  1.55 us
    all_to_all x1, waiting for transfers between devices, body(): gathered = lax.all_to_all(shares, ('gx', 'gy'), 0, 0)  1.33 us
  transfers between devices with their start and end apart: 10, of which 5 were waited for; matrix products, arithmetic and copies ran while one was open for 0% of the time, Pallas kernels for 22%

profile of v9, /device:TPU:0, one launch (start us, length us, event | category | flops | bytes accessed | tf_op | source)
XLA Modules:
  0.0 31.6 jit_solution(10313817029421764325)
XLA Ops:
  0.6 0.0 copy-start
  0.6 0.0 copy-start.1
  0.7 0.0 copy-start.2
  0.7 1.3 %pack_rows.1 = (f32[264,128]{1,0:T(8,128)S(1)}, f32[264,128]{1,0:T(8,128)S(1)}, f32[1,2,3,8,256]{4,3,2,1,0:T(8,128)S(1)}, f32[3,16]{1,0:T(4,128)S(1)}, s32[1,1,6...) custom-call(f32[3,8,32,128]{3,2,1,0:T(8,128)} %vel.3, f32[6,8,32,128]{3,2,1,0:T(8,128)} %stress.3, ...), custom_call_target="tpu_custom_call" | custom-call | tf_op jit(solution)/shard_map/pack_rows/pallas_call | solution.py:605
  1.9 6.0 %collective-permute-start = (f32[264,128]{1,0:T(8,128)S(1)}, f32[264,128]{1,0:T(8,128)S(1)}, u32[]{:S(2)}, u32[]{:S(2)}) collective-permute-start(f32[264,128]{1,0:T(8,128)S(1)} %get-tuple-element.56), channel_id=1, source_target_pairs={{0,28},{4,8},{8,4},{12,16},{16,12},{20,24},{24,20},{28,0},{1,29},{... | collective-permute-start | bytes 405512 | tf_op jit(solution)/shard_map/ppermute | solution.py:622
  8.0 0.0 collective-permute-start.1
  8.0 0.1 slices.1
  8.1 0.1 collective-permute-start.2
  8.2 0.0 copy-done
  8.2 0.0 copy-done.1
  8.3 0.0 copy-done.2
  8.3 0.8 %pack_columns.1 = (f32[6,8,40,128]{3,2,1,0:T(8,128)S(1)}, f32[3,8,40,128]{3,2,1,0:T(8,128)S(1)}, f32[96,128]{1,0:T(8,128)S(1)}, f32[96,128]{1,0:T(8,128)S(1)}, f32[10,40,128]{2,1,0:T(8,128)S(1)}) custom-call(f32[3,8,32,128]{3,2,1,0:T(8,128)S(1)} %copy-done.1, f32[6,8,32,128]{3,2,1,0:T(8,128)S(1)} %copy-done, s32[8,32,128]{2,1,0:T(8,128)S(1)} %copy-done.2), custom_call_target="tpu_custom_call" | custom-call | tf_op jit(solution)/shard_map/pack_columns/pallas_call | solution.py:625
  9.1 0.4 %materials.1 = (f32[8,40,128]{2,1,0:T(8,128)S(1)}, f32[8,40,128]{2,1,0:T(8,128)S(1)}, f32[8,40,128]{2,1,0:T(8,128)S(1)}, f32[8,128]{1,0:T(8,128)S(1)}) custom-call(s32[8,32,128]{2,1,0:T(8,128)S(1)} %copy-done.2, f32[3,16]{1,0:T(4,128)S(1)} %get-tuple-element.51.table), custom_call_target="tpu_custom_call" | custom-call | tf_op jit(solution)/shard_map/materials/pallas_call | solution.py:662
  9.5 2.6 %collective-permute-done.2.got = f32[4,16,128]{2,1,0:T(8,128)S(1)} collective-permute-done((f32[4,16,128]{2,1,0:T(8,128)S(1)}, f32[4,16,128]{2,1,0:T(8,128)S(1)}, u32[]{:S(2)}, u32[]{:S(2)}) %collective-permute-start.2) | collective-permute-done | bytes 32800 | tf_op jit(solution)/shard_map/ppermute | solution.py:636
  12.1 0.1 ends.1
  12.2 0.1 collective-permute-start.3
  12.3 1.6 %collective-permute-start.4 = (f32[104,128]{1,0:T(8,128)S(1)}, f32[104,128]{1,0:T(8,128)S(1)}, u32[]{:S(2)}, u32[]{:S(2)}) collective-permute-start(f32[104,128]{1,0:T(8,128)S(1)} %get-tuple-element.73), channel_id=1, source_target_pairs={{0,1},{1,0},{2,3},{3,2},{4,5},{5,4},{6,7},{7,6},{8,9},{9,8},{10,11... | collective-permute-start | bytes 159752 | tf_op jit(solution)/shard_map/ppermute | solution.py:680
  13.9 0.0 collective-permute-done.rb
  13.9 0.6 %collective-permute-done.1.ra = f32[264,128]{1,0:T(8,128)S(1)} collective-permute-done((f32[264,128]{1,0:T(8,128)S(1)}, f32[264,128]{1,0:T(8,128)S(1)}, u32[]{:S(2)}, u32[]{:S(2)}) %collective-permute-start.1) | collective-permute-done | bytes 135200 | tf_op jit(solution)/shard_map/ppermute | solution.py:623
  14.5 0.3 %unpack.1 = (f32[6,8,40,128]{3,2,1,0:T(8,128)S(1)}, f32[3,8,40,128]{3,2,1,0:T(8,128)S(1)}, f32[8,40,128]{2,1,0:T(8,128)S(1)}, f32[8,40,128]{2,1,0:T(8,128)S(1)},...) custom-call(f32[6,8,40,128]{3,2,1,0:T(8,128)S(1)} %get-tuple-element, ...), custom_call_target="tpu_custom_call", output_to_operand_aliasing={{0}: (0, {}), {1}: (1, {}), {2}: (2, {}), {3}: (3, {}), {4}... | custom-call | tf_op jit(solution)/shard_map/unpack/pallas_call | solution.py:682
  14.8 0.9 %collective-permute-start.5 = (f32[3,8,128]{2,1,0:T(8,128)S(1)}, f32[3,8,128]{2,1,0:T(8,128)S(1)}, u32[]{:S(2)}, u32[]{:S(2)}) collective-permute-start(f32[3,8,128]{2,1,0:T(8,128)S(1)} %get-tuple-element.78), channel_id=1, source_target_pairs={{0,3},{1,2},{2,1},{3,0},{4,7},{5,6},{6,5},{7,4},{8,11},{9,10},{10,... | collective-permute-start | bytes 36872 | tf_op jit(solution)/shard_map/ppermute | solution.py:692
  15.6 0.8 %collective-permute-start.6 = (f32[3,8,128]{2,1,0:T(8,128)S(1)}, f32[3,8,128]{2,1,0:T(8,128)S(1)}, u32[]{:S(2)}, u32[]{:S(2)}) collective-permute-start(f32[3,8,128]{2,1,0:T(8,128)S(1)} %get-tuple-element.79), channel_id=1, source_target_pairs={{0,1},{1,0},{2,3},{3,2},{4,5},{5,4},{6,7},{7,6},{8,9},{9,8},{10,11... | collective-permute-start | bytes 36872 | tf_op jit(solution)/shard_map/ppermute | solution.py:693
  16.5 0.2 inner.1
  16.6 0.0 collective-permute-done.3.cb
  16.6 0.0 collective-permute-done.4.ca
  16.7 0.2 edges.1
  16.9 0.8 %collective-permute-start.7 = (f32[2,16,128]{2,1,0:T(8,128)S(1)}, f32[2,16,128]{2,1,0:T(8,128)S(1)}, u32[]{:S(2)}, u32[]{:S(2)}) collective-permute-start(f32[2,16,128]{2,1,0:T(8,128)S(1)} %get-tuple-element.91), channel_id=1, source_target_pairs={{0,16},{4,20},{8,24},{12,28},{16,0},{20,4},{24,8},{28,12},{1,17},{... | collective-permute-start | bytes 49160 | tf_op jit(solution)/shard_map/ppermute | solution.py:636
  17.7 0.4 %collective-permute-done.5.tcb = f32[3,8,128]{2,1,0:T(8,128)S(1)} collective-permute-done((f32[3,8,128]{2,1,0:T(8,128)S(1)}, f32[3,8,128]{2,1,0:T(8,128)S(1)}, u32[]{:S(2)}, u32[]{:S(2)}) %collective-permute-start.5) | collective-permute-done | bytes 12320 | tf_op jit(solution)/shard_map/ppermute | solution.py:692
  18.0 0.0 collective-permute-done.6.tca
  18.0 1.5 %cone.1 = (f32[6,8,40,128]{3,2,1,0:T(8,128)S(1)}, f32[3,8,40,128]{3,2,1,0:T(8,128)S(1)}, f32[10,40,128]{2,1,0:T(8,128)S(1)}, f32[3,40,128]{2,1,0:T(8,128)S(1)}, ...) custom-call(f32[6,8,40,128]{3,2,1,0:T(8,128)S(1)} %get-tuple-element, ...), custom_call_target="tpu_custom_call", output_to_operand_aliasing={{0}: (0, {}), {1}: (1, {}), {2}: (5, {}), {3}: (6, {})} | custom-call | tf_op jit(solution)/shard_map/cone/pallas_call | solution.py:714
  19.6 3.8 %all-to-all-start = ((f32[32,2,128]{2,1,0:T(2,128)}), f32[32,2,128]{2,1,0:T(2,128)S(1)}, u32[]{:S(2)}, u32[]{:S(2)}) async-start(f32[32,2,128]{2,1,0:T(2,128)} %get-tuple-element.94), calls=%async_computation | async-start | bytes 65536 | tf_op jit(solution)/shard_map/all_to_all | solution.py:727
  23.4 0.0 collective-permute-done.7
  23.4 1.8 %collective-permute-start.8 = (f32[1,16,128]{2,1,0:T(8,128)S(1)}, f32[1,16,128]{2,1,0:T(8,128)S(1)}, u32[]{:S(2)}, u32[]{:S(2)}) collective-permute-start(f32[1,16,128]{2,1,0:T(8,128)S(1)} %get-tuple-element.96), channel_id=1, source_target_pairs={{0,4},{4,0},{8,12},{12,8},{16,20},{20,16},{24,28},{28,24},{1,5},{5... | collective-permute-start | bytes 24584 | tf_op jit(solution)/shard_map/ppermute | solution.py:636
  25.2 1.2 %upper.1 = (f32[6,8,40,128]{3,2,1,0:T(8,128)S(1)}, f32[3,8,40,128]{3,2,1,0:T(8,128)S(1)}, f32[9,40,128]{2,1,0:T(8,128)S(1)}) custom-call(f32[6,8,40,128]{3,2,1,0:T(8,128)S(1)} %get-tuple-element.82.S_in, f32[3,8,40,128]{3,2,1,0:T(8,128)S(1)} %get-tuple-element.83.V_in, ...), custom_call_target="tpu_custom_call", output_to_operand_aliasing={{0}: (0, {}), {1}: (1, {}), {2}: (8, {})} | custom-call | tf_op jit(solution)/shard_map/upper/pallas_call | solution.py:728
  26.4 0.7 %collective-permute-done.8.got = f32[1,16,128]{2,1,0:T(8,128)S(1)} collective-permute-done((f32[1,16,128]{2,1,0:T(8,128)S(1)}, f32[1,16,128]{2,1,0:T(8,128)S(1)}, u32[]{:S(2)}, u32[]{:S(2)}) %collective-permute-start.8) | collective-permute-done | bytes 8224 | tf_op jit(solution)/shard_map/ppermute | solution.py:636
  27.1 2.2 %lower.1 = (f32[6,8,40,128]{3,2,1,0:T(8,128)S(1)}, f32[3,8,40,128]{3,2,1,0:T(8,128)S(1)}, f32[10,40,128]{2,1,0:T(8,128)S(1)}, f32[3,8,32,128]{3,2,1,0:T(8,128)}, f32[6,8,32,128]{3,2,1,0:T(8,128)}) custom-call(f32[6,8,40,128]{3,2,1,0:T(8,128)S(1)} %get-tuple-element.88.S_in, ...), custom_call_target="tpu_custom_call", output_to_operand_aliasing={{0}: (0, {}), {1}: (1, {}), {2}: (5, {})} | custom-call | tf_op jit(solution)/shard_map/lower/pallas_call | solution.py:745
  29.3 1.3 %all-to-all-done.shares = f32[32,2,128]{2,1,0:T(2,128)S(1)} async-done(((f32[32,2,128]{2,1,0:T(2,128)}), f32[32,2,128]{2,1,0:T(2,128)S(1)}, u32[]{:S(2)}, u32[]{:S(2)}) %all-to-all-start) | async-done | bytes 32800 | tf_op jit(solution)/shard_map/all_to_all | solution.py:727
  30.6 1.0 %sum_by_building.1 = f32[2,1024]{1,0:T(2,128)} custom-call(f32[32,2,128]{2,1,0:T(2,128)S(1)} %all-to-all-done.shares), custom_call_target="tpu_custom_call" | custom-call | tf_op jit(solution)/shard_map/sum_by_building/pallas_call | solution.py:737
  (3 shorter events, 0.0 us)
Async XLA Ops:
  0.6 7.6 %copy-start = (f32[6,8,32,128]{3,2,1,0:T(8,128)S(1)}, f32[6,8,32,128]{3,2,1,0:T(8,128)}, u32[]{:S(2)}) copy-start(f32[6,8,32,128]{3,2,1,0:T(8,128)} %stress.3) | copy-start | bytes 2359300
  0.6 7.6 %copy-start.1 = (f32[3,8,32,128]{3,2,1,0:T(8,128)S(1)}, f32[3,8,32,128]{3,2,1,0:T(8,128)}, u32[]{:S(2)}) copy-start(f32[3,8,32,128]{3,2,1,0:T(8,128)} %vel.3) | copy-start | bytes 1179652
  0.7 7.6 %copy-start.2 = (s32[8,32,128]{2,1,0:T(8,128)S(1)}, s32[8,32,128]{2,1,0:T(8,128)}, u32[]{:S(2)}) copy-start(s32[8,32,128]{2,1,0:T(8,128)} %zones.5) | copy-start | bytes 393220
  1.9 12.0 %collective-permute-start = (f32[264,128]{1,0:T(8,128)S(1)}, f32[264,128]{1,0:T(8,128)S(1)}, u32[]{:S(2)}, u32[]{:S(2)}) collective-permute-start(f32[264,128]{1,0:T(8,128)S(1)} %get-tuple-element.56), channel_id=1, source_target_pairs={{0,28},{4,8},{8,4},{12,16},{16,12},{20,24},{24,20},{28,0},{1,29},{... | collective-permute-start | bytes 405512 | tf_op jit(solution)/shard_map/ppermute | solution.py:622
  8.0 6.5 %collective-permute-start.1 = (f32[264,128]{1,0:T(8,128)S(1)}, f32[264,128]{1,0:T(8,128)S(1)}, u32[]{:S(2)}, u32[]{:S(2)}) collective-permute-start(f32[264,128]{1,0:T(8,128)S(1)} %get-tuple-element.57), channel_id=1, source_target_pairs={{0,4},{4,0},{8,12},{12,8},{16,20},{20,16},{24,28},{28,24},{1,5},{5... | collective-permute-start | bytes 405512 | tf_op jit(solution)/shard_map/ppermute | solution.py:623
  8.1 4.0 %collective-permute-start.2 = (f32[4,16,128]{2,1,0:T(8,128)S(1)}, f32[4,16,128]{2,1,0:T(8,128)S(1)}, u32[]{:S(2)}, u32[]{:S(2)}) collective-permute-start(f32[4,16,128]{2,1,0:T(8,128)S(1)} %get-tuple-element.65), channel_id=1, source_target_pairs={{0,8},{4,12},{8,0},{12,4},{16,24},{20,28},{24,16},{28,20},{1,9},{5... | collective-permute-start | bytes 98312 | tf_op jit(solution)/shard_map/ppermute | solution.py:636
  12.2 4.4 %collective-permute-start.3 = (f32[104,128]{1,0:T(8,128)S(1)}, f32[104,128]{1,0:T(8,128)S(1)}, u32[]{:S(2)}, u32[]{:S(2)}) collective-permute-start(f32[104,128]{1,0:T(8,128)S(1)} %get-tuple-element.72), channel_id=1, source_target_pairs={{0,3},{1,2},{2,1},{3,0},{4,7},{5,6},{6,5},{7,4},{8,11},{9,10},{10,... | collective-permute-start | bytes 159752 | tf_op jit(solution)/shard_map/ppermute | solution.py:679
  12.3 4.4 %collective-permute-start.4 = (f32[104,128]{1,0:T(8,128)S(1)}, f32[104,128]{1,0:T(8,128)S(1)}, u32[]{:S(2)}, u32[]{:S(2)}) collective-permute-start(f32[104,128]{1,0:T(8,128)S(1)} %get-tuple-element.73), channel_id=1, source_target_pairs={{0,1},{1,0},{2,3},{3,2},{4,5},{5,4},{6,7},{7,6},{8,9},{9,8},{10,11... | collective-permute-start | bytes 159752 | tf_op jit(solution)/shard_map/ppermute | solution.py:680
  14.8 3.2 %collective-permute-start.5 = (f32[3,8,128]{2,1,0:T(8,128)S(1)}, f32[3,8,128]{2,1,0:T(8,128)S(1)}, u32[]{:S(2)}, u32[]{:S(2)}) collective-permute-start(f32[3,8,128]{2,1,0:T(8,128)S(1)} %get-tuple-element.78), channel_id=1, source_target_pairs={{0,3},{1,2},{2,1},{3,0},{4,7},{5,6},{6,5},{7,4},{8,11},{9,10},{10,... | collective-permute-start | bytes 36872 | tf_op jit(solution)/shard_map/ppermute | solution.py:692
  15.6 2.4 %collective-permute-start.6 = (f32[3,8,128]{2,1,0:T(8,128)S(1)}, f32[3,8,128]{2,1,0:T(8,128)S(1)}, u32[]{:S(2)}, u32[]{:S(2)}) collective-permute-start(f32[3,8,128]{2,1,0:T(8,128)S(1)} %get-tuple-element.79), channel_id=1, source_target_pairs={{0,1},{1,0},{2,3},{3,2},{4,5},{5,4},{6,7},{7,6},{8,9},{9,8},{10,11... | collective-permute-start | bytes 36872 | tf_op jit(solution)/shard_map/ppermute | solution.py:693
  16.9 6.5 %collective-permute-start.7 = (f32[2,16,128]{2,1,0:T(8,128)S(1)}, f32[2,16,128]{2,1,0:T(8,128)S(1)}, u32[]{:S(2)}, u32[]{:S(2)}) collective-permute-start(f32[2,16,128]{2,1,0:T(8,128)S(1)} %get-tuple-element.91), channel_id=1, source_target_pairs={{0,16},{4,20},{8,24},{12,28},{16,0},{20,4},{24,8},{28,12},{1,17},{... | collective-permute-start | bytes 49160 | tf_op jit(solution)/shard_map/ppermute | solution.py:636
  19.6 11.0 %all-to-all-start = ((f32[32,2,128]{2,1,0:T(2,128)}), f32[32,2,128]{2,1,0:T(2,128)S(1)}, u32[]{:S(2)}, u32[]{:S(2)}) async-start(f32[32,2,128]{2,1,0:T(2,128)} %get-tuple-element.94), calls=%async_computation | async-start | bytes 65536 | tf_op jit(solution)/shard_map/all_to_all | solution.py:727
  23.4 3.7 %collective-permute-start.8 = (f32[1,16,128]{2,1,0:T(8,128)S(1)}, f32[1,16,128]{2,1,0:T(8,128)S(1)}, u32[]{:S(2)}, u32[]{:S(2)}) collective-permute-start(f32[1,16,128]{2,1,0:T(8,128)S(1)} %get-tuple-element.96), channel_id=1, source_target_pairs={{0,4},{4,0},{8,12},{12,8},{16,20},{20,16},{24,28},{28,24},{1,5},{5... | collective-permute-start | bytes 24584 | tf_op jit(solution)/shard_map/ppermute | solution.py:636
